TPU v7x, 32 devices: a whole 2x2x4 slice. The times are simulated.
32 devices in a mesh: seq: 8 (over z, y), batch: 4 (over x, core).
Axes of the slice: x: 2, y: 2, z: 4, core: 2. Of those that a mesh axis runs over, the one named last changes fastest.
Arguments:
- tokens: bfloat16 [4, 1024, 2048], P('batch', 'seq'), may hold values from -6 to 6
- out_grad: bfloat16 [4, 1024, 2048], P('batch', 'seq'), may hold values from -6 to 6
- doc_lengths: int32 [4, 8], P('batch'), may hold values from 1 to 960, 1024 in all within a row
- qkv_weight: float32 [2048, 6144], P(('seq', 'batch')), may hold values from -0.125 to 0.125
- qkv_first: float32 [2048, 6144], P(('seq', 'batch')), may hold values from -40 to 40
- qkv_second: float32 [2048, 6144], P(('seq', 'batch')), may hold values from 106.496 to 1720.32
- out_weight: float32 [2048, 2048], P(('seq', 'batch')), may hold values from -1.75 to 1.75
- out_first: float32 [2048, 2048], P(('seq', 'batch')), may hold values from -6 to 6
- out_second: float32 [2048, 2048], P(('seq', 'batch')), may hold values from 0.6 to 9.6
- gate_up_weight: float32 [2048, 16384], P(('seq', 'batch')), may hold values from -0.125 to 0.125
- gate_up_first: float32 [2048, 16384], P(('seq', 'batch')), may hold values from -6 to 6
- gate_up_second: float32 [2048, 16384], P(('seq', 'batch')), may hold values from 9.4208 to 155.648
- down_weight: float32 [2048, 8192], P(('seq', 'batch')), may hold values from -0.0625 to 0.0625
- down_first: float32 [2048, 8192], P(('seq', 'batch')), may hold values from -24 to 24
- down_second: float32 [2048, 8192], P(('seq', 'batch')), may hold values from 38.5024 to 614.4
- gains: float32 [2, 2048], replicated, may hold values from 0.5 to 1.5
- gain_first: float32 [2, 2048], replicated, may hold values from -48 to 48
- gain_second: float32 [2, 2048], replicated, may hold values from 151.552 to 2457.6
Outputs:
- block_out: bfloat16 [4, 1024, 2048], P('batch', 'seq')
- input_grad: float32 [4, 1024, 2048], P('batch', 'seq')
- qkv_first_new: float32 [2048, 6144], P(('seq', 'batch'))
- qkv_second_new: float32 [2048, 6144], P(('seq', 'batch'))
- qkv_new: float32 [2048, 6144], P(('seq', 'batch'))
- out_first_new: float32 [2048, 2048], P(('seq', 'batch'))
- out_second_new: float32 [2048, 2048], P(('seq', 'batch'))
- out_new: float32 [2048, 2048], P(('seq', 'batch'))
- gate_up_first_new: float32 [2048, 16384], P(('seq', 'batch'))
- gate_up_second_new: float32 [2048, 16384], P(('seq', 'batch'))
- gate_up_new: float32 [2048, 16384], P(('seq', 'batch'))
- down_first_new: float32 [2048, 8192], P(('seq', 'batch'))
- down_second_new: float32 [2048, 8192], P(('seq', 'batch'))
- down_new: float32 [2048, 8192], P(('seq', 'batch'))
- gain_first_new: float32 [2, 2048], replicated
- gain_second_new: float32 [2, 2048], replicated
- gain_new: float32 [2, 2048], replicated
Inputs may be any that keep to these rules, and one draw needn't show every extreme that they name: `doc_lengths`: each row gives the lengths of the 8 documents of one sequence in order, summing to 1024; one of them has exactly 960 positions.
All inputs are finite; a program needn't handle non-finite values.
Results may differ from a plain program's by a relative error of at most 0.015.
Values may be sent and summed in bfloat16 or wider, within the bound.
No kernel may reach another device: no remote copies, remote signals or barrier semaphores. Data moves between devices by JAX's collectives and lax.ppermute only.
A program may use at most 704 MiB of HBM per device.

v0:
```python
import jax
import jax.numpy as jnp
from jax import lax
from jax.sharding import PartitionSpec as P

HD = 64
STEP = 10


norm_eps = 1e-05
rope_base = 130000.0
beta_one = 0.9
beta_two = 0.95
adam_eps = 1e-08
weight_decay = 0.1
masked_score = -1e30
rate_qkv = 0.05
rate_out = 0.5
rate_gate = 0.05
rate_down = 0.03
rate_gain = 0.3


def passed_along(value, axis, steps):
    count = lax.axis_size(axis)
    first, last = (max(0, -steps), min(count, count - steps))
    return lax.ppermute(value, axis, [(source, source + steps) for source in range(first, last)])


def shifted(value, axis, steps):
    count = lax.axis_size(axis)
    pairs = [(source, (source + steps) % count) for source in range(count)]
    return lax.ppermute(value, axis, pairs)


def rotate_half(values):
    middle = values.shape[-1] // 2
    return jnp.concatenate([-values[..., middle:], values[..., :middle]], axis=-1)


def rope_tables(positions):
    inverse = rope_base ** (-jnp.arange(0, HD, 2, dtype=jnp.float32) / HD)
    angles = positions.astype(jnp.float32)[:, None] * inverse[None, :]
    angles = jnp.concatenate([angles, angles], axis=1)
    return (jnp.cos(angles)[:, None, :], jnp.sin(angles)[:, None, :])


def apply_rope(values, cos_table, sin_table):
    return values * cos_table + rotate_half(values) * sin_table


def undo_rope(values, cos_table, sin_table):
    return values * cos_table - rotate_half(values) * sin_table


def doc_numbers(lengths, positions):
    ends_running = jnp.cumsum(lengths)
    return jnp.sum((positions[:, None] >= ends_running[None, :]).astype(jnp.int32), axis=1)


def unit_rows(values):
    scale_rows = lax.rsqrt(jnp.mean(values * values, axis=-1, keepdims=True) + norm_eps)
    return (values * scale_rows, scale_rows)


def norm_back(grad_normed, unit_values, scale_rows, gain_row):
    grad_unit = grad_normed * gain_row
    gain_part = jnp.sum(grad_normed * unit_values, axis=0)
    grad_values = scale_rows * (
        grad_unit - unit_values * jnp.mean(grad_unit * unit_values, axis=-1, keepdims=True)
    )
    return (grad_values, gain_part)


def contract_rows(left_side, right_side):
    return lax.dot_general(
        left_side, right_side, (((0,), (0,)), ((), ())), preferred_element_type=jnp.float32
    )


def contract_cols(left_side, right_side):
    return lax.dot_general(
        left_side, right_side, (((1,), (1,)), ((), ())), preferred_element_type=jnp.float32
    )


def block_diagonal(blocks):
    widths = [block.shape[1] for block in blocks]
    layers = []
    for place, block in enumerate(blocks):
        pieces = []
        for other, width in enumerate(widths):
            if other == place:
                pieces.append(block)
            else:
                pieces.append(jnp.zeros((block.shape[0], width), block.dtype))
        layers.append(jnp.concatenate(pieces, axis=1))
    return jnp.concatenate(layers, axis=0)


def stacked_terms(stacked_left, diagonal_right):
    return contract_rows(stacked_left, diagonal_right)


def adam_update(weight, first_moment, second, gradient, step_rate):
    first_new = beta_one * first_moment + (1.0 - beta_one) * gradient
    second_new = beta_two * second + (1.0 - beta_two) * gradient * gradient
    first_hat = first_new / (1.0 - beta_one**STEP)
    second_hat = second_new / (1.0 - beta_two**STEP)
    weight_new = weight - step_rate * (
        first_hat / (jnp.sqrt(second_hat) + adam_eps) + weight_decay * weight
    )
    return (first_new, second_new, weight_new)


def on_device(
    tokens,
    out_grad,
    doc_lengths,
    qkv_weight,
    qkv_first,
    qkv_second,
    out_weight,
    out_first,
    out_second,
    gate_up_weight,
    gate_up_first,
    gate_up_second,
    down_weight,
    down_first,
    down_second,
    gains,
    gain_first,
    gain_second,
):
    local_rows = tokens.shape[1]
    model_width = tokens.shape[2]
    head_count = model_width // HD
    hidden_width = down_weight.shape[1]
    score_scale = HD ** (-0.5)
    block_total = lax.axis_size("seq")
    block_index = lax.axis_index("seq")
    first_position = block_index * local_rows
    last_position = first_position + local_rows - 1
    positions = first_position + jnp.arange(local_rows, dtype=jnp.int32)
    lengths = doc_lengths[0]
    query_docs = doc_numbers(lengths, positions)
    doc_starts = jnp.cumsum(lengths) - lengths
    first_start = jnp.sum(
        jnp.where(jnp.arange(lengths.shape[0], dtype=jnp.int32) == query_docs[0], doc_starts, 0)
    )
    cos_table, sin_table = rope_tables(positions)
    qkv_full, out_full = (
        lax.all_gather(qkv_weight.astype(jnp.bfloat16), ("seq", "batch"), axis=0, tiled=True),
        lax.all_gather(out_weight.astype(jnp.bfloat16), ("seq", "batch"), axis=0, tiled=True),
    )
    gate_full, down_full = (
        lax.all_gather(gate_up_weight.astype(jnp.bfloat16), ("seq", "batch"), axis=0, tiled=True),
        lax.all_gather(down_weight.astype(jnp.bfloat16), ("seq", "batch"), axis=0, tiled=True),
    )

    def allowed_pairs(key_start, key_rows):
        key_positions = key_start + jnp.arange(key_rows, dtype=jnp.int32)
        key_docs = doc_numbers(lengths, key_positions)
        allowed = (key_positions[None, :] <= positions[:, None]) & (
            key_docs[None, :] == query_docs[:, None]
        )
        return allowed[None]

    def needed_block(key_start, key_rows):
        return (key_start <= last_position) & (key_start + key_rows - 1 >= first_start)

    inputs = tokens[0].astype(jnp.float32)
    unit_one, scale_one = unit_rows(inputs)
    act_one = (unit_one * gains[0]).astype(jnp.bfloat16)
    qkv = jnp.dot(act_one, qkv_full, preferred_element_type=jnp.float32)
    query = apply_rope(
        qkv[:, :model_width].reshape(local_rows, head_count, HD), cos_table, sin_table
    ).astype(jnp.bfloat16)
    key_rows_here = (
        apply_rope(
            qkv[:, model_width : 2 * model_width].reshape(local_rows, head_count, HD),
            cos_table,
            sin_table,
        )
        .astype(jnp.bfloat16)
        .reshape(local_rows, model_width)
    )
    value_rows = qkv[:, 2 * model_width :].astype(jnp.bfloat16)
    initial = (
        jnp.full((head_count, local_rows), masked_score, jnp.float32),
        jnp.zeros((head_count, local_rows), jnp.float32),
        jnp.zeros((head_count, local_rows, HD), jnp.float32),
    )
    row_start = jnp.int32(0)
    key_part = lax.all_gather(key_rows_here, "seq", axis=0, tiled=True)
    value_part = lax.all_gather(value_rows, "seq", axis=0, tiled=True)
    key_count = key_part.shape[0]

    def attend_compute(online_state):
        running_max, running_total, weighted = online_state
        scores = (
            jnp.einsum(
                "qhd,khd->hqk",
                query,
                key_part.reshape(key_count, head_count, HD),
                preferred_element_type=jnp.float32,
            )
            * score_scale
        )
        allowed = allowed_pairs(row_start, key_count)
        new_max = jnp.maximum(
            running_max, jnp.max(jnp.where(allowed, scores, masked_score), axis=-1)
        )
        weights_now = jnp.where(allowed, jnp.exp(scores - new_max[..., None]), 0.0)
        new_total = jnp.sum(weights_now, axis=-1)
        new_weighted = jnp.einsum(
            "hqk,khd->hqd",
            weights_now.astype(jnp.bfloat16),
            value_part.reshape(key_count, head_count, HD),
            preferred_element_type=jnp.float32,
        )
        return (new_max, new_total, new_weighted)

    final_max, final_total, final_weighted = lax.cond(
        needed_block(row_start, key_count),
        attend_compute,
        lambda online_state: online_state,
        initial,
    )
    attended = jnp.transpose(final_weighted / final_total[..., None], (1, 0, 2))
    log_total = final_max + jnp.log(final_total)
    attn_low = attended.reshape(local_rows, model_width).astype(jnp.bfloat16)
    middle = inputs + jnp.dot(attn_low, out_full, preferred_element_type=jnp.float32)
    unit_two, scale_two = unit_rows(middle)
    act_two = (unit_two * gains[1]).astype(jnp.bfloat16)
    gate_up = jnp.dot(act_two, gate_full, preferred_element_type=jnp.float32)
    gate_part = gate_up[:, :hidden_width]
    up_part = gate_up[:, hidden_width:]
    sigmoid_gate = jax.nn.sigmoid(gate_part)
    silu_gate = gate_part * sigmoid_gate
    hidden_low = (silu_gate * up_part).astype(jnp.bfloat16)
    ffn_out = contract_cols(hidden_low, down_full)
    block_out = (middle + ffn_out).astype(jnp.bfloat16)[None]
    out_low = out_grad[0]
    out_float = out_low.astype(jnp.float32)
    grad_hidden = jnp.dot(out_low, down_full, preferred_element_type=jnp.float32)
    grad_gate = grad_hidden * up_part * (sigmoid_gate * (1.0 + gate_part * (1.0 - sigmoid_gate)))
    grad_up = grad_hidden * silu_gate
    grad_gate_up = jnp.concatenate([grad_gate, grad_up], axis=1).astype(jnp.bfloat16)
    grad_act_two = contract_cols(grad_gate_up, gate_full)
    grad_mid_norm, gain_two_grad = norm_back(grad_act_two, unit_two, scale_two, gains[1])
    grad_middle = out_float + grad_mid_norm
    ffn_left = jnp.concatenate([act_two, out_low], axis=0)
    ffn_right = block_diagonal([grad_gate_up, hidden_low])
    ffn_grads = lax.psum_scatter(
        stacked_terms(ffn_left, ffn_right), ("seq", "batch"), scatter_dimension=0, tiled=True
    )
    grad_attn_low = grad_middle.astype(jnp.bfloat16)
    grad_heads = (
        contract_cols(grad_attn_low, out_full)
        .astype(jnp.bfloat16)
        .reshape(local_rows, head_count, HD)
    )
    delta_rows = jnp.transpose(jnp.sum(grad_heads.astype(jnp.float32) * attended, axis=-1))

    def visit_block(step_index, loop_state):
        key_now, value_now, key_grad, value_grad, query_grad = loop_state
        source = jnp.mod(block_index - step_index, block_total)
        key_start = source * local_rows

        def visit_compute(grad_state):
            key_acc, value_acc, query_acc = grad_state
            key_heads = key_now.reshape(local_rows, head_count, HD)
            value_heads = value_now.reshape(local_rows, head_count, HD)
            allowed = allowed_pairs(key_start, local_rows)
            scores = (
                jnp.einsum("qhd,khd->hqk", query, key_heads, preferred_element_type=jnp.float32)
                * score_scale
            )
            probs = jnp.where(allowed, jnp.exp(scores - log_total[..., None]), 0.0)
            value_acc = value_acc + jnp.einsum(
                "hqk,qhd->khd",
                probs.astype(jnp.bfloat16),
                grad_heads,
                preferred_element_type=jnp.float32,
            ).reshape(local_rows, model_width)
            grad_probs = jnp.einsum(
                "qhd,khd->hqk", grad_heads, value_heads, preferred_element_type=jnp.float32
            )
            grad_scores = (probs * (grad_probs - delta_rows[..., None])).astype(jnp.bfloat16)
            query_acc = (
                query_acc
                + jnp.einsum(
                    "hqk,khd->qhd", grad_scores, key_heads, preferred_element_type=jnp.float32
                )
                * score_scale
            )
            key_acc = key_acc + (
                jnp.einsum("hqk,qhd->khd", grad_scores, query, preferred_element_type=jnp.float32)
                * score_scale
            ).reshape(local_rows, model_width)
            return (key_acc, value_acc, query_acc)

        key_grad, value_grad, query_grad = lax.cond(
            needed_block(key_start, local_rows),
            visit_compute,
            lambda grad_state: grad_state,
            (key_grad, value_grad, query_grad),
        )
        key_now, value_now = passed_along((key_now, value_now), "seq", 1)
        key_grad, value_grad = (
            shifted(key_grad.astype(jnp.bfloat16), "seq", 1).astype(key_grad.dtype),
            shifted(value_grad.astype(jnp.bfloat16), "seq", 1).astype(value_grad.dtype),
        )
        return (key_now, value_now, key_grad, value_grad, query_grad)

    loop_initial = (
        key_rows_here,
        value_rows,
        jnp.zeros((local_rows, model_width), jnp.float32),
        jnp.zeros((local_rows, model_width), jnp.float32),
        jnp.zeros((local_rows, head_count, HD), jnp.float32),
    )
    loop_final = lax.fori_loop(0, block_total, visit_block, loop_initial)
    key_grad, value_grad, query_grad = (loop_final[2], loop_final[3], loop_final[4])
    grad_query = undo_rope(query_grad, cos_table, sin_table).reshape(local_rows, model_width)
    grad_key = undo_rope(
        key_grad.reshape(local_rows, head_count, HD), cos_table, sin_table
    ).reshape(local_rows, model_width)
    grad_qkv = jnp.concatenate([grad_query, grad_key, value_grad], axis=1).astype(jnp.bfloat16)
    grad_act_one = contract_cols(grad_qkv, qkv_full)
    grad_in_norm, gain_one_grad = norm_back(grad_act_one, unit_one, scale_one, gains[0])
    input_grad = (grad_middle + grad_in_norm)[None]
    gain_grad = lax.psum(jnp.stack([gain_one_grad, gain_two_grad]), ("seq", "batch"))
    attn_left = jnp.concatenate([act_one, attn_low], axis=0)
    attn_right = block_diagonal([grad_qkv, grad_attn_low])
    attention_grads = lax.psum_scatter(
        stacked_terms(attn_left, attn_right), ("seq", "batch"), scatter_dimension=0, tiled=True
    )
    qkv_m, qkv_s, qkv_w = adam_update(
        qkv_weight, qkv_first, qkv_second, attention_grads[:, : 3 * model_width], rate_qkv
    )
    out_m, out_s, out_w = adam_update(
        out_weight, out_first, out_second, attention_grads[:, 3 * model_width :], rate_out
    )
    gate_m, gate_s, gate_w = adam_update(
        gate_up_weight, gate_up_first, gate_up_second, ffn_grads[:, : 2 * hidden_width], rate_gate
    )
    down_m, down_s, down_w = adam_update(
        down_weight, down_first, down_second, ffn_grads[:, 2 * hidden_width :], rate_down
    )
    gain_m, gain_s, gain_w = adam_update(gains, gain_first, gain_second, gain_grad, rate_gain)
    return (
        block_out,
        input_grad,
        qkv_m,
        qkv_s,
        qkv_w,
        out_m,
        out_s,
        out_w,
        gate_m,
        gate_s,
        gate_w,
        down_m,
        down_s,
        down_w,
        gain_m,
        gain_s,
        gain_w,
    )


def solution(mesh):
    return jax.shard_map(
        on_device,
        mesh=mesh,
        in_specs=(
            P("batch", "seq", None),
            P("batch", "seq", None),
            P("batch", None),
            P(("seq", "batch"), None),
            P(("seq", "batch"), None),
            P(("seq", "batch"), None),
            P(("seq", "batch"), None),
            P(("seq", "batch"), None),
            P(("seq", "batch"), None),
            P(("seq", "batch"), None),
            P(("seq", "batch"), None),
            P(("seq", "batch"), None),
            P(("seq", "batch"), None),
            P(("seq", "batch"), None),
            P(("seq", "batch"), None),
            P(),
            P(),
            P(),
        ),
        out_specs=(
            P("batch", "seq", None),
            P("batch", "seq", None),
            P(("seq", "batch"), None),
            P(("seq", "batch"), None),
            P(("seq", "batch"), None),
            P(("seq", "batch"), None),
            P(("seq", "batch"), None),
            P(("seq", "batch"), None),
            P(("seq", "batch"), None),
            P(("seq", "batch"), None),
            P(("seq", "batch"), None),
            P(("seq", "batch"), None),
            P(("seq", "batch"), None),
            P(("seq", "batch"), None),
            P(),
            P(),
            P(),
        ),
        check_vma=False,
    )
```

profile of v0, /device:TPU:0, one launch (start us, length us, event | category | flops | bytes accessed | tf_op | source)
XLA Modules:
  0.0 3863.2 jit_solution(11823995200929579968)
XLA Ops:
  12.6 156.2 %all-gather.7.cloned.1.call-done = bf16[2048,6144]{1,0:T(8,128)(2,1)} async-done(((bf16[64,6144]{1,0:T(8,128)(2,1)}), bf16[2048,6144]{1,0:T(8,128)(2,1)}) %all-gather.7.cloned.1.call-update) | async-done | bytes 25165840 | tf_op jit(solution)/shard_map/all_gather | solution.py:154
  168.8 10.1 fusion.87
  203.1 59.0 %all-gather.9.cloned.1.call-done = bf16[1024,2048]{1,0:T(8,128)(2,1)} async-done(((bf16[128,2048]{1,0:T(8,128)(2,1)}), bf16[1024,2048]{1,0:T(8,128)(2,1)}) %all-gather.9.cloned.1.call-update) | async-done | bytes 4194320 | tf_op jit(solution)/shard_map/all_gather | solution.py:196
  262.1 74.4 %all-gather.11.cloned.1.call-done = bf16[1024,2048]{1,0:T(8,128)(2,1)} async-done(((bf16[128,2048]{1,0:T(8,128)(2,1)}), bf16[1024,2048]{1,0:T(8,128)(2,1)}) %all-gather.11.cloned.1.call-update) | async-done | bytes 4194320 | tf_op jit(solution)/shard_map/all_gather | solution.py:197
  336.5 35.4 conditional.2
  374.6 41.0 %all-gather.13.cloned.1.call-done = bf16[2048,2048]{1,0:T(8,128)(2,1)} async-done(((bf16[64,2048]{1,0:T(8,128)(2,1)}), bf16[2048,2048]{1,0:T(8,128)(2,1)}) %all-gather.13.cloned.1.call-update) | async-done | bytes 8388624 | tf_op jit(solution)/shard_map/all_gather | solution.py:155
  420.5 353.2 %all-gather.15.cloned.1.call-done = bf16[2048,16384]{1,0:T(8,128)(2,1)} async-done(((bf16[64,16384]{1,0:T(8,128)(2,1)}), bf16[2048,16384]{1,0:T(8,128)(2,1)}) %all-gather.15.cloned.1.call-update) | async-done | bytes 67108880 | tf_op jit(solution)/shard_map/all_gather | solution.py:158
  773.7 27.2 fusion.88
  801.0 169.0 %all-gather.17.cloned.1.call-done = bf16[2048,8192]{1,0:T(8,128)(2,1)} async-done(((bf16[64,8192]{1,0:T(8,128)(2,1)}), bf16[2048,8192]{1,0:T(8,128)(2,1)}) %all-gather.17.cloned.1.call-update) | async-done | bytes 33554448 | tf_op jit(solution)/shard_map/all_gather | solution.py:159
  970.0 19.2 multiply_convert_fusion.2
  989.2 30.7 multiply_reduce_fusion
  1031.6 436.5 %while.26 = (s32[]{:T(128)}, bf16[128,2048]{0,1:T(8,128)(2,1)S(1)}, bf16[128,2048]{0,1:T(8,128)(2,1)S(1)}, f32[128,2048]{0,1:T(8,128)}, f32[128,2048]{0,1:T(8,12...) while((s32[]{:T(128)}, bf16[128,2048]{0,1:T(8,128)(2,1)S(1)}, ...), condition=%wide.region_18.19_spmd.clone, body=%wide.region_13.0_spmd.clone.sunk | while | flops 342150368 | bytes 55121792 | solution.py:325
  1060.7 9.6 collective-permute-done.3
  1078.4 10.7 collective-permute-done.1
  1093.0 10.1 collective-permute-start.2
  1138.3 9.7 collective-permute-done.1
  1154.4 10.2 collective-permute-start.3
  1188.2 10.0 collective-permute-done.1
  1202.2 10.6 collective-permute-start.2
  1275.2 13.0 collective-permute-start.1
  1320.8 11.5 collective-permute-start
  1337.4 12.3 collective-permute-done.2
  1389.9 16.0 collective-permute-done.2
  1437.6 22.6 collective-permute-done.2
  1480.4 24.5 fusion.28
  1509.7 69.7 %fusion.17 = f32[2048,24576]{1,0:T(8,128)} fusion(bf16[128,8192]{1,0:T(8,128)(2,1)S(1)} %copy-done.8, bf16[128,16384]{1,0:T(8,128)(2,1)} %pad_maximum_fusion, bf16[128,2048]{1,0:T(8,128)(2,1)S(1)} %bitcast.104, bf16[128,2048]{1,0:T(8,128)(2,1)S(1)} %copy-done.19), kind=kOutput, calls=%fused_computation.35 | convolution fusion | flops 25822232576 | bytes 208666624 | tf_op jit(solution)/shard_map/dot_general | solution.py:76
  1580.2 14.6 fusion.50
  1594.9 62.2 %psum.7 = f32[2,2048]{1,0:T(2,128)S(1)} all-reduce(f32[2,2048]{1,0:T(2,128)S(1)} %pad_maximum_fusion.3), channel_id=1, replica_groups=mesh['seq'=8,'batch'=4] {'seq','batch'}, use_global_device_ids=true, to_apply=%region_24.25 | all-reduce | flops 4096 | bytes 32768 | tf_op jit(solution)/shard_map/psum | solution.py:335
  1661.2 16.9 fusion.36
  1678.1 549.3 %reduce-scatter.3.cloned.1.call-done = f32[64,8192]{1,0:T(8,128)} async-done(((f32[2048,8192]{1,0:T(8,128)}), f32[64,8192]{1,0:T(8,128)}) %reduce-scatter.3.cloned.1.call-update) | async-done | bytes 2097168 | tf_op jit(solution)/shard_map/reduce_scatter | solution.py:338
  2235.4 1603.9 %reduce-scatter.5.cloned.1.call-done = f32[64,24576]{1,0:T(8,128)} async-done(((f32[2048,24576]{1,0:T(8,128)}), f32[64,24576]{1,0:T(8,128)}) %reduce-scatter.5.cloned.1.call-update) | async-done | bytes 6291472 | tf_op jit(solution)/shard_map/reduce_scatter | solution.py:256
  3839.3 11.5 multiply_subtract_fusion
  (321 shorter events, 410.8 us)
Async XLA Ops:
  7.2 161.6 %all-gather.7.cloned.1.call-start = ((), (), s32[]{:S(2)}) async-start(), calls=%async_computation.2 | async-start | bytes 25952256 | tf_op jit(solution)/shard_map/all_gather | solution.py:154
  9.7 252.4 %all-gather.9.cloned.1.call-start = ((), (), s32[]{:S(2)}) async-start(), calls=%async_computation.3 | async-start | bytes 4718592 | tf_op jit(solution)/shard_map/all_gather | solution.py:196
  190.4 146.1 %all-gather.11.cloned.1.call-start = ((), (), s32[]{:S(2)}) async-start(), calls=%async_computation.4 | async-start | bytes 4718592 | tf_op jit(solution)/shard_map/all_gather | solution.py:197
  191.3 224.2 %all-gather.13.cloned.1.call-start = ((), (), s32[]{:S(2)}) async-start(), calls=%async_computation.5 | async-start | bytes 8650752 | tf_op jit(solution)/shard_map/all_gather | solution.py:155
  193.2 580.5 %all-gather.15.cloned.1.call-start = ((), (), s32[]{:S(2)}) async-start(), calls=%async_computation.6 | async-start | bytes 69206016 | tf_op jit(solution)/shard_map/all_gather | solution.py:158
  197.1 772.9 %all-gather.17.cloned.1.call-start = ((), (), s32[]{:S(2)}) async-start(), calls=%async_computation.7 | async-start | bytes 34603008 | tf_op jit(solution)/shard_map/all_gather | solution.py:159
  198.3 2029.2 %reduce-scatter.3.cloned.1.call-start = ((), (), s32[]{:S(2)}) async-start(), calls=%async_computation.8 | async-start | bytes 69206016 | tf_op jit(solution)/shard_map/reduce_scatter | solution.py:338
  1043.6 34.8 collective-permute-start
  1046.6 42.5 %collective-permute-start.1 = (bf16[128,2048]{0,1:T(8,128)(2,1)}, bf16[128,2048]{0,1:T(8,128)(2,1)S(1)}, u32[]{:S(2)}, u32[]{:S(2)}) collective-permute-start(bf16[128,2048]{0,1:T(8,128)(2,1)} %copy.105), channel_id=1, source_target_pairs={{0,4},{4,8},{8,12},{12,16},{16,20},{20,24},{24,28},{1,5},{5,9},{9,... | collective-permute-start | bytes 1572872 | tf_op jit(solution)/shard_map/while/body/eval_jaxpr/ppermute | solution.py:27
  1104.5 33.8 collective-permute-start
  1106.4 41.5 %collective-permute-start.1 = (bf16[128,2048]{0,1:T(8,128)(2,1)}, bf16[128,2048]{0,1:T(8,128)(2,1)S(1)}, u32[]{:S(2)}, u32[]{:S(2)}) collective-permute-start(bf16[128,2048]{0,1:T(8,128)(2,1)} %copy.105), channel_id=1, source_target_pairs={{0,4},{4,8},{8,12},{12,16},{16,20},{20,24},{24,28},{1,5},{5,9},{9,... | collective-permute-start | bytes 1572872 | tf_op jit(solution)/shard_map/while/body/eval_jaxpr/ppermute | solution.py:27
  1154.4 30.7 collective-permute-start.3
  1166.6 31.6 collective-permute-start.1
  1202.2 32.5 collective-permute-start.2
  1216.1 31.7 collective-permute-start
  1225.2 30.8 collective-permute-start.1
  1260.0 32.7 collective-permute-start.2
  1263.4 36.9 collective-permute-start.3
  1270.9 31.5 collective-permute-start
  1275.2 30.5 collective-permute-start.1
  1309.7 40.1 %collective-permute-start.2 = (bf16[128,2048]{0,1:T(8,128)(2,1)}, bf16[128,2048]{0,1:T(8,128)(2,1)S(1)}, u32[]{:S(2)}, u32[]{:S(2)}) collective-permute-start(bf16[128,2048]{0,1:T(8,128)(2,1)} %convert_element_type.210), channel_id=1, source_target_pairs={{0,4},{4,8},{8,12},{12,16},{16,20},{20,24},{24,28},{28,0},{1,5},{5... | collective-permute-start | bytes 1572872 | tf_op jit(solution)/shard_map/while/body/eval_jaxpr/ppermute | solution.py:33
  1317.4 39.0 %collective-permute-start.3 = (bf16[128,2048]{0,1:T(8,128)(2,1)S(1)}, bf16[128,2048]{0,1:T(8,128)(2,1)}, u32[]{:S(2)}, u32[]{:S(2)}) collective-permute-start(bf16[128,2048]{0,1:T(8,128)(2,1)S(1)} %convert_element_type.212), channel_id=1, source_target_pairs={{0,4},{4,8},{8,12},{12,16},{16,20},{20,24},{24,28},{28,0},{1,5},{5... | collective-permute-start | bytes 1572872 | tf_op jit(solution)/shard_map/while/body/eval_jaxpr/ppermute | solution.py:33
  1320.8 37.7 collective-permute-start
  1363.1 42.8 %collective-permute-start.2 = (bf16[128,2048]{0,1:T(8,128)(2,1)}, bf16[128,2048]{0,1:T(8,128)(2,1)S(1)}, u32[]{:S(2)}, u32[]{:S(2)}) collective-permute-start(bf16[128,2048]{0,1:T(8,128)(2,1)} %convert_element_type.210), channel_id=1, source_target_pairs={{0,4},{4,8},{8,12},{12,16},{16,20},{20,24},{24,28},{28,0},{1,5},{5... | collective-permute-start | bytes 1572872 | tf_op jit(solution)/shard_map/while/body/eval_jaxpr/ppermute | solution.py:33
  1366.4 45.2 %collective-permute-start.3 = (bf16[128,2048]{0,1:T(8,128)(2,1)S(1)}, bf16[128,2048]{0,1:T(8,128)(2,1)}, u32[]{:S(2)}, u32[]{:S(2)}) collective-permute-start(bf16[128,2048]{0,1:T(8,128)(2,1)S(1)} %convert_element_type.212), channel_id=1, source_target_pairs={{0,4},{4,8},{8,12},{12,16},{16,20},{20,24},{24,28},{28,0},{1,5},{5... | collective-permute-start | bytes 1572872 | tf_op jit(solution)/shard_map/while/body/eval_jaxpr/ppermute | solution.py:33
  1375.4 38.3 collective-permute-start
  1380.6 33.1 collective-permute-start.1
  1417.7 42.5 %collective-permute-start.2 = (bf16[128,2048]{0,1:T(8,128)(2,1)}, bf16[128,2048]{0,1:T(8,128)(2,1)S(1)}, u32[]{:S(2)}, u32[]{:S(2)}) collective-permute-start(bf16[128,2048]{0,1:T(8,128)(2,1)} %convert_element_type.210), channel_id=1, source_target_pairs={{0,4},{4,8},{8,12},{12,16},{16,20},{20,24},{24,28},{28,0},{1,5},{5... | collective-permute-start | bytes 1572872 | tf_op jit(solution)/shard_map/while/body/eval_jaxpr/ppermute | solution.py:33
  1419.5 46.5 %collective-permute-start.3 = (bf16[128,2048]{0,1:T(8,128)(2,1)S(1)}, bf16[128,2048]{0,1:T(8,128)(2,1)}, u32[]{:S(2)}, u32[]{:S(2)}) collective-permute-start(bf16[128,2048]{0,1:T(8,128)(2,1)S(1)} %convert_element_type.212), channel_id=1, source_target_pairs={{0,4},{4,8},{8,12},{12,16},{16,20},{20,24},{24,28},{28,0},{1,5},{5... | collective-permute-start | bytes 1572872 | tf_op jit(solution)/shard_map/while/body/eval_jaxpr/ppermute | solution.py:33
  1424.0 44.1 %collective-permute-start = (bf16[128,2048]{0,1:T(8,128)(2,1)S(1)}, bf16[128,2048]{0,1:T(8,128)(2,1)S(1)}, u32[]{:S(2)}, u32[]{:S(2)}) collective-permute-start(bf16[128,2048]{0,1:T(8,128)(2,1)S(1)} %copy.104), channel_id=1, source_target_pairs={{0,4},{4,8},{8,12},{12,16},{16,20},{20,24},{24,28},{1,5},{5,9},{9,... | collective-permute-start | bytes 1572872 | tf_op jit(solution)/shard_map/while/body/eval_jaxpr/ppermute | solution.py:27
  1432.4 35.6 collective-permute-start.1
  1504.9 2334.4 %reduce-scatter.5.cloned.1.call-start = ((), (), s32[]{:S(2)}) async-start(), calls=%async_computation.9 | async-start | bytes 207618048 | tf_op jit(solution)/shard_map/reduce_scatter | solution.py:256
  (58 other events, 6655.0 us)
Sparse Core Ops, SparseCore 0:
  11.5 157.3 all-gather.6
  190.5 71.5 all-gather.8
  264.8 71.6 all-gather.10
  339.8 75.7 all-gather.12
  418.8 354.8 all-gather.14
  777.0 192.9 all-gather.16
  1505.0 722.3 reduce-scatter.2
  2233.9 1605.3 reduce-scatter.4
where the time goes:
time: 3870 us; the launch traced here: 3860 us
  waiting for transfers between devices  3200 us (83%)
  matrix products  244 us (6%)
  starting transfers between devices  177 us (5%)
  other arithmetic  112 us (3%)
  blocking collectives  62.2 us (2%)
  local copies, waits for them, and re-layouts  43.9 us (1%)
    reduce_scatter x1, waiting for transfers between devices, on_device(): lax.psum_scatter(stacked_terms(ffn_left, ffn_right), ('seq', 'batch'), sc...  1600 us
    reduce_scatter x1, waiting for transfers between devices, on_device(): lax.psum_scatter(stacked_terms(attn_left, attn_right), ('seq', 'batch'),...  549 us
    all_gather x1, waiting for transfers between devices, on_device(): lax.all_gather(gate_up_weight.astype(jnp.bfloat16), ('seq', 'batch'), axi...  353 us
    all_gather x1, waiting for transfers between devices, on_device(): lax.all_gather(down_weight.astype(jnp.bfloat16), ('seq', 'batch'), axis=0...  169 us
    all_gather x1, waiting for transfers between devices, on_device(): lax.all_gather(qkv_weight.astype(jnp.bfloat16), ('seq', 'batch'), axis=0,...  156 us
    ppermute x16, waiting for transfers between devices, shifted(): return lax.ppermute(value, axis, pairs)  134 us
    ppermute x16, starting transfers between devices, passed_along(): lax.ppermute(value, axis, [(source, source + steps) for source in range(f...  97.3 us
    dot_general x2, matrix products, contract_rows(): lax.dot_general(left_side, right_side, (((0,), (0,)), ((), ())), preferre...  94.1 us
  transfers between devices with their start and end apart: 40, of which 34 were waited for; matrix products, arithmetic and copies ran while one was open for 6% of the time, Pallas kernels for 0%

commit v1 on v0

v1 whole, which is shorter than its diff:
```python
import jax
import jax.numpy as jnp
from jax import lax
from jax.experimental import pallas as pl
from jax.experimental.pallas import tpu as pltpu
from jax.sharding import PartitionSpec as P

HD = 64
STEP = 10
LANES = 128
QUERY_ROWS = 256


norm_eps = 1e-05
rope_base = 130000.0
beta_one = 0.9
beta_two = 0.95
adam_eps = 1e-08
weight_decay = 0.1
masked_score = -1e30
rate_qkv = 0.05
rate_out = 0.5
rate_gate = 0.05
rate_down = 0.03
rate_gain = 0.3


def rotate_half(values):
    middle = values.shape[-1] // 2
    return jnp.concatenate([-values[..., middle:], values[..., :middle]], axis=-1)


def rope_tables(positions):
    inverse = rope_base ** (-jnp.arange(0, HD, 2, dtype=jnp.float32) / HD)
    angles = positions.astype(jnp.float32)[:, None] * inverse[None, :]
    angles = jnp.concatenate([angles, angles], axis=1)
    return (jnp.cos(angles), jnp.sin(angles))


def apply_rope(values, cos_table, sin_table):
    return values * cos_table + rotate_half(values) * sin_table


def undo_rope(values, cos_table, sin_table):
    return values * cos_table - rotate_half(values) * sin_table


def unit_rows(values):
    scale_rows = lax.rsqrt(jnp.mean(values * values, axis=-1, keepdims=True) + norm_eps)
    return (values * scale_rows, scale_rows)


def norm_back(grad_normed, unit_values, scale_rows, gain_row):
    grad_unit = grad_normed * gain_row
    gain_part = jnp.sum(grad_normed * unit_values, axis=0)
    grad_values = scale_rows * (
        grad_unit - unit_values * jnp.mean(grad_unit * unit_values, axis=-1, keepdims=True)
    )
    return (grad_values, gain_part)


def contract_rows(left_side, right_side):
    return lax.dot_general(
        left_side, right_side, (((0,), (0,)), ((), ())), preferred_element_type=jnp.float32
    )


def contract_cols(left_side, right_side):
    return lax.dot_general(
        left_side, right_side, (((1,), (1,)), ((), ())), preferred_element_type=jnp.float32
    )


def matmul(left_side, right_side):
    return jnp.dot(left_side, right_side, preferred_element_type=jnp.float32)


def adam_update(weight, first_moment, second, gradient, step_rate):
    first_new = beta_one * first_moment + (1.0 - beta_one) * gradient
    second_new = beta_two * second + (1.0 - beta_two) * gradient * gradient
    first_hat = first_new / (1.0 - beta_one**STEP)
    second_hat = second_new / (1.0 - beta_two**STEP)
    weight_new = weight - step_rate * (
        first_hat / (jnp.sqrt(second_hat) + adam_eps) + weight_decay * weight
    )
    return (first_new, second_new, weight_new)


def swapped(value, axis, bit):
    count = lax.axis_size(axis)
    return lax.ppermute(value, axis, [(source, source ^ bit) for source in range(count)])


def ring_order(count):
    return list(range(0, count, 2)) + list(range(count - 1, 0, -2))


def ring_shift(value, steps):
    count = lax.axis_size("seq")
    order = ring_order(count)
    pairs = [(order[i], order[(i + steps) % count]) for i in range(count)]
    return lax.ppermute(value, "seq", pairs)


def ring_place(offset):
    count = lax.axis_size("seq")
    order = ring_order(count)
    table = jnp.array([order[(order.index(own) + offset) % count] for own in range(count)], jnp.int32)
    return table[lax.axis_index("seq")]


def ring_gather(parts, fillers=()):
    count = lax.axis_size("seq")
    far = count // 2
    packed = jnp.concatenate(parts, axis=1) if len(parts) > 1 else parts[0]
    middle = packed.shape[1] // 2
    blocks = {0: packed}
    ahead = behind = packed
    for step in range(1, far):
        if 0 <= step - 2 < len(fillers):
            ahead, behind = after_all((ahead, behind), fillers[step - 2])
        ahead, behind = ring_shift(ahead, 1), ring_shift(behind, -1)
        blocks[-step], blocks[step] = ahead, behind
    if far - 2 < len(fillers):
        ahead, behind = after_all((ahead, behind), fillers[far - 2])
    left, right = ring_shift(ahead[:, :middle], 1), ring_shift(behind[:, middle:], -1)
    blocks[far] = jnp.concatenate([left, right], axis=1)
    gathered = []
    first = 0
    for part in parts:
        last = first + part.shape[1]
        gathered.append({offset: block[:, first:last] for offset, block in blocks.items()})
        first = last
    return gathered


def with_rows(block, rows):
    if block.shape[0] >= rows:
        return jnp.concatenate(jnp.split(block, block.shape[0] // rows, axis=0), axis=1)
    return jnp.concatenate(jnp.split(block, rows // block.shape[0], axis=1), axis=0)


def stacked_rows(blocks):
    rows, width = blocks[0].shape
    whole = jnp.zeros((len(blocks) * rows, width), blocks[0].dtype)
    for offset, block in blocks.items():
        whole = lax.dynamic_update_slice(whole, block, (ring_place(offset) * rows, 0))
    return whole


def stacked_columns(blocks):
    rows, width = blocks[0].shape
    whole = jnp.zeros((rows, len(blocks) * width), blocks[0].dtype)
    for offset, block in blocks.items():
        whole = lax.dynamic_update_slice(whole, block, (0, ring_place(offset) * width))
    return whole


def ring_rows(whole, offsets):
    rows = whole.shape[0] // lax.axis_size("seq")
    return jnp.concatenate(
        [lax.dynamic_slice_in_dim(whole, ring_place(o) * rows, rows, 0) for o in offsets], axis=0
    )


def added(block, got):
    return (block.astype(jnp.float32) + got.astype(jnp.float32)).astype(block.dtype)


def ring_scatter_sum(parts, fillers=()):
    far = lax.axis_size("seq") // 2
    first, second = parts
    ahead, behind = (ring_shift(first[far], 1),), (ring_shift(second[far], -1),)
    for turn, step in enumerate(range(far - 1, 0, -1)):
        onward = [first[step], second[step]]
        backward = [first[-step], second[-step]]
        if turn == 0:
            onward[0] = added(onward[0], ahead[0])
            backward[1] = added(backward[1], behind[0])
        else:
            onward = [added(block, got) for block, got in zip(onward, ahead)]
            backward = [added(block, got) for block, got in zip(backward, behind)]
        if turn < len(fillers):
            moved = after_all(onward + backward, fillers[turn])
            onward, backward = moved[:2], moved[2:]
        ahead = [ring_shift(block, 1) for block in onward]
        behind = [ring_shift(block, -1) for block in backward]
    return [
        own.astype(jnp.float32) + left.astype(jnp.float32) + right.astype(jnp.float32)
        for own, left, right in zip((first[0], second[0]), ahead, behind)
    ]


def ring_scatter_one(whole, fillers=()):
    far = lax.axis_size("seq") // 2
    middle = whole.shape[1] // 2
    offsets = [0] + [sign * step for step in range(1, far) for sign in (1, -1)] + [far]
    blocks = {offset: ring_rows(whole, [offset]) for offset in offsets}
    halves = ring_scatter_sum(
        (
            {offset: block[:, :middle] for offset, block in blocks.items()},
            {offset: block[:, middle:] for offset, block in blocks.items()},
        ),
        fillers,
    )
    return jnp.concatenate(halves, axis=1)


def sum_everywhere(values):
    total = lax.axis_size("seq") * lax.axis_size("batch")
    copies = jnp.broadcast_to(values[None], (total,) + values.shape)
    return jnp.sum(lax.all_to_all(copies, ("seq", "batch"), 0, 0, tiled=True), axis=0)


def after(value, *others):
    return lax.optimization_barrier((value,) + others)[0]


def after_all(values, others):
    return lax.optimization_barrier(tuple(values) + tuple(others))[: len(values)]


def batch_bits():
    count = lax.axis_size("batch")
    bits = []
    while (1 << len(bits)) < count:
        bits.append(1 << len(bits))
    return bits


def of_offset(choices, offset):
    index = lax.axis_index("batch")
    picked = choices[offset]
    for own in range(1, len(choices)):
        picked = jnp.where(index == own, choices[own ^ offset], picked)
    return picked


def offset_order():
    order = [0]
    for bit in reversed(batch_bits()):
        order = order + [offset ^ bit for offset in order]
    return order


def batch_columns(rows, rows_own):
    count, width = rows.shape
    batch_total = lax.axis_size("batch")
    blocks = rows.reshape(count, -1, batch_total, rows_own)
    return [blocks[:, :, b].reshape(count, width // batch_total) for b in range(batch_total)]


def to_relative(rows, rows_own):
    columns = batch_columns(rows, rows_own)
    return jnp.concatenate([of_offset(columns, m) for m in offset_order()], axis=1)


def from_relative(rows, rows_own):
    count, width = rows.shape
    batch_total = lax.axis_size("batch")
    order = offset_order()
    part = width // batch_total
    columns = [
        rows[:, order.index(m) * part : (order.index(m) + 1) * part] for m in range(batch_total)
    ]
    blocks = [
        of_offset(columns, b).reshape(count, width // (batch_total * rows_own), rows_own)
        for b in range(batch_total)
    ]
    return jnp.stack(blocks, axis=2).reshape(count, width)


def gather_pieces(block):
    pieces = [block]
    for bit in reversed(batch_bits()):
        pieces = pieces + [swapped(piece, "batch", bit) for piece in pieces]
    return pieces


def gather_batch(block):
    return jnp.concatenate(gather_pieces(block), axis=0)


def partial_sum_batch(left, right):
    width = left.shape[1]
    held = None
    sends = []

    def product(first, last):
        part = contract_rows(left[:, first:last], right)
        return part if held is None else part + held[first:last]

    for bit in batch_bits():
        half = width // 2
        sends.append(product(half, width).astype(jnp.bfloat16))
        got = swapped(sends[-1], "batch", bit).astype(jnp.float32)
        held = got if held is None else held[:half] + got
        width = half
    return (product(0, width).astype(jnp.bfloat16), sends)


def scatter_sum_batch(blocks):
    held = blocks
    for bit in batch_bits():
        pairs = held.reshape((held.shape[0] // 2, 2) + held.shape[1:])
        got = swapped(pairs[:, 1], "batch", bit)
        held = (pairs[:, 0].astype(jnp.float32) + got.astype(jnp.float32)).astype(jnp.bfloat16)
    return held[0]


def seqs_in_block(columns, seq_total):
    return max(1, min(seq_total, 1024 // columns))


def rounded_by_owner(weight, groups):
    rows_own, width = weight.shape
    seq_total = lax.axis_size("seq")
    columns = width // (groups * seq_total)
    if columns % LANES:
        blocks = weight.astype(jnp.bfloat16).reshape(rows_own, groups, seq_total, columns)
        return jnp.transpose(blocks, (2, 0, 1, 3)).reshape(seq_total, rows_own, groups * columns)
    taken = seqs_in_block(columns, seq_total)
    steps = seq_total // taken

    def kernel(weight_ref, out_ref):
        for place in range(taken):
            out_ref[place] = weight_ref[:, place * columns : (place + 1) * columns].astype(
                jnp.bfloat16
            )

    return pl.pallas_call(
        kernel,
        grid=(groups, steps),
        in_specs=[pl.BlockSpec((rows_own, taken * columns), lambda g, j: (0, g * steps + j))],
        out_specs=pl.BlockSpec((taken, rows_own, columns), lambda g, j: (j, 0, g)),
        out_shape=jax.ShapeDtypeStruct(
            (seq_total, rows_own, groups * columns), jnp.bfloat16
        ),
        cost_estimate=pl.CostEstimate(flops=0, bytes_accessed=weight.size * 6, transcendentals=0),
    )(weight)


def to_column_owners(blocks):
    got = lax.all_to_all(blocks, "seq", 0, 0, tiled=True)
    return got.reshape(-1, blocks.shape[2])


def to_row_owners(grad):
    seq_total = lax.axis_size("seq")
    blocks = grad.reshape(seq_total, grad.shape[0] // seq_total, grad.shape[1])
    return lax.all_to_all(blocks, "seq", 0, 0, tiled=True)


def adam_by_owner(weight, first_moment, second, gradient, groups, step_rate, skipped=0):
    rows_own, width = weight.shape
    seq_total = lax.axis_size("seq")
    columns = width // (groups * seq_total)
    if columns % LANES:
        own = gradient[:, :, skipped * columns : (skipped + groups) * columns]
        natural = jnp.transpose(
            own.reshape(seq_total, rows_own, groups, columns), (1, 2, 0, 3)
        ).reshape(rows_own, width)
        return adam_update(weight, first_moment, second, natural.astype(jnp.float32), step_rate)
    taken = seqs_in_block(columns, seq_total)
    steps = seq_total // taken

    def kernel(weight_ref, first_ref, second_ref, gradient_ref, *out_refs):
        for place in range(taken):
            here = slice(place * columns, (place + 1) * columns)
            results = adam_update(
                weight_ref[:, here],
                first_ref[:, here],
                second_ref[:, here],
                gradient_ref[place].astype(jnp.float32),
                step_rate,
            )
            for out_ref, result in zip(out_refs, results):
                out_ref[:, here] = result

    whole = pl.BlockSpec((rows_own, taken * columns), lambda g, j: (0, g * steps + j))
    return pl.pallas_call(
        kernel,
        grid=(groups, steps),
        in_specs=[whole] * 3 + [
            pl.BlockSpec((taken, rows_own, columns), lambda g, j: (j, 0, g + skipped))
        ],
        out_specs=[whole] * 3,
        out_shape=[jax.ShapeDtypeStruct(weight.shape, jnp.float32)] * 3,
        cost_estimate=pl.CostEstimate(
            flops=weight.size * 15, bytes_accessed=weight.size * 26, transcendentals=weight.size
        ),
    )(weight, first_moment, second, gradient)


def swap_halves(values):
    lane = lax.broadcasted_iota(jnp.int32, values.shape, 1)
    return jnp.where(
        lane % HD < HD // 2,
        pltpu.roll(values, LANES - HD // 2, 1),
        pltpu.roll(values, HD // 2, 1),
    )


def of_head(values, head, axis=1):
    lane = lax.broadcasted_iota(jnp.int32, values.shape, axis)
    return jnp.where(lane // HD == head, values, jnp.zeros_like(values))


def allowed_here(starts_ref, first, rows):
    shape = (rows, QUERY_ROWS)
    key = lax.broadcasted_iota(jnp.int32, shape, 0)
    query = lax.broadcasted_iota(jnp.int32, shape, 1) + first
    return (key <= query) & (key >= starts_ref[:, first : first + QUERY_ROWS])


def mm_last(left, right):
    return lax.dot_general(
        left, right, (((1,), (1,)), ((), ())), preferred_element_type=jnp.float32
    )


def attend_kernel(
    query_in, key_in, value_in, cos_ref, sin_ref, starts_ref,
    out_ref, low_ref, query_ref, key_ref, value_ref, total_ref, key_own, value_turned,
):
    length = query_in.shape[0]
    cos, sin = cos_ref[...], sin_ref[...]
    raw_query, raw_key = query_in[...], key_in[...]
    query_ref[...] = (raw_query * cos + swap_halves(raw_query) * sin).astype(jnp.bfloat16) * HD**-0.5
    key_ref[...] = (raw_key * cos + swap_halves(raw_key) * sin).astype(jnp.bfloat16)
    value_ref[...] = value_in[...].astype(jnp.bfloat16)
    turned = value_in[...].T
    for head in range(2):
        key_own[head] = of_head(key_ref[...], head)
        value_turned[head] = of_head(turned, head, 0).astype(jnp.bfloat16)
    for first in range(0, length, QUERY_ROWS):
        last = first + QUERY_ROWS
        allowed = allowed_here(starts_ref, first, last)
        weighted = jnp.zeros((LANES, QUERY_ROWS), jnp.float32)
        for head in range(2):
            scores = mm_last(key_own[head, :last], query_ref[first:last])
            scores = jnp.where(allowed, scores, masked_score)
            top = jnp.max(scores, axis=0, keepdims=True)
            powers = jnp.exp(scores - top)
            total = jnp.sum(powers, axis=0, keepdims=True)
            probs = (powers * (1.0 / total)).astype(jnp.bfloat16)
            weighted += matmul(value_turned[head, :, :last], probs)
            total_ref[0, head : head + 1, first:last] = top + jnp.log(total)
        attended = weighted.T
        out_ref[first:last] = attended
        low_ref[first:last] = attended.astype(jnp.bfloat16)


def attend_back_kernel(
    query_ref, key_ref, value_ref, grad_ref, attended_ref, total_ref, cos_ref, sin_ref, starts_ref,
    out_ref, key_own, value_own, key_turned, key_grad, value_grad,
):
    length = query_ref.shape[0]
    pair = pl.program_id(0)
    width = out_ref.shape[1] // 3
    turned = key_ref[...].astype(jnp.float32).T
    for head in range(2):
        key_own[head] = of_head(key_ref[...], head)
        value_own[head] = of_head(value_ref[...], head)
        key_turned[head] = of_head(turned, head, 0).astype(jnp.bfloat16)
    key_grad[...] = jnp.zeros_like(key_grad)
    value_grad[...] = jnp.zeros_like(value_grad)

    def undone(values, rows):
        back = values * cos_ref[rows] - swap_halves(values) * sin_ref[rows]
        return back.astype(jnp.bfloat16)

    def lanes(group):
        return pl.ds(pl.multiple_of(group * width + pair * LANES, LANES), LANES)

    for first in range(0, length, QUERY_ROWS):
        last = first + QUERY_ROWS
        rows = slice(first, last)
        allowed = allowed_here(starts_ref, first, last)
        grad, query = grad_ref[rows], query_ref[rows]
        products = (grad.astype(jnp.float32) * attended_ref[rows]).T
        query_grad = jnp.zeros((LANES, QUERY_ROWS), jnp.float32)
        for head in range(2):
            scores = mm_last(key_own[head, :last], query)
            probs = jnp.where(allowed, jnp.exp(scores - total_ref[0, head : head + 1, rows]), 0.0)
            delta = jnp.sum(products[head * HD : (head + 1) * HD], axis=0, keepdims=True)
            grad_probs = mm_last(value_own[head, :last], grad)
            grad_scores = (probs * (grad_probs - delta)).astype(jnp.bfloat16)
            value_grad[:last] += matmul(probs.astype(jnp.bfloat16), of_head(grad, head))
            key_grad[:last] += matmul(grad_scores, of_head(query, head))
            query_grad += matmul(key_turned[head, :, :last], grad_scores)
        out_ref[rows, lanes(0)] = undone(query_grad.T * HD**-0.5, rows)
    everything = slice(0, length)
    out_ref[:, lanes(1)] = undone(key_grad[...], everything)
    out_ref[:, lanes(2)] = value_grad[...].astype(jnp.bfloat16)


def attend_forward(qkv, cos_table, sin_table, starts):
    length, width = qkv.shape[0], qkv.shape[1] // 3
    pairs = width // LANES
    whole = pl.BlockSpec((length, LANES), lambda p: (0, 0))
    own = pl.BlockSpec((length, LANES), lambda p: (0, p))
    low = jax.ShapeDtypeStruct((length, width), jnp.bfloat16)
    work = pairs * length * length
    return pl.pallas_call(
        attend_kernel,
        grid=(pairs,),
        in_specs=[
            own,
            pl.BlockSpec((length, LANES), lambda p: (0, pairs + p)),
            pl.BlockSpec((length, LANES), lambda p: (0, 2 * pairs + p)),
            whole,
            whole,
            pl.BlockSpec((1, length), lambda p: (0, 0)),
        ],
        out_specs=[own] * 5 + [pl.BlockSpec((1, 2, length), lambda p: (p, 0, 0))],
        out_shape=[
            jax.ShapeDtypeStruct((length, width), jnp.float32),
            low,
            low,
            low,
            low,
            jax.ShapeDtypeStruct((pairs, 2, length), jnp.float32),
        ],
        scratch_shapes=[
            pltpu.VMEM((2, length, LANES), jnp.bfloat16),
            pltpu.VMEM((2, LANES, length), jnp.bfloat16),
        ],
        compiler_params=pltpu.CompilerParams(vmem_limit_bytes=48 << 20),
        cost_estimate=pl.CostEstimate(
            flops=8 * work * LANES, bytes_accessed=qkv.size * 8, transcendentals=2 * work
        ),
    )(qkv, qkv, qkv, cos_table, sin_table, starts)


def attend_backward(query, key, value, grad, attended, total, cos_table, sin_table, starts):
    length, width = query.shape
    pairs = width // LANES
    whole = pl.BlockSpec((length, LANES), lambda p: (0, 0))
    own = pl.BlockSpec((length, LANES), lambda p: (0, p))
    work = pairs * length * length
    return pl.pallas_call(
        attend_back_kernel,
        grid=(pairs,),
        in_specs=[own] * 5
        + [
            pl.BlockSpec((1, 2, length), lambda p: (p, 0, 0)),
            whole,
            whole,
            pl.BlockSpec((1, length), lambda p: (0, 0)),
        ],
        out_specs=pl.BlockSpec((length, 3 * width), lambda p: (0, 0)),
        out_shape=jax.ShapeDtypeStruct((length, 3 * width), jnp.bfloat16),
        scratch_shapes=[
            pltpu.VMEM((2, length, LANES), jnp.bfloat16),
            pltpu.VMEM((2, length, LANES), jnp.bfloat16),
            pltpu.VMEM((2, LANES, length), jnp.bfloat16),
            pltpu.VMEM((length, LANES), jnp.float32),
            pltpu.VMEM((length, LANES), jnp.float32),
        ],
        compiler_params=pltpu.CompilerParams(vmem_limit_bytes=48 << 20),
        cost_estimate=pl.CostEstimate(
            flops=20 * work * LANES, bytes_accessed=query.size * 16, transcendentals=2 * work
        ),
    )(query, key, value, grad, attended, total, cos_table, sin_table, starts)


def on_device(
    tokens,
    out_grad,
    doc_lengths,
    qkv_weight,
    qkv_first,
    qkv_second,
    out_weight,
    out_first,
    out_second,
    gate_up_weight,
    gate_up_first,
    gate_up_second,
    down_weight,
    down_first,
    down_second,
    gains,
    gain_first,
    gain_second,
):
    local_rows = tokens.shape[1]
    model_width = tokens.shape[2]
    rows_own = qkv_weight.shape[0]
    seq_total = lax.axis_size("seq")
    batch_total = lax.axis_size("batch")
    head_width = model_width // seq_total
    heads = head_width // HD
    length = local_rows * seq_total
    hidden = down_weight.shape[1] // seq_total
    score_scale = HD ** (-0.5)
    positions = jnp.arange(length, dtype=jnp.int32)
    ends = jnp.cumsum(doc_lengths[0])
    starts = jnp.max(jnp.where(positions[:, None] >= ends[None, :], ends[None, :], 0), axis=1)
    cos_table, sin_table = rope_tables(positions)
    in_pairs = head_width % LANES == 0 and length % QUERY_ROWS == 0
    if in_pairs:
        sign = jnp.where(jnp.arange(HD) < HD // 2, -1.0, 1.0)
        cos_pair = jnp.tile(cos_table, (1, 2))
        sin_pair = jnp.tile(sin_table * sign, (1, 2))

    def split_heads(columns):
        return jnp.transpose(columns.reshape(length, heads, HD), (1, 0, 2))

    def join_heads(values):
        return jnp.transpose(values, (1, 0, 2)).reshape(length, head_width)

    def allowed_pairs():
        return (
            (positions[None, :] <= positions[:, None]) & (positions[None, :] >= starts[:, None])
        )[None]

    def attention(qkv):
        if in_pairs:
            attended, low, *kept = attend_forward(qkv, cos_pair, sin_pair, starts[None])
            return (low, (attended, kept))
        query = split_heads(qkv[:, :head_width])
        query = apply_rope(query, cos_table, sin_table).astype(jnp.bfloat16)
        key = split_heads(qkv[:, head_width : 2 * head_width])
        key = apply_rope(key, cos_table, sin_table).astype(jnp.bfloat16)
        value = split_heads(qkv[:, 2 * head_width :]).astype(jnp.bfloat16)
        scores = jnp.einsum("hqd,hkd->hqk", query, key, preferred_element_type=jnp.float32)
        scores = jnp.where(allowed_pairs(), scores * score_scale, masked_score)
        probs = jax.nn.softmax(scores, axis=-1)
        attended = jnp.einsum(
            "hqk,hkd->hqd", probs.astype(jnp.bfloat16), value, preferred_element_type=jnp.float32
        )
        return (join_heads(attended.astype(jnp.bfloat16)), (attended, (query, key, value, probs)))

    def attention_back(grad, kept):
        if in_pairs:
            attended, (query, key, value, total) = kept
            return attend_backward(
                query, key, value, grad, attended, total, cos_pair, sin_pair, starts[None]
            )
        attended, (query, key, value, probs) = kept
        grad = split_heads(grad)
        delta = jnp.sum(grad.astype(jnp.float32) * attended, axis=-1, keepdims=True)
        grad_probs = jnp.einsum("hqd,hkd->hqk", grad, value, preferred_element_type=jnp.float32)
        grad_scores = (probs * (grad_probs - delta)).astype(jnp.bfloat16)

        def over_queries(left, right):
            return jnp.einsum("hqk,hqd->hkd", left, right, preferred_element_type=jnp.float32)

        grad_value = over_queries(probs.astype(jnp.bfloat16), grad)
        grad_key = over_queries(grad_scores, query) * score_scale
        grad_query = (
            jnp.einsum("hqk,hkd->hqd", grad_scores, key, preferred_element_type=jnp.float32)
            * score_scale
        )
        return jnp.concatenate(
            [
                join_heads(undo_rope(grad_query, cos_table, sin_table)),
                join_heads(undo_rope(grad_key, cos_table, sin_table)),
                join_heads(grad_value),
            ],
            axis=1,
        ).astype(jnp.bfloat16)

    far = seq_total // 2
    first_row = lax.axis_index("seq") * local_rows
    gains_here = to_relative(gains, rows_own)
    tokens_here = to_relative(tokens[0], rows_own)
    grads_here = to_relative(out_grad[0], rows_own)
    out_here = jnp.stack(batch_columns(out_weight.astype(jnp.bfloat16), rows_own))
    out_here = lax.all_to_all(out_here, "batch", 0, 0, tiled=True).reshape(head_width, -1)
    out_here = with_rows(out_here, local_rows)
    qkv_low = rounded_by_owner(qkv_weight, 3)
    gate_low = rounded_by_owner(gate_up_weight, 2)
    down_low = rounded_by_owner(down_weight, 1)
    qkv_block = to_column_owners(qkv_low)
    tokens_all, grads_all, out_all = ring_gather(
        after_all([tokens_here, grads_here, out_here], (qkv_low, gate_low, down_low)),
        ((qkv_block,),),
    )
    tokens_all, grads_all = stacked_rows(tokens_all), stacked_rows(grads_all)
    out_all = stacked_rows(
        {offset: with_rows(block, head_width) for offset, block in out_all.items()}
    )
    qkv_full = gather_batch(qkv_block)
    gate_block = to_column_owners(after(gate_low, tokens_all))
    down_block = to_column_owners(after(down_low, gate_block))

    inputs = tokens_all.astype(jnp.float32)
    act_one = (unit_rows(inputs)[0] * gains_here[0]).astype(jnp.bfloat16)
    qkv = matmul(act_one, qkv_full)
    attn_own, attn_kept = attention(qkv)

    out_full = jnp.concatenate(gather_pieces(out_all), axis=1)

    attn_own_late = after(attn_own, gate_block)
    attn_all = stacked_columns(ring_gather([attn_own_late], ((down_block,),))[0])
    gate_full = gather_batch(gate_block)
    down_full = gather_batch(down_block)
    middle_all = inputs + matmul(attn_all, out_full)
    act_two = (unit_rows(middle_all)[0] * gains_here[1]).astype(jnp.bfloat16)

    def feed_forward(rows, grads):
        gate_up = matmul(rows, gate_full)
        gate_part = gate_up[:, :hidden]
        up_part = gate_up[:, hidden:]
        sigmoid_gate = jax.nn.sigmoid(gate_part)
        silu_gate = gate_part * sigmoid_gate
        hidden_low = (silu_gate * up_part).astype(jnp.bfloat16)
        grad_hidden = matmul(grads, down_full)
        grad_gate = (
            grad_hidden * up_part * (sigmoid_gate * (1.0 + gate_part * (1.0 - sigmoid_gate)))
        )
        grad_up = grad_hidden * silu_gate
        grad_gate_up = jnp.concatenate([grad_gate, grad_up], axis=1).astype(jnp.bfloat16)
        grad_two = contract_cols(grad_gate_up, gate_full).astype(jnp.bfloat16)
        block_part = contract_cols(hidden_low, down_full).astype(jnp.bfloat16)
        return (grad_gate_up, hidden_low, grad_two, block_part)

    offsets = [far] + [sign * step for step in range(far - 1, 0, -1) for sign in (1, -1)] + [0]
    grad_gate_up, hidden_low, grad_two, block_part = feed_forward(act_two, grads_all)
    hidden_late, gate_up_late = after_all((hidden_low, grad_gate_up), (grad_two, block_part))
    down_own, down_sends = partial_sum_batch(grads_all, hidden_late)
    gate_own, gate_sends = partial_sum_batch(act_two, gate_up_late)
    grad_two, block_rest = ring_scatter_sum(
        [
            {offset: ring_rows(whole, [offset]) for offset in offsets}
            for whole in (grad_two, block_part)
        ],
        ((down_sends[0], gate_sends[0]), (down_sends[-1], gate_sends[-1]), (down_own,)),
    )

    def own_rows(whole):
        return lax.dynamic_slice_in_dim(whole, first_row, local_rows, 0)

    middle = own_rows(middle_all)
    unit_two, scale_two = unit_rows(middle)
    block_out = from_relative((middle + block_rest).astype(jnp.bfloat16), rows_own)
    grad_mid_norm, gain_two_grad = norm_back(grad_two, unit_two, scale_two, gains_here[1])
    grad_middle = grads_here.astype(jnp.float32) + grad_mid_norm
    grad_attn_low = grad_middle.astype(jnp.bfloat16)
    grad_heads = contract_cols(grad_attn_low, out_full).astype(jnp.bfloat16)
    by_owner = jnp.concatenate(
        [
            grad_heads.reshape(local_rows, seq_total, head_width),
            from_relative(grad_attn_low, rows_own).reshape(local_rows, seq_total, head_width),
        ],
        axis=2,
    )
    got = lax.all_to_all(jnp.transpose(by_owner, (1, 0, 2)), "seq", 0, 0, tiled=True)
    got = got.reshape(length, 2 * head_width)
    grad_heads = got[:, :head_width]
    grad_attn_own = got[:, head_width:]
    down_grad = to_row_owners(after(down_own, got))
    gate_grad = to_row_owners(after(gate_own, down_grad))

    grad_qkv = attention_back(grad_heads, attn_kept)
    qkv_own, qkv_sends = partial_sum_batch(act_one, grad_qkv)
    out_part = contract_rows(attn_all, grad_attn_own).astype(jnp.bfloat16)
    out_part = out_part.reshape(seq_total, batch_total, rows_own, head_width)
    out_part = [
        out_part[:, b].reshape(seq_total * rows_own, head_width) for b in range(batch_total)
    ]
    out_own = scatter_sum_batch(jnp.stack([of_offset(out_part, m) for m in range(batch_total)]))
    grad_qkv = after(grad_qkv, qkv_sends[0], out_own)
    grad_one_part = contract_cols(grad_qkv, qkv_full)
    gain_one_part = jnp.sum(grad_one_part * act_one.astype(jnp.float32), axis=0)
    gain_grad = jnp.stack([gain_one_part / gains_here[0], gain_two_grad])
    gain_grad = sum_everywhere(from_relative(gain_grad, rows_own))
    down_m, down_s, down_w = adam_by_owner(
        down_weight, down_first, down_second, down_grad, 1, rate_down
    )
    grad_one = ring_scatter_one(
        grad_one_part.astype(jnp.bfloat16), ((qkv_sends[-1], down_m), (gate_grad,), (qkv_own,))
    )
    unit_one, scale_one = unit_rows(tokens_here.astype(jnp.float32))
    grad_in_norm = norm_back(grad_one, unit_one, scale_one, gains_here[0])[0]
    input_grad = from_relative(grad_middle + grad_in_norm, rows_own)
    qkv_grad = to_row_owners(
        jnp.concatenate([after(qkv_own, gate_grad), out_own], axis=1)
    )

    qkv_m, qkv_s, qkv_w = adam_by_owner(
        qkv_weight, qkv_first, qkv_second, qkv_grad, 3, rate_qkv
    )
    out_m, out_s, out_w = adam_by_owner(
        out_weight, out_first, out_second, qkv_grad, 1, rate_out, skipped=3
    )
    gate_m, gate_s, gate_w = adam_by_owner(
        gate_up_weight, gate_up_first, gate_up_second, gate_grad, 2, rate_gate
    )
    gain_m, gain_s, gain_w = adam_update(gains, gain_first, gain_second, gain_grad, rate_gain)
    return (
        block_out[None],
        input_grad[None],
        qkv_m,
        qkv_s,
        qkv_w,
        out_m,
        out_s,
        out_w,
        gate_m,
        gate_s,
        gate_w,
        down_m,
        down_s,
        down_w,
        gain_m,
        gain_s,
        gain_w,
    )


def solution(mesh):
    rows = P(("seq", "batch"), None)
    blocks = P("batch", "seq", None)
    return jax.shard_map(
        on_device,
        mesh=mesh,
        in_specs=(blocks, blocks, P("batch", None)) + (rows,) * 12 + (P(),) * 3,
        out_specs=(blocks, blocks) + (rows,) * 12 + (P(),) * 3,
        check_vma=False,
    )
```

time: 3870 us -> 743 us (0.19)
  waiting for transfers between devices: 3200 us -> 281 us
  matrix products: 244 us -> 122 us
  Pallas kernels: 0 us -> 69.5 us
  starting transfers between devices: 177 us -> 114 us
  blocking collectives: 62.2 us -> 0 us
  other arithmetic: 112 us -> 63.2 us
    reduce_scatter x2 -> x0, waiting for transfers between devices: 2150 us -> none  [the longest x1 1600 us: on_device(): lax.psum_scatter(stacked_terms(ffn_left, ffn_right), ('seq', 'batch'), sc...]
    all_gather x6 -> x0, waiting for transfers between devices: 853 us -> none  [the longest x1 353 us: on_device(): lax.all_gather(gate_up_weight.astype(jnp.bfloat16), ('seq', 'batch'), axi...]
    ppermute x32 -> x64, starting transfers between devices: 177 us -> 73.2 us  [the longest x44 60.2 us: ring_shift(): return lax.ppermute(value, 'seq', pairs)]
    pallas_call x0 -> x9, Pallas kernels: none -> 69.5 us  [the longest x4 32.6 us: adam_by_owner(): pl.pallas_call(kernel, grid=(groups, steps), in_specs=[whole] * 3 + [pl.B...]
    all_to_all x0 -> x9, waiting for transfers between devices: none -> 63 us  [the longest x3 36.3 us: to_column_owners(): got = lax.all_to_all(blocks, 'seq', 0, 0, tiled=True)]
    psum x1 -> x0, blocking collectives: 62.2 us -> none  [on_device(): lax.psum(jnp.stack([gain_one_grad, gain_two_grad]), ('seq', 'batch'))]
    dot_general x2 -> x10, matrix products: 94.1 us -> 39.3 us  [contract_rows(): lax.dot_general(left_side, right_side, (((0,), (0,)), ((), ())), preferre...]
    all_to_all x0 -> x9, starting transfers between devices: none -> 41.1 us  [the longest x3 16 us: to_column_owners(): got = lax.all_to_all(blocks, 'seq', 0, 0, tiled=True)]
  transfers between devices with their start and end apart: 40 -> 73, of which waited for: 34 -> 40; matrix products, arithmetic and copies ran while one was open for 6% -> 24% of each run, Pallas kernels for 0% -> 8%
where the time goes in v1:
time: 743 us; the launch traced here: 728 us
  waiting for transfers between devices  281 us (38%)
  matrix products  122 us (16%)
  starting transfers between devices  114 us (15%)
  Pallas kernels  69.5 us (9%)
  local copies, waits for them, and re-layouts  66.5 us (9%)
  other arithmetic  63.2 us (9%)
  between operations  11.5 us (2%)
    ppermute x44, waiting for transfers between devices, ring_shift(): return lax.ppermute(value, 'seq', pairs)  201 us
    ppermute x44, starting transfers between devices, ring_shift(): return lax.ppermute(value, 'seq', pairs)  60.2 us
    dot_general x4, matrix products, matmul(): return jnp.dot(left_side, right_side, preferred_element_type=jnp.float32)  45.4 us
    dot_general x10, matrix products, contract_rows(): lax.dot_general(left_side, right_side, (((0,), (0,)), ((), ())), preferre...  39.3 us
    dot_general x4, matrix products, contract_cols(): lax.dot_general(left_side, right_side, (((1,), (1,)), ((), ())), preferre...  37.5 us
    all_to_all x3, waiting for transfers between devices, to_column_owners(): got = lax.all_to_all(blocks, 'seq', 0, 0, tiled=True)  36.3 us
    pallas_call x4, Pallas kernels, adam_by_owner(): pl.pallas_call(kernel, grid=(groups, steps), in_specs=[whole] * 3 + [pl.B...  32.6 us
    all_to_all x1, waiting for transfers between devices, on_device(): lax.all_to_all(jnp.transpose(by_owner, (1, 0, 2)), 'seq', 0, 0, tiled=True)  19.9 us
  transfers between devices with their start and end apart: 73, of which 40 were waited for; matrix products, arithmetic and copies ran while one was open for 24% of the time, Pallas kernels for 8%

profile of v1, /device:TPU:0, one launch (start us, length us, event | category | flops | bytes accessed | tf_op | source)
XLA Modules:
  0.0 728.2 jit_solution(4846840267504694839)
XLA Ops:
  22.6 9.8 %shard_map.810 = bf16[8,64,2048]{2,1,0:T(8,128)(2,1)} custom-call(f32[64,16384]{1,0:T(8,128)} %weight_ref.13), custom_call_target="tpu_custom_call" | custom-call | bytes 6291456 | tf_op jit(solution)/shard_map/pallas_call | solution.py:331
  33.4 6.5 all-to-all-start.1
  51.1 10.5 %all-to-all-done.1 = bf16[8,64,768]{2,1,0:T(8,128)(2,1)} async-done(((bf16[8,64,768]{2,1,0:T(8,128)(2,1)}), bf16[8,64,768]{2,1,0:T(8,128)(2,1)}, u32[]{:S(2)}, u32[]{:S(2)}) %all-to-all-start.1) | async-done | bytes 786464 | tf_op jit(solution)/shard_map/all_to_all | solution.py:344
  61.6 22.9 %collective-permute-done.1 = bf16[128,5120]{1,0:T(8,128)(2,1)} collective-permute-done((bf16[128,5120]{1,0:T(8,128)(2,1)}, bf16[128,5120]{1,0:T(8,128)(2,1)}, u32[]{:S(2)}, u32[]{:S(2)}) %collective-permute-start.1) | collective-permute-done | bytes 1310752 | tf_op jit(solution)/shard_map/ppermute | solution.py:102
  108.4 8.6 %collective-permute-done.2 = bf16[128,5120]{1,0:T(8,128)(2,1)} collective-permute-done((bf16[128,5120]{1,0:T(8,128)(2,1)S(1)}, bf16[128,5120]{1,0:T(8,128)(2,1)}, u32[]{:S(2)}, u32[]{:S(2)}) %collective-permute-start.2) | collective-permute-done | bytes 1310752 | tf_op jit(solution)/shard_map/ppermute | solution.py:102
  126.6 20.3 %collective-permute-done.4 = bf16[128,5120]{1,0:T(8,128)(2,1)S(1)} collective-permute-done((bf16[128,5120]{1,0:T(8,128)(2,1)}, bf16[128,5120]{1,0:T(8,128)(2,1)S(1)}, u32[]{:S(2)}, u32[]{:S(2)}) %collective-permute-start.4) | collective-permute-done | bytes 1310752 | tf_op jit(solution)/shard_map/ppermute | solution.py:102
  151.5 10.3 %collective-permute-done.6 = bf16[128,2560]{1,0:T(8,128)(2,1)S(1)} collective-permute-done((bf16[128,2560]{1,0:T(8,128)(2,1)S(1)}, bf16[128,2560]{1,0:T(8,128)(2,1)S(1)}, u32[]{:S(2)}, u32[]{:S(2)}) %collective-permute-start.6) | collective-permute-done | bytes 655392 | tf_op jit(solution)/shard_map/ppermute | solution.py:102
  190.5 25.8 %all-to-all-done.2 = bf16[8,64,2048]{2,1,0:T(8,128)(2,1)} async-done(((bf16[8,64,2048]{2,1,0:T(8,128)(2,1)}), bf16[8,64,2048]{2,1,0:T(8,128)(2,1)}, u32[]{:S(2)}, u32[]{:S(2)}) %all-to-all-start.2) | async-done | bytes 2097184 | tf_op jit(solution)/shard_map/all_to_all | solution.py:344
  220.6 8.2 %fusion.51.query_in.key_in.value_in = f32[1024,768]{1,0:T(8,128)} fusion(bf16[1024,2048]{1,0:T(8,128)(2,1)} %fusion.2, bf16[512,768]{1,0:T(8,128)(2,1)} %collective-permute-done.9, bf16[512,768]{1,0:T(8,128)(2,1)} %collective-permute-done.8, bf16[512,768]{1,0:T(8,128)(2,1)} %collective-permute-done.7, bf16[512,768]{1,0:T(8,128)(2,1)} %bitcast.14), kind=kOutput, calls=%fused_computation.91 | convolution fusion | flops 3233808384 | bytes 10485760 | tf_op jit(solution)/shard_map/dot_general | solution.py:75
  228.7 8.8 %shard_map.812 = (f32[1024,256]{1,0:T(8,128)S(1)}, bf16[1024,256]{1,0:T(8,128)(2,1)S(1)}, bf16[1024,256]{1,0:T(8,128)(2,1)S(1)}, bf16[1024,256]{1,0:T(8,128)(2,1...) custom-call(f32[1024,768]{1,0:T(8,128)} %fusion.51.query_in.key_in.value_in, ...), custom_call_target="tpu_custom_call" | custom-call | flops 2147483648 | bytes 6291456 | tf_op jit(solution)/shard_map/pallas_call | solution.py:505
  242.7 13.6 %collective-permute-done.11 = bf16[1024,256]{1,0:T(8,128)(2,1)S(1)} collective-permute-done((bf16[1024,256]{1,0:T(8,128)(2,1)S(1)}, bf16[1024,256]{1,0:T(8,128)(2,1)S(1)}, u32[]{:S(2)}, u32[]{:S(2)}) %collective-permute-start.11) | collective-permute-done | bytes 524320 | tf_op jit(solution)/shard_map/ppermute | solution.py:102
  259.1 11.2 %collective-permute-done.12 = bf16[1024,256]{1,0:T(8,128)(2,1)S(1)} collective-permute-done((bf16[1024,256]{1,0:T(8,128)(2,1)}, bf16[1024,256]{1,0:T(8,128)(2,1)S(1)}, u32[]{:S(2)}, u32[]{:S(2)}) %collective-permute-start.12) | collective-permute-done | bytes 524320 | tf_op jit(solution)/shard_map/ppermute | solution.py:102
  273.7 8.8 %collective-permute-done.14 = bf16[1024,256]{1,0:T(8,128)(2,1)S(1)} collective-permute-done((bf16[1024,256]{1,0:T(8,128)(2,1)S(1)}, bf16[1024,256]{1,0:T(8,128)(2,1)S(1)}, u32[]{:S(2)}, u32[]{:S(2)}) %collective-permute-start.14) | collective-permute-done | bytes 524320 | tf_op jit(solution)/shard_map/ppermute | solution.py:102
  301.5 10.5 %collective-permute-done.25 = bf16[512,1024]{1,0:T(8,128)(2,1)} collective-permute-done((bf16[512,1024]{1,0:T(8,128)(2,1)}, bf16[512,1024]{1,0:T(8,128)(2,1)}, u32[]{:S(2)}, u32[]{:S(2)}) %collective-permute-start.25) | collective-permute-done | bytes 1048608 | tf_op jit(solution)/shard_map/ppermute | solution.py:91
  312.0 14.6 %multiply_reduce_fusion.1 = (f32[1024]{0:T(1024)S(1)}, f32[1024,2048]{1,0:T(8,128)}) fusion(bf16[1024,2048]{1,0:T(8,128)(2,1)S(1)} %maximum_dynamic-update-slice_fusion, bf16[2048,512]{1,0:T(8,128)(2,1)} %collective-permute-done.21, bf16[2048,512]{1,0:T(8,128)(2,1)} %collective-permute-done.20, bf16[2048,512]{1,0:T(8,128)(2,1)} %collective-permute-done.19, ...), kind=kOutput, calls=%fused_computation.10 | convolution fusion | flops 8631876608 | bytes 25169920 | tf_op jit(solution)/shard_map/dot_general | solution.py:75
  330.8 12.4 %fusion.24 = f32[1024,2048]{1,0:T(8,128)S(1)} fusion(bf16[1024,2048]{1,0:T(8,128)(2,1)S(1)} %multiply_convert_fusion, bf16[512,2048]{1,0:T(8,128)(2,1)} %collective-permute-done.24, bf16[512,2048]{1,0:T(8,128)(2,1)} %collective-permute-done.23, bf16[512,2048]{1,0:T(8,128)(2,1)} %collective-permute-done.22, bf16[512,2048]{1,0:T(8,128)(2,1)} %bitcast.26), kind=kOutput, calls=%fused_computation.46 | convolution fusion | flops 8623489024 | bytes 20971520 | tf_op jit(solution)/shard_map/dot_general | solution.py:75
  343.3 10.2 %multiply_convert_fusion.2 = (bf16[1024,1024]{1,0:T(8,128)(2,1)S(1)}, bf16[1024,1024]{1,0:T(8,128)(2,1)S(1)}, bf16[1024,1024]{1,0:T(8,128)(2,1)}) fusion(f32[1024,2048]{1,0:T(8,128)S(1)} %fusion.24, bf16[1024,2048]{1,0:T(8,128)(2,1)} %get-tuple-element.275, bf16[512,1024]{1,0:T(8,128)(2,1)} %collective-permute-done.27, ...), kind=kOutput, calls=%fused_computation.19 | convolution fusion | flops 4327473152 | bytes 23068672 | tf_op jit(solution)/shard_map/dot_general | solution.py:75
  357.9 14.8 %convolution_convert_fusion = bf16[1024,2048]{1,0:T(8,128)(2,1)} fusion(bf16[512,2048]{1,0:T(8,128)(2,1)} %collective-permute-done.24, bf16[512,2048]{1,0:T(8,128)(2,1)} %collective-permute-done.23, bf16[512,2048]{1,0:T(8,128)(2,1)} %collective-permute-done.22, bf16[512,2048]{1,0:T(8,128)(2,1)} %bitcast.26, bf16[1024,1024]{1,0:T(8,128)(2,1)} %copy-done.27, ...), kind=kOutput, calls=%fused_computation.23 | convolution fusion | flops 8633974784 | bytes 16777216 | tf_op jit(solution)/shard_map/dot_general | solution.py:69
  372.7 9.4 %convolution_convert_fusion.2 = bf16[1024,2048]{1,0:T(8,128)(2,1)} fusion(bf16[1024,1024]{1,0:T(8,128)(2,1)} %get-tuple-element.86, bf16[512,1024]{1,0:T(8,128)(2,1)} %collective-permute-done.27, bf16[512,1024]{1,0:T(8,128)(2,1)} %collective-permute-done.26, bf16[512,1024]{1,0:T(8,128)(2,1)} %collective-permute-done.25, bf16[512,1024]{1,0:T(8,128)(2,1)} %bitcast.29), kind=kOutput, calls=%fused_computation.25 | convolution fusion | flops 4313841664 | bytes 10485760 | tf_op jit(solution)/shard_map/dot_general | solution.py:69
  394.8 7.4 %collective-permute-done.28 = bf16[128,2048]{1,0:T(8,128)(2,1)S(1)} collective-permute-done((bf16[128,2048]{1,0:T(8,128)(2,1)S(1)}, bf16[128,2048]{1,0:T(8,128)(2,1)S(1)}, u32[]{:S(2)}, u32[]{:S(2)}) %collective-permute-start.28) | collective-permute-done | bytes 524320 | tf_op jit(solution)/shard_map/ppermute | solution.py:102
  412.4 11.3 %collective-permute-done.30 = bf16[128,2048]{1,0:T(8,128)(2,1)S(1)} collective-permute-done((bf16[128,2048]{1,0:T(8,128)(2,1)S(1)}, bf16[128,2048]{1,0:T(8,128)(2,1)S(1)}, u32[]{:S(2)}, u32[]{:S(2)}) %collective-permute-start.30) | collective-permute-done | bytes 524320 | tf_op jit(solution)/shard_map/ppermute | solution.py:102
  445.8 6.8 collective-permute-done.40
  473.3 9.6 %collective-permute-done.43 = bf16[128,2048]{1,0:T(8,128)(2,1)S(1)} collective-permute-done((bf16[128,2048]{1,0:T(8,128)(2,1)}, bf16[128,2048]{1,0:T(8,128)(2,1)S(1)}, u32[]{:S(2)}, u32[]{:S(2)}) %collective-permute-start.43) | collective-permute-done | bytes 524320 | tf_op jit(solution)/shard_map/ppermute | solution.py:102
  514.5 19.9 %all-to-all-done.4 = bf16[8,128,512]{1,2,0:T(8,128)(2,1)} async-done(((bf16[8,128,512]{1,2,0:T(8,128)(2,1)}), bf16[8,128,512]{1,2,0:T(8,128)(2,1)}, u32[]{:S(2)}, u32[]{:S(2)}) %all-to-all-start.4) | async-done | bytes 1048608 | tf_op jit(solution)/shard_map/all_to_all | solution.py:751
  544.2 8.6 %shard_map.813 = bf16[1024,768]{1,0:T(8,128)(2,1)S(1)} custom-call(bf16[1024,256]{1,0:T(8,128)(2,1)S(1)} %get-tuple-element.100.query_ref, bf16[1024,256]{1,0:T(8,128)(2,1)S(1)} %copy-done.1, bf16[1024,256]{1,0:T(8,128)(2,1)S(1)} %copy-done.3, bf16[1024,256]{1,0:T(8,128)(2,1)S(1)} %slice.459.grad_ref, f32[1024,256]{1,0:T(8,128)S(1)} %get-tuple-element.103.attended_ref, ...), custom_call_target="tpu_custom_call" | custom-call | flops 5368709120 | bytes 4194304 | tf_op jit(solution)/shard_map/pallas_call | solution.py:542
  555.9 7.4 %multiply_reduce_fusion = (f32[2048]{0:T(1024)S(1)}, bf16[1024,2048]{1,0:T(8,128)(2,1)}) fusion(bf16[1024,2048]{1,0:T(8,128)(2,1)S(1)} %copy-done.16, bf16[1024,768]{1,0:T(8,128)(2,1)S(1)} %shard_map.813, bf16[512,768]{1,0:T(8,128)(2,1)} %collective-permute-done.9, bf16[512,768]{1,0:T(8,128)(2,1)} %collective-permute-done.8, ...), kind=kOutput, calls=%fused_computation.8 | convolution fusion | flops 3242194944 | bytes 13115392 | tf_op jit(solution)/shard_map/dot_general | solution.py:69
  610.0 12.8 %collective-permute-done.46 = bf16[128,1024]{1,0:T(8,128)(2,1)S(1)} collective-permute-done((bf16[128,1024]{1,0:T(8,128)(2,1)S(1)}, bf16[128,1024]{1,0:T(8,128)(2,1)S(1)}, u32[]{:S(2)}, u32[]{:S(2)}) %collective-permute-start.46) | collective-permute-done | bytes 262176 | tf_op jit(solution)/shard_map/ppermute | solution.py:102
  622.8 9.2 %collective-permute-done.45 = bf16[128,1024]{1,0:T(8,128)(2,1)S(1)} collective-permute-done((bf16[128,1024]{1,0:T(8,128)(2,1)S(1)}, bf16[128,1024]{1,0:T(8,128)(2,1)S(1)}, u32[]{:S(2)}, u32[]{:S(2)}) %collective-permute-start.45) | collective-permute-done | bytes 262176 | tf_op jit(solution)/shard_map/ppermute | solution.py:102
  634.0 8.2 %shard_map.814 = (f32[64,8192]{1,0:T(8,128)}, f32[64,8192]{1,0:T(8,128)}, f32[64,8192]{1,0:T(8,128)}) custom-call(f32[64,8192]{1,0:T(8,128)} %weight_ref.10, f32[64,8192]{1,0:T(8,128)} %first_ref.4, f32[64,8192]{1,0:T(8,128)} %second_ref.4, bf16[8,64,1024]{2,1,0:T(8,128)(2,1)} %all-to-all-done.5.gradient_ref), custom_call_target="tpu_custom_call" | custom-call | flops 7864320 | bytes 13631488 | tf_op jit(solution)/shard_map/pallas_call | solution.py:381
  642.2 13.6 %collective-permute-start.48 = (bf16[128,1024]{1,0:T(8,128)(2,1)}, bf16[128,1024]{1,0:T(8,128)(2,1)}, u32[]{:S(2)}, u32[]{:S(2)}) collective-permute-start(bf16[128,1024]{1,0:T(8,128)(2,1)} %get-tuple-element.108), channel_id=1, source_target_pairs={{0,8},{8,16},{16,24},{24,28},{28,20},{20,12},{12,4},{4,0},{1,9},{9... | collective-permute-start | bytes 786440 | tf_op jit(solution)/shard_map/ppermute | solution.py:102
  697.5 15.6 %shard_map.817 = (f32[64,16384]{1,0:T(8,128)}, f32[64,16384]{1,0:T(8,128)}, f32[64,16384]{1,0:T(8,128)}) custom-call(f32[64,16384]{1,0:T(8,128)} %weight_ref.13, f32[64,16384]{1,0:T(8,128)} %first_ref.7, f32[64,16384]{1,0:T(8,128)} %second_ref.7, bf16[8,64,2048]{2,1,0:T(8,128)(2,1)} %all-to-all-done.6.gradient_ref), custom_call_target="tpu_custom_call" | custom-call | flops 15728640 | bytes 27262976 | tf_op jit(solution)/shard_map/pallas_call | solution.py:381
  721.6 6.3 shard_map.815
  (432 shorter events, 342.7 us)
Async XLA Ops:
  6.7 26.6 %all-to-all-start = ((bf16[4,64,512]{2,1,0:T(8,128)(2,1)}), bf16[4,64,512]{2,1,0:T(8,128)(2,1)S(1)}, u32[]{:S(2)}, u32[]{:S(2)}) async-start(bf16[4,64,512]{2,1,0:T(8,128)(2,1)} %pad_maximum_fusion.21), calls=%async_computation | async-start | bytes 524288 | tf_op jit(solution)/shard_map/all_to_all | solution.py:672
  33.4 28.2 %all-to-all-start.1 = ((bf16[8,64,768]{2,1,0:T(8,128)(2,1)}), bf16[8,64,768]{2,1,0:T(8,128)(2,1)}, u32[]{:S(2)}, u32[]{:S(2)}) async-start(bf16[8,64,768]{2,1,0:T(8,128)(2,1)} %shard_map.809), calls=%async_computation.1 | async-start | bytes 1572864 | tf_op jit(solution)/shard_map/all_to_all | solution.py:344
  48.0 36.5 %collective-permute-start.1 = (bf16[128,5120]{1,0:T(8,128)(2,1)}, bf16[128,5120]{1,0:T(8,128)(2,1)}, u32[]{:S(2)}, u32[]{:S(2)}) collective-permute-start(bf16[128,5120]{1,0:T(8,128)(2,1)} %constant_dynamic-update-slice_fusion.9), channel_id=1, source_target_pairs={{0,4},{8,0},{16,8},{24,16},{28,24},{20,28},{12,20},{4,12},{1,5},{9... | collective-permute-start | bytes 3932168 | tf_op jit(solution)/shard_map/ppermute | solution.py:102
  50.0 34.5 %collective-permute-start = (bf16[128,5120]{1,0:T(8,128)(2,1)}, bf16[128,5120]{1,0:T(8,128)(2,1)S(1)}, u32[]{:S(2)}, u32[]{:S(2)}) collective-permute-start(bf16[128,5120]{1,0:T(8,128)(2,1)} %constant_dynamic-update-slice_fusion.9), channel_id=1, source_target_pairs={{0,8},{8,16},{16,24},{24,28},{28,20},{20,12},{12,4},{4,0},{1,9},{9... | collective-permute-start | bytes 3932168 | tf_op jit(solution)/shard_map/ppermute | solution.py:102
  84.5 32.5 %collective-permute-start.2 = (bf16[128,5120]{1,0:T(8,128)(2,1)S(1)}, bf16[128,5120]{1,0:T(8,128)(2,1)}, u32[]{:S(2)}, u32[]{:S(2)}) collective-permute-start(bf16[128,5120]{1,0:T(8,128)(2,1)S(1)} %collective-permute-done), channel_id=1, source_target_pairs={{0,8},{8,16},{16,24},{24,28},{28,20},{20,12},{12,4},{4,0},{1,9},{9... | collective-permute-start | bytes 3932168 | tf_op jit(solution)/shard_map/ppermute | solution.py:102
  89.5 30.1 %collective-permute-start.3 = (bf16[128,5120]{1,0:T(8,128)(2,1)}, bf16[128,5120]{1,0:T(8,128)(2,1)}, u32[]{:S(2)}, u32[]{:S(2)}) collective-permute-start(bf16[128,5120]{1,0:T(8,128)(2,1)} %collective-permute-done.1), channel_id=1, source_target_pairs={{0,4},{8,0},{16,8},{24,16},{28,24},{20,28},{12,20},{4,12},{1,5},{9... | collective-permute-start | bytes 3932168 | tf_op jit(solution)/shard_map/ppermute | solution.py:102
  105.7 114.8 %collective-permute-start.8 = (bf16[512,768]{1,0:T(8,128)(2,1)}, bf16[512,768]{1,0:T(8,128)(2,1)}, u32[]{:S(2)}, u32[]{:S(2)}) collective-permute-start(bf16[512,768]{1,0:T(8,128)(2,1)} %bitcast.14), channel_id=1, source_target_pairs={{0,1},{1,0},{2,3},{3,2},{4,5},{5,4},{6,7},{7,6},{8,9},{9,8},{10,11... | collective-permute-start | bytes 2359304 | tf_op jit(solution)/shard_map/ppermute | solution.py:91
  105.7 68.2 %collective-permute-start.7 = (bf16[512,768]{1,0:T(8,128)(2,1)}, bf16[512,768]{1,0:T(8,128)(2,1)}, u32[]{:S(2)}, u32[]{:S(2)}) collective-permute-start(bf16[512,768]{1,0:T(8,128)(2,1)} %bitcast.14), channel_id=1, source_target_pairs={{0,2},{1,3},{2,0},{3,1},{4,6},{5,7},{6,4},{7,5},{8,10},{9,11},{10,... | collective-permute-start | bytes 2359304 | tf_op jit(solution)/shard_map/ppermute | solution.py:91
  117.0 30.0 %collective-permute-start.4 = (bf16[128,5120]{1,0:T(8,128)(2,1)}, bf16[128,5120]{1,0:T(8,128)(2,1)S(1)}, u32[]{:S(2)}, u32[]{:S(2)}) collective-permute-start(bf16[128,5120]{1,0:T(8,128)(2,1)} %collective-permute-done.2), channel_id=1, source_target_pairs={{0,8},{8,16},{16,24},{24,28},{28,20},{20,12},{12,4},{4,0},{1,9},{9... | collective-permute-start | bytes 3932168 | tf_op jit(solution)/shard_map/ppermute | solution.py:102
  119.6 29.4 %collective-permute-start.5 = (bf16[128,5120]{1,0:T(8,128)(2,1)}, bf16[128,5120]{1,0:T(8,128)(2,1)S(1)}, u32[]{:S(2)}, u32[]{:S(2)}) collective-permute-start(bf16[128,5120]{1,0:T(8,128)(2,1)} %collective-permute-done.3), channel_id=1, source_target_pairs={{0,4},{8,0},{16,8},{24,16},{28,24},{20,28},{12,20},{4,12},{1,5},{9... | collective-permute-start | bytes 3932168 | tf_op jit(solution)/shard_map/ppermute | solution.py:102
  165.2 51.0 %all-to-all-start.2 = ((bf16[8,64,2048]{2,1,0:T(8,128)(2,1)}), bf16[8,64,2048]{2,1,0:T(8,128)(2,1)}, u32[]{:S(2)}, u32[]{:S(2)}) async-start(bf16[8,64,2048]{2,1,0:T(8,128)(2,1)} %shard_map.810), calls=%async_computation.2 | async-start | bytes 4194304 | tf_op jit(solution)/shard_map/all_to_all | solution.py:344
  173.9 46.6 %collective-permute-start.9 = (bf16[512,768]{1,0:T(8,128)(2,1)}, bf16[512,768]{1,0:T(8,128)(2,1)}, u32[]{:S(2)}, u32[]{:S(2)}) collective-permute-start(bf16[512,768]{1,0:T(8,128)(2,1)} %collective-permute-done.7), channel_id=1, source_target_pairs={{0,1},{1,0},{2,3},{3,2},{4,5},{5,4},{6,7},{7,6},{8,9},{9,8},{10,11... | collective-permute-start | bytes 2359304 | tf_op jit(solution)/shard_map/ppermute | solution.py:91
  180.6 78.0 %collective-permute-start.19 = (bf16[2048,512]{1,0:T(8,128)(2,1)}, bf16[2048,512]{1,0:T(8,128)(2,1)}, u32[]{:S(2)}, u32[]{:S(2)}) collective-permute-start(bf16[2048,512]{1,0:T(8,128)(2,1)} %maximum_dynamic-update-slice_fusion.8), channel_id=1, source_target_pairs={{0,2},{1,3},{2,0},{3,1},{4,6},{5,7},{6,4},{7,5},{8,10},{9,11},{10,... | collective-permute-start | bytes 6291464 | tf_op jit(solution)/shard_map/ppermute | solution.py:91
  216.3 40.8 %all-to-all-start.3 = ((bf16[8,64,1024]{2,1,0:T(8,128)(2,1)}), bf16[8,64,1024]{2,1,0:T(8,128)(2,1)}, u32[]{:S(2)}, u32[]{:S(2)}) async-start(bf16[8,64,1024]{2,1,0:T(8,128)(2,1)} %shard_map.811), calls=%async_computation.3 | async-start | bytes 2097152 | tf_op jit(solution)/shard_map/all_to_all | solution.py:344
  241.2 59.7 %collective-permute-start.20 = (bf16[2048,512]{1,0:T(8,128)(2,1)}, bf16[2048,512]{1,0:T(8,128)(2,1)}, u32[]{:S(2)}, u32[]{:S(2)}) collective-permute-start(bf16[2048,512]{1,0:T(8,128)(2,1)} %maximum_dynamic-update-slice_fusion.8), channel_id=1, source_target_pairs={{0,1},{1,0},{2,3},{3,2},{4,5},{5,4},{6,7},{7,6},{8,9},{9,8},{10,11... | collective-permute-start | bytes 6291464 | tf_op jit(solution)/shard_map/ppermute | solution.py:91
  241.2 60.3 %collective-permute-start.22 = (bf16[512,2048]{1,0:T(8,128)(2,1)}, bf16[512,2048]{1,0:T(8,128)(2,1)}, u32[]{:S(2)}, u32[]{:S(2)}) collective-permute-start(bf16[512,2048]{1,0:T(8,128)(2,1)} %bitcast.26), channel_id=1, source_target_pairs={{0,2},{1,3},{2,0},{3,1},{4,6},{5,7},{6,4},{7,5},{8,10},{9,11},{10,... | collective-permute-start | bytes 6291464 | tf_op jit(solution)/shard_map/ppermute | solution.py:91
  258.6 53.4 %collective-permute-start.21 = (bf16[2048,512]{1,0:T(8,128)(2,1)}, bf16[2048,512]{1,0:T(8,128)(2,1)}, u32[]{:S(2)}, u32[]{:S(2)}) collective-permute-start(bf16[2048,512]{1,0:T(8,128)(2,1)} %collective-permute-done.19), channel_id=1, source_target_pairs={{0,1},{1,0},{2,3},{3,2},{4,5},{5,4},{6,7},{7,6},{8,9},{9,8},{10,11... | collective-permute-start | bytes 6291464 | tf_op jit(solution)/shard_map/ppermute | solution.py:91
  282.5 29.5 %collective-permute-start.25 = (bf16[512,1024]{1,0:T(8,128)(2,1)}, bf16[512,1024]{1,0:T(8,128)(2,1)}, u32[]{:S(2)}, u32[]{:S(2)}) collective-permute-start(bf16[512,1024]{1,0:T(8,128)(2,1)} %bitcast.29), channel_id=1, source_target_pairs={{0,2},{1,3},{2,0},{3,1},{4,6},{5,7},{6,4},{7,5},{8,10},{9,11},{10,... | collective-permute-start | bytes 3145736 | tf_op jit(solution)/shard_map/ppermute | solution.py:91
  300.7 30.1 %collective-permute-start.23 = (bf16[512,2048]{1,0:T(8,128)(2,1)}, bf16[512,2048]{1,0:T(8,128)(2,1)}, u32[]{:S(2)}, u32[]{:S(2)}) collective-permute-start(bf16[512,2048]{1,0:T(8,128)(2,1)} %bitcast.26), channel_id=1, source_target_pairs={{0,1},{1,0},{2,3},{3,2},{4,5},{5,4},{6,7},{7,6},{8,9},{9,8},{10,11... | collective-permute-start | bytes 6291464 | tf_op jit(solution)/shard_map/ppermute | solution.py:91
  300.8 42.4 %collective-permute-start.26 = (bf16[512,1024]{1,0:T(8,128)(2,1)}, bf16[512,1024]{1,0:T(8,128)(2,1)}, u32[]{:S(2)}, u32[]{:S(2)}) collective-permute-start(bf16[512,1024]{1,0:T(8,128)(2,1)} %bitcast.29), channel_id=1, source_target_pairs={{0,1},{1,0},{2,3},{3,2},{4,5},{5,4},{6,7},{7,6},{8,9},{9,8},{10,11... | collective-permute-start | bytes 3145736 | tf_op jit(solution)/shard_map/ppermute | solution.py:91
  301.4 29.4 %collective-permute-start.24 = (bf16[512,2048]{1,0:T(8,128)(2,1)}, bf16[512,2048]{1,0:T(8,128)(2,1)}, u32[]{:S(2)}, u32[]{:S(2)}) collective-permute-start(bf16[512,2048]{1,0:T(8,128)(2,1)} %collective-permute-done.22), channel_id=1, source_target_pairs={{0,1},{1,0},{2,3},{3,2},{4,5},{5,4},{6,7},{7,6},{8,9},{9,8},{10,11... | collective-permute-start | bytes 6291464 | tf_op jit(solution)/shard_map/ppermute | solution.py:91
  312.0 31.3 %collective-permute-start.27 = (bf16[512,1024]{1,0:T(8,128)(2,1)}, bf16[512,1024]{1,0:T(8,128)(2,1)}, u32[]{:S(2)}, u32[]{:S(2)}) collective-permute-start(bf16[512,1024]{1,0:T(8,128)(2,1)} %collective-permute-done.25), channel_id=1, source_target_pairs={{0,1},{1,0},{2,3},{3,2},{4,5},{5,4},{6,7},{7,6},{8,9},{9,8},{10,11... | collective-permute-start | bytes 3145736 | tf_op jit(solution)/shard_map/ppermute | solution.py:91
  387.0 48.4 %collective-permute-start.35 = (bf16[1024,2048]{1,0:T(8,128)(2,1)S(1)}, bf16[1024,2048]{1,0:T(8,128)(2,1)S(1)}, u32[]{:S(2)}, u32[]{:S(2)}) collective-permute-start(bf16[1024,2048]{1,0:T(8,128)(2,1)S(1)} %convolution_convert_fusion.1), channel_id=1, source_target_pairs={{0,1},{1,0},{2,3},{3,2},{4,5},{5,4},{6,7},{7,6},{8,9},{9,8},{10,11... | collective-permute-start | bytes 12582920 | tf_op jit(solution)/shard_map/ppermute | solution.py:91
  394.1 30.5 %collective-permute-start.34 = (bf16[1024,1024]{1,0:T(8,128)(2,1)S(1)}, bf16[1024,1024]{1,0:T(8,128)(2,1)S(1)}, u32[]{:S(2)}, u32[]{:S(2)}) collective-permute-start(bf16[1024,1024]{1,0:T(8,128)(2,1)S(1)} %fusion.15), channel_id=1, source_target_pairs={{0,1},{1,0},{2,3},{3,2},{4,5},{5,4},{6,7},{7,6},{8,9},{9,8},{10,11... | collective-permute-start | bytes 6291464 | tf_op jit(solution)/shard_map/ppermute | solution.py:91
  508.6 25.7 %all-to-all-start.4 = ((bf16[8,128,512]{1,2,0:T(8,128)(2,1)}), bf16[8,128,512]{1,2,0:T(8,128)(2,1)}, u32[]{:S(2)}, u32[]{:S(2)}) async-start(bf16[8,128,512]{1,2,0:T(8,128)(2,1)} %maximum_bitcast_fusion), calls=%async_computation.4 | async-start | bytes 2097152 | tf_op jit(solution)/shard_map/all_to_all | solution.py:751
  512.9 63.0 %collective-permute-start.52 = (bf16[512,2048]{1,0:T(8,128)(2,1)}, bf16[512,2048]{1,0:T(8,128)(2,1)}, u32[]{:S(2)}, u32[]{:S(2)}) collective-permute-start(bf16[512,2048]{1,0:T(8,128)(2,1)} %fusion.5), channel_id=1, source_target_pairs={{0,2},{1,3},{2,0},{3,1},{4,6},{5,7},{6,4},{7,5},{8,10},{9,11},{10,... | collective-permute-start | bytes 6291464 | tf_op jit(solution)/shard_map/ppermute | solution.py:91
  537.7 28.2 %all-to-all-start.5 = ((bf16[8,64,1024]{2,1,0:T(8,128)(2,1)}), bf16[8,64,1024]{2,1,0:T(8,128)(2,1)}, u32[]{:S(2)}, u32[]{:S(2)}) async-start(bf16[8,64,1024]{2,1,0:T(8,128)(2,1)} %bitcast.116), calls=%async_computation.5 | async-start | bytes 2097152 | tf_op jit(solution)/shard_map/all_to_all | solution.py:351
  586.4 86.3 %all-to-all-start.6 = ((bf16[8,64,2048]{2,1,0:T(8,128)(2,1)}), bf16[8,64,2048]{2,1,0:T(8,128)(2,1)}, u32[]{:S(2)}, u32[]{:S(2)}) async-start(bf16[8,64,2048]{2,1,0:T(8,128)(2,1)} %bitcast.50), calls=%async_computation.6 | async-start | bytes 4194304 | tf_op jit(solution)/shard_map/all_to_all | solution.py:351
  601.0 31.0 %collective-permute-start.45 = (bf16[128,1024]{1,0:T(8,128)(2,1)S(1)}, bf16[128,1024]{1,0:T(8,128)(2,1)S(1)}, u32[]{:S(2)}, u32[]{:S(2)}) collective-permute-start(bf16[128,1024]{1,0:T(8,128)(2,1)S(1)} %get-tuple-element.223), channel_id=1, source_target_pairs={{0,8},{8,16},{16,24},{24,28},{28,20},{20,12},{12,4},{4,0},{1,9},{9... | collective-permute-start | bytes 786440 | tf_op jit(solution)/shard_map/ppermute | solution.py:102
  602.3 55.6 %collective-permute-start.63 = (bf16[1,512,256]{2,1,0:T(8,128)(2,1)S(1)}, bf16[1,512,256]{2,1,0:T(8,128)(2,1)S(1)}, u32[]{:S(2)}, u32[]{:S(2)}) collective-permute-start(bf16[1,512,256]{2,1,0:T(8,128)(2,1)S(1)} %slice_bitcast_fusion.2), channel_id=1, source_target_pairs={{0,2},{1,3},{2,0},{3,1},{4,6},{5,7},{6,4},{7,5},{8,10},{9,11},{10,... | collective-permute-start | bytes 786440 | tf_op jit(solution)/shard_map/ppermute | solution.py:91
  608.9 68.0 %collective-permute-start.57 = (bf16[512,768]{1,0:T(8,128)(2,1)}, bf16[512,768]{1,0:T(8,128)(2,1)}, u32[]{:S(2)}, u32[]{:S(2)}) collective-permute-start(bf16[512,768]{1,0:T(8,128)(2,1)} %fusion.23), channel_id=1, source_target_pairs={{0,2},{1,3},{2,0},{3,1},{4,6},{5,7},{6,4},{7,5},{8,10},{9,11},{10,... | collective-permute-start | bytes 2359304 | tf_op jit(solution)/shard_map/ppermute | solution.py:91
  681.0 37.2 %all-to-all-start.7 = ((bf16[8,64,1024]{2,1,0:T(8,128)(2,1)}), bf16[8,64,1024]{2,1,0:T(8,128)(2,1)S(1)}, u32[]{:S(2)}, u32[]{:S(2)}) async-start(bf16[8,64,1024]{2,1,0:T(8,128)(2,1)} %pad_maximum_fusion.11), calls=%async_computation.7 | async-start | bytes 2097152 | tf_op jit(solution)/shard_map/all_to_all | solution.py:351
  (100 other events, 1634.0 us)

commit v2 on v1

--- a/solution.py
+++ b/solution.py
@@ -109,6 +109,10 @@
     return table[lax.axis_index("seq")]
 
 
+def filled(arrays, filler):
+    return filler(arrays) if callable(filler) else after_all(arrays, filler)
+
+
 def ring_gather(parts, fillers=()):
     count = lax.axis_size("seq")
     far = count // 2
@@ -118,11 +122,11 @@
     ahead = behind = packed
     for step in range(1, far):
         if 0 <= step - 2 < len(fillers):
-            ahead, behind = after_all((ahead, behind), fillers[step - 2])
+            ahead, behind = filled((ahead, behind), fillers[step - 2])
         ahead, behind = ring_shift(ahead, 1), ring_shift(behind, -1)
         blocks[-step], blocks[step] = ahead, behind
     if far - 2 < len(fillers):
-        ahead, behind = after_all((ahead, behind), fillers[far - 2])
+        ahead, behind = filled((ahead, behind), fillers[far - 2])
     left, right = ring_shift(ahead[:, :middle], 1), ring_shift(behind[:, middle:], -1)
     blocks[far] = jnp.concatenate([left, right], axis=1)
     gathered = []
@@ -170,7 +174,7 @@
 def ring_scatter_sum(parts, fillers=()):
     far = lax.axis_size("seq") // 2
     first, second = parts
-    ahead, behind = (ring_shift(first[far], 1),), (ring_shift(second[far], -1),)
+    ahead, behind = [ring_shift(first[far], 1)], [ring_shift(second[far], -1)]
     for turn, step in enumerate(range(far - 1, 0, -1)):
         onward = [first[step], second[step]]
         backward = [first[-step], second[-step]]
@@ -181,10 +185,19 @@
             onward = [added(block, got) for block, got in zip(onward, ahead)]
             backward = [added(block, got) for block, got in zip(backward, behind)]
         if turn < len(fillers):
-            moved = after_all(onward + backward, fillers[turn])
+            needed = fillers[turn]
+            if callable(needed):
+                needed = needed(ahead + behind)
+            moved = after_all(onward + backward, needed)
             onward, backward = moved[:2], moved[2:]
         ahead = [ring_shift(block, 1) for block in onward]
         behind = [ring_shift(block, -1) for block in backward]
+    if far - 1 < len(fillers):
+        needed = fillers[far - 1]
+        if callable(needed):
+            needed = needed(ahead + behind)
+        moved = after_all(ahead + behind, needed)
+        ahead, behind = moved[:2], moved[2:]
     return [
         own.astype(jnp.float32) + left.astype(jnp.float32) + right.astype(jnp.float32)
         for own, left, right in zip((first[0], second[0]), ahead, behind)
@@ -493,6 +506,157 @@
     everything = slice(0, length)
     out_ref[:, lanes(1)] = undone(key_grad[...], everything)
     out_ref[:, lanes(2)] = value_grad[...].astype(jnp.bfloat16)
+
+
+def project_kernel(total, attended_ref, inputs_ref, gain_ref, *refs):
+    weight_refs, (middle_ref, unit_ref) = refs[:total], refs[total:]
+    width = inputs_ref.shape[1]
+    part = width // total
+    attended = attended_ref[...]
+    squares = 0.0
+    for place, weight_ref in enumerate(weight_refs):
+        columns = slice(place * part, (place + 1) * part)
+        block = inputs_ref[:, columns].astype(jnp.float32) + matmul(attended, weight_ref[...])
+        middle_ref[:, columns] = block
+        squares += jnp.sum(block * block, axis=1, keepdims=True)
+    scale = lax.rsqrt(squares / width + norm_eps)
+    unit_ref[...] = (middle_ref[...] * scale * gain_ref[...]).astype(jnp.bfloat16)
+
+
+def project_rows(attended, inputs, gain, pieces):
+    length, width = inputs.shape
+    total = len(pieces)
+    rows = pl.BlockSpec((QUERY_ROWS, width), lambda i: (i, 0))
+    return pl.pallas_call(
+        lambda *refs: project_kernel(total, *refs),
+        grid=(length // QUERY_ROWS,),
+        in_specs=[rows, rows, pl.BlockSpec((1, width), lambda i: (0, 0))]
+        + [pl.BlockSpec((width, width // total), lambda i: (0, 0))] * total,
+        out_specs=[rows, rows],
+        out_shape=[
+            jax.ShapeDtypeStruct((length, width), jnp.float32),
+            jax.ShapeDtypeStruct((length, width), jnp.bfloat16),
+        ],
+        compiler_params=pltpu.CompilerParams(vmem_limit_bytes=48 << 20),
+        cost_estimate=pl.CostEstimate(
+            flops=2 * length * width * width,
+            bytes_accessed=10 * length * width + 2 * width * width,
+            transcendentals=length,
+        ),
+    )(attended, inputs, gain, *pieces)
+
+
+def summed_product(left_ref, weight_refs):
+    part = left_ref.shape[1] // len(weight_refs)
+    return sum(
+        matmul(left_ref[:, place * part : (place + 1) * part], weight_ref[...])
+        for place, weight_ref in enumerate(weight_refs)
+    )
+
+
+def hidden_kernel(total, rows_ref, *refs):
+    gate_ref, up_ref, low_ref = refs[2 * total :]
+    gate = summed_product(rows_ref, refs[:total])
+    up = summed_product(rows_ref, refs[total : 2 * total])
+    gate_ref[...] = gate
+    up_ref[...] = up
+    low_ref[...] = (gate * jax.nn.sigmoid(gate) * up).astype(jnp.bfloat16)
+
+
+def hidden_units(rows, gate_pieces):
+    length, width = rows.shape
+    total = len(gate_pieces)
+    hidden = gate_pieces[0].shape[1] // 2
+    tile = min(hidden, 2 * LANES)
+    steps = hidden // tile
+    own = pl.BlockSpec((length, tile), lambda j: (0, j))
+    wide = jax.ShapeDtypeStruct((length, hidden), jnp.float32)
+    return pl.pallas_call(
+        lambda *refs: hidden_kernel(total, *refs),
+        grid=(steps,),
+        in_specs=[pl.BlockSpec((length, width), lambda j: (0, 0))]
+        + [pl.BlockSpec((width // total, tile), lambda j: (0, j))] * total
+        + [pl.BlockSpec((width // total, tile), lambda j: (0, steps + j))] * total,
+        out_specs=[own] * 3,
+        out_shape=[wide, wide, jax.ShapeDtypeStruct((length, hidden), jnp.bfloat16)],
+        compiler_params=pltpu.CompilerParams(vmem_limit_bytes=48 << 20),
+        cost_estimate=pl.CostEstimate(
+            flops=4 * length * width * hidden,
+            bytes_accessed=2 * length * width + 4 * width * hidden + 10 * length * hidden,
+            transcendentals=length * hidden,
+        ),
+    )(rows, *gate_pieces, *gate_pieces)
+
+
+def hidden_back_kernel(total, grads_ref, gate_ref, up_ref, *refs):
+    grad_ref = refs[total]
+    tile = gate_ref.shape[1]
+    hidden = grad_ref.shape[1] // 2
+    grad = summed_product(grads_ref, refs[:total])
+    gate, up = gate_ref[...], up_ref[...]
+    sigmoid = jax.nn.sigmoid(gate)
+    first = pl.multiple_of(pl.program_id(0) * tile, tile)
+    grad_gate = grad * up * (sigmoid * (1.0 + gate * (1.0 - sigmoid)))
+    grad_ref[:, pl.ds(first, tile)] = grad_gate.astype(jnp.bfloat16)
+    second = pl.multiple_of(hidden + pl.program_id(0) * tile, tile)
+    grad_ref[:, pl.ds(second, tile)] = (grad * (gate * sigmoid)).astype(jnp.bfloat16)
+
+
+def hidden_back(grads, gate, up, down_pieces):
+    length, width = grads.shape
+    total = len(down_pieces)
+    hidden = gate.shape[1]
+    tile = min(hidden, 2 * LANES)
+    own = pl.BlockSpec((length, tile), lambda j: (0, j))
+    return pl.pallas_call(
+        lambda *refs: hidden_back_kernel(total, *refs),
+        grid=(hidden // tile,),
+        in_specs=[pl.BlockSpec((length, width), lambda j: (0, 0)), own, own]
+        + [pl.BlockSpec((width // total, tile), lambda j: (0, j))] * total,
+        out_specs=pl.BlockSpec((length, 2 * hidden), lambda j: (0, 0)),
+        out_shape=jax.ShapeDtypeStruct((length, 2 * hidden), jnp.bfloat16),
+        compiler_params=pltpu.CompilerParams(vmem_limit_bytes=48 << 20),
+        cost_estimate=pl.CostEstimate(
+            flops=2 * length * width * hidden,
+            bytes_accessed=2 * length * width + 2 * width * hidden + 12 * length * hidden,
+            transcendentals=length * hidden,
+        ),
+    )(grads, gate, up, *down_pieces)
+
+
+def back_kernel(total, left_ref, *refs):
+    each = pl.num_programs(0) // total
+    for place in range(total):
+
+        @pl.when(pl.program_id(0) // each == place)
+        def _():
+            refs[total][...] = mm_last(left_ref[...], refs[place][...]).astype(jnp.bfloat16)
+
+
+def back_to_model(left, pieces):
+    length, inner = left.shape
+    total = len(pieces)
+    part = pieces[0].shape[0]
+    tile = min(part, 2 * LANES)
+    each = part // tile
+
+    def rows_of(place):
+        return pl.BlockSpec((tile, inner), lambda i: (jnp.clip(i - place * each, 0, each - 1), 0))
+
+    return pl.pallas_call(
+        lambda *refs: back_kernel(total, *refs),
+        grid=(total * each,),
+        in_specs=[pl.BlockSpec((length, inner), lambda i: (0, 0))]
+        + [rows_of(place) for place in range(total)],
+        out_specs=pl.BlockSpec((length, tile), lambda i: (0, i)),
+        out_shape=jax.ShapeDtypeStruct((length, part * total), jnp.bfloat16),
+        compiler_params=pltpu.CompilerParams(vmem_limit_bytes=48 << 20),
+        cost_estimate=pl.CostEstimate(
+            flops=2 * length * part * total * inner,
+            bytes_accessed=2 * inner * (length + part * total) + 2 * length * part * total,
+            transcendentals=0,
+        ),
+    )(left, *pieces)
 
 
 def attend_forward(qkv, cos_table, sin_table, starts):
@@ -668,68 +832,96 @@
     gains_here = to_relative(gains, rows_own)
     tokens_here = to_relative(tokens[0], rows_own)
     grads_here = to_relative(out_grad[0], rows_own)
-    out_here = jnp.stack(batch_columns(out_weight.astype(jnp.bfloat16), rows_own))
-    out_here = lax.all_to_all(out_here, "batch", 0, 0, tiled=True).reshape(head_width, -1)
-    out_here = with_rows(out_here, local_rows)
     qkv_low = rounded_by_owner(qkv_weight, 3)
+    out_columns = batch_columns(after(out_weight, qkv_low).astype(jnp.bfloat16), rows_own)
+    out_here = [
+        swapped(of_offset(out_columns, m), "batch", m) if m else of_offset(out_columns, m)
+        for m in range(batch_total)
+    ]
+    out_here = [of_offset(out_here, b) for b in range(batch_total)]
+    out_here = with_rows(jnp.concatenate(out_here, axis=0), local_rows)
     gate_low = rounded_by_owner(gate_up_weight, 2)
     down_low = rounded_by_owner(down_weight, 1)
     qkv_block = to_column_owners(qkv_low)
-    tokens_all, grads_all, out_all = ring_gather(
-        after_all([tokens_here, grads_here, out_here], (qkv_low, gate_low, down_low)),
-        ((qkv_block,),),
-    )
-    tokens_all, grads_all = stacked_rows(tokens_all), stacked_rows(grads_all)
+    tokens_all, out_all = ring_gather(
+        [after(tokens_here, qkv_low), out_here], ((qkv_block,), (gate_low, down_low))
+    )
+    tokens_all = stacked_rows(tokens_all)
     out_all = stacked_rows(
         {offset: with_rows(block, head_width) for offset, block in out_all.items()}
     )
     qkv_full = gather_batch(qkv_block)
     gate_block = to_column_owners(after(gate_low, tokens_all))
-    down_block = to_column_owners(after(down_low, gate_block))
-
     inputs = tokens_all.astype(jnp.float32)
     act_one = (unit_rows(inputs)[0] * gains_here[0]).astype(jnp.bfloat16)
     qkv = matmul(act_one, qkv_full)
     attn_own, attn_kept = attention(qkv)
 
-    out_full = jnp.concatenate(gather_pieces(out_all), axis=1)
-
+    out_pieces = gather_pieces(out_all)
+    out_full = jnp.concatenate(out_pieces, axis=1)
+
+    gate_block = after(gate_block, attn_own)
+    down_block = to_column_owners(after(down_low, gate_block))
     attn_own_late = after(attn_own, gate_block)
     attn_all = stacked_columns(ring_gather([attn_own_late], ((down_block,),))[0])
-    gate_full = gather_batch(gate_block)
-    down_full = gather_batch(down_block)
-    middle_all = inputs + matmul(attn_all, out_full)
-    act_two = (unit_rows(middle_all)[0] * gains_here[1]).astype(jnp.bfloat16)
-
-    def feed_forward(rows, grads):
-        gate_up = matmul(rows, gate_full)
-        gate_part = gate_up[:, :hidden]
-        up_part = gate_up[:, hidden:]
+    gate_pieces, down_pieces = gather_pieces(gate_block), gather_pieces(down_block)
+    grads_here_late = after(grads_here, attn_all)
+    if in_pairs and length * model_width <= 1 << 21:
+        middle_all, act_two = project_rows(attn_all, tokens_all, gains_here[1:], out_pieces)
+        gate_part, up_part, hidden_low = hidden_units(act_two, gate_pieces)
+        late = {}
+
+        def block_meanwhile(moved):
+            *moved, low = lax.optimization_barrier((*moved, hidden_low))
+            late["block"] = back_to_model(low, down_pieces)
+            return moved
+
+        grads_all = ring_gather(
+            [grads_here_late],
+            ((act_two,), block_meanwhile, lambda moved: after_all(moved, (late["block"],))),
+        )
+        grads_all, block_part = stacked_rows(grads_all[0]), late["block"]
+        grad_gate_up = hidden_back(grads_all, gate_part, up_part, down_pieces)
+        grad_two = back_to_model(grad_gate_up, gate_pieces)
+    else:
+        grads_all = stacked_rows(ring_gather([grads_here_late])[0])
+        middle_all = inputs + matmul(attn_all, out_full)
+        act_two = (unit_rows(middle_all)[0] * gains_here[1]).astype(jnp.bfloat16)
+        gate_full, down_full = jnp.concatenate(gate_pieces), jnp.concatenate(down_pieces)
+        gate_up = matmul(act_two, gate_full)
+        gate_part, up_part = gate_up[:, :hidden], gate_up[:, hidden:]
         sigmoid_gate = jax.nn.sigmoid(gate_part)
         silu_gate = gate_part * sigmoid_gate
         hidden_low = (silu_gate * up_part).astype(jnp.bfloat16)
-        grad_hidden = matmul(grads, down_full)
+        grad_hidden = matmul(grads_all, down_full)
         grad_gate = (
             grad_hidden * up_part * (sigmoid_gate * (1.0 + gate_part * (1.0 - sigmoid_gate)))
         )
-        grad_up = grad_hidden * silu_gate
-        grad_gate_up = jnp.concatenate([grad_gate, grad_up], axis=1).astype(jnp.bfloat16)
+        grad_gate_up = jnp.concatenate([grad_gate, grad_hidden * silu_gate], axis=1)
+        grad_gate_up = grad_gate_up.astype(jnp.bfloat16)
         grad_two = contract_cols(grad_gate_up, gate_full).astype(jnp.bfloat16)
         block_part = contract_cols(hidden_low, down_full).astype(jnp.bfloat16)
-        return (grad_gate_up, hidden_low, grad_two, block_part)
 
     offsets = [far] + [sign * step for step in range(far - 1, 0, -1) for sign in (1, -1)] + [0]
-    grad_gate_up, hidden_low, grad_two, block_part = feed_forward(act_two, grads_all)
-    hidden_late, gate_up_late = after_all((hidden_low, grad_gate_up), (grad_two, block_part))
-    down_own, down_sends = partial_sum_batch(grads_all, hidden_late)
-    gate_own, gate_sends = partial_sum_batch(act_two, gate_up_late)
+    sums = {}
+
+    def weight_sums(arrived):
+        late = after_all((hidden_low, grad_gate_up), arrived)
+        sums["down"] = partial_sum_batch(grads_all, late[0])
+        sums["gate"] = partial_sum_batch(act_two, late[1])
+        return ()
+
+    def sent(stage):
+        return lambda arrived: (sums["down"][1][stage], sums["gate"][1][stage])
+
     grad_two, block_rest = ring_scatter_sum(
         [
             {offset: ring_rows(whole, [offset]) for offset in offsets}
             for whole in (grad_two, block_part)
         ],
-        ((down_sends[0], gate_sends[0]), (down_sends[-1], gate_sends[-1]), (down_own,)),
-    )
+        (weight_sums, lambda arrived: (*sent(0)(arrived), *sent(-1)(arrived))),
+    )
+    down_own, gate_own = sums["down"][0], sums["gate"][0]
 
     def own_rows(whole):
         return lax.dynamic_slice_in_dim(whole, first_row, local_rows, 0)
@@ -748,12 +940,13 @@
         ],
         axis=2,
     )
-    got = lax.all_to_all(jnp.transpose(by_owner, (1, 0, 2)), "seq", 0, 0, tiled=True)
+    down_grad = to_row_owners(down_own)
+    by_owner = after(jnp.transpose(by_owner, (1, 0, 2)), down_grad)
+    got = lax.all_to_all(by_owner, "seq", 0, 0, tiled=True)
     got = got.reshape(length, 2 * head_width)
     grad_heads = got[:, :head_width]
     grad_attn_own = got[:, head_width:]
-    down_grad = to_row_owners(after(down_own, got))
-    gate_grad = to_row_owners(after(gate_own, down_grad))
+    gate_grad = to_row_owners(after(gate_own, got))
 
     grad_qkv = attention_back(grad_heads, attn_kept)
     qkv_own, qkv_sends = partial_sum_batch(act_one, grad_qkv)
@@ -763,32 +956,37 @@
         out_part[:, b].reshape(seq_total * rows_own, head_width) for b in range(batch_total)
     ]
     out_own = scatter_sum_batch(jnp.stack([of_offset(out_part, m) for m in range(batch_total)]))
-    grad_qkv = after(grad_qkv, qkv_sends[0], out_own)
+    grad_qkv = after(grad_qkv, qkv_sends[0], out_own, gate_grad)
     grad_one_part = contract_cols(grad_qkv, qkv_full)
     gain_one_part = jnp.sum(grad_one_part * act_one.astype(jnp.float32), axis=0)
     gain_grad = jnp.stack([gain_one_part / gains_here[0], gain_two_grad])
-    gain_grad = sum_everywhere(from_relative(gain_grad, rows_own))
+    gain_grad = from_relative(gain_grad, rows_own)
     down_m, down_s, down_w = adam_by_owner(
         down_weight, down_first, down_second, down_grad, 1, rate_down
     )
+    gate_m, gate_s, gate_w = adam_by_owner(
+        gate_up_weight, gate_up_first, gate_up_second, gate_grad, 2, rate_gate
+    )
+
+    def last_transfer(arrived):
+        both = jnp.concatenate([after(qkv_own, gate_grad, *arrived), out_own], axis=1)
+        sums["rest"] = to_row_owners(both)
+        return (gate_m,)
+
     grad_one = ring_scatter_one(
-        grad_one_part.astype(jnp.bfloat16), ((qkv_sends[-1], down_m), (gate_grad,), (qkv_own,))
-    )
+        after(grad_one_part.astype(jnp.bfloat16), gate_grad),
+        ((qkv_sends[-1], down_m), last_transfer, (), lambda arrived: (sums["rest"],)),
+    )
+    qkv_grad = sums["rest"]
+    gain_grad = sum_everywhere(after(gain_grad, qkv_grad))
     unit_one, scale_one = unit_rows(tokens_here.astype(jnp.float32))
     grad_in_norm = norm_back(grad_one, unit_one, scale_one, gains_here[0])[0]
     input_grad = from_relative(grad_middle + grad_in_norm, rows_own)
-    qkv_grad = to_row_owners(
-        jnp.concatenate([after(qkv_own, gate_grad), out_own], axis=1)
-    )
-
     qkv_m, qkv_s, qkv_w = adam_by_owner(
         qkv_weight, qkv_first, qkv_second, qkv_grad, 3, rate_qkv
     )
     out_m, out_s, out_w = adam_by_owner(
         out_weight, out_first, out_second, qkv_grad, 1, rate_out, skipped=3
-    )
-    gate_m, gate_s, gate_w = adam_by_owner(
-        gate_up_weight, gate_up_first, gate_up_second, gate_grad, 2, rate_gate
     )
     gain_m, gain_s, gain_w = adam_update(gains, gain_first, gain_second, gain_grad, rate_gain)
     return (

time: 743 us -> 682 us (0.918)
  Pallas kernels: 69.5 us -> 135 us
  waiting for transfers between devices: 281 us -> 221 us
  matrix products: 122 us -> 63 us
  other arithmetic: 63.2 us -> 54 us
    pallas_call x0 -> x5, Pallas kernels: none -> 65.4 us  [the longest x2 24.1 us: back_to_model(): pl.pallas_call(lambda *refs: back_kernel(total, *refs), grid=(total * eac...]
    dot_general x4 -> x1, matrix products: 45.4 us -> 8.44 us  [matmul(): return jnp.dot(left_side, right_side, preferred_element_type=jnp.float32)]
    ppermute x44 -> x52, waiting for transfers between devices: 201 us -> 175 us  [ring_shift(): return lax.ppermute(value, 'seq', pairs)]
    dot_general x4 -> x2, matrix products: 37.5 us -> 12.5 us  [contract_cols(): lax.dot_general(left_side, right_side, (((1,), (1,)), ((), ())), preferre...]
    all_to_all x3, waiting for transfers between devices: 36.3 us -> 14.2 us  [to_column_owners(): got = lax.all_to_all(blocks, 'seq', 0, 0, tiled=True)]
    all_to_all x3, waiting for transfers between devices: 1.99 us -> 17.1 us  [to_row_owners(): return lax.all_to_all(blocks, 'seq', 0, 0, tiled=True)]
    ppermute x20 -> x23, waiting for transfers between devices: 17.4 us -> 5.61 us  [swapped(): lax.ppermute(value, axis, [(source, source ^ bit) for source in range(cou...]
    all_to_all x2 -> x1, waiting for transfers between devices: 19.9 us -> 8.69 us  [on_device(): got = lax.all_to_all(by_owner, 'seq', 0, 0, tiled=True)]
  transfers between devices with their start and end apart: 73 -> 83, of which waited for: 40 -> 42; matrix products, arithmetic and copies ran while one was open for 24% -> 24% of each run, Pallas kernels for 8% -> 19%
where the time goes in v2:
time: 682 us; the launch traced here: 672 us
  waiting for transfers between devices  221 us (32%)
  Pallas kernels  135 us (20%)
  starting transfers between devices  118 us (17%)
  local copies, waits for them, and re-layouts  70.2 us (10%)
  matrix products  63 us (9%)
  other arithmetic  54 us (8%)
  between operations  11.7 us (2%)
    ppermute x52, waiting for transfers between devices, ring_shift(): return lax.ppermute(value, 'seq', pairs)  175 us
    ppermute x52, starting transfers between devices, ring_shift(): return lax.ppermute(value, 'seq', pairs)  62.4 us
    dot_general x10, matrix products, contract_rows(): lax.dot_general(left_side, right_side, (((0,), (0,)), ((), ())), preferre...  42 us
    pallas_call x4, Pallas kernels, adam_by_owner(): pl.pallas_call(kernel, grid=(groups, steps), in_specs=[whole] * 3 + [pl.B...  32.5 us
    pallas_call x2, Pallas kernels, back_to_model(): pl.pallas_call(lambda *refs: back_kernel(total, *refs), grid=(total * eac...  24.1 us
    pallas_call x3, Pallas kernels, rounded_by_owner(): pl.pallas_call(kernel, grid=(groups, steps), in_specs=[pl.BlockSpec((rows...  19.6 us
    all_to_all x3, waiting for transfers between devices, to_row_owners(): return lax.all_to_all(blocks, 'seq', 0, 0, tiled=True)  17.1 us
    convert_element_type x9, other arithmetic, added(): (block.astype(jnp.float32) + got.astype(jnp.float32)).astype(block.dtype)  16.9 us
  transfers between devices with their start and end apart: 83, of which 42 were waited for; matrix products, arithmetic and copies ran while one was open for 24% of the time, Pallas kernels for 19%

profile of v2, /device:TPU:0, one launch (start us, length us, event | category | flops | bytes accessed | tf_op | source)
XLA Modules:
  0.0 672.5 jit_solution(12372970152494525846)
XLA Ops:
  5.2 7.3 %all-to-all-start = ((bf16[8,64,768]{2,1,0:T(8,128)(2,1)}), bf16[8,64,768]{2,1,0:T(8,128)(2,1)}, u32[]{:S(2)}, u32[]{:S(2)}) async-start(bf16[8,64,768]{2,1,0:T(8,128)(2,1)} %shard_map.809), calls=%async_computation | async-start | bytes 1572864 | tf_op jit(solution)/shard_map/all_to_all | solution.py:357
  43.0 9.8 %shard_map.810 = bf16[8,64,2048]{2,1,0:T(8,128)(2,1)} custom-call(f32[64,16384]{1,0:T(8,128)} %weight_ref.11), custom_call_target="tpu_custom_call" | custom-call | bytes 6291456 | tf_op jit(solution)/shard_map/pallas_call | solution.py:344
  60.2 12.1 %collective-permute-done.4 = bf16[128,3072]{1,0:T(8,128)(2,1)S(1)} collective-permute-done((bf16[128,3072]{1,0:T(8,128)(2,1)S(1)}, bf16[128,3072]{1,0:T(8,128)(2,1)S(1)}, u32[]{:S(2)}, u32[]{:S(2)}) %collective-permute-start.4) | collective-permute-done | bytes 786464 | tf_op jit(solution)/shard_map/ppermute | solution.py:102
  79.3 12.6 %collective-permute-done.5 = bf16[128,3072]{1,0:T(8,128)(2,1)S(1)} collective-permute-done((bf16[128,3072]{1,0:T(8,128)(2,1)}, bf16[128,3072]{1,0:T(8,128)(2,1)S(1)}, u32[]{:S(2)}, u32[]{:S(2)}) %collective-permute-start.5) | collective-permute-done | bytes 786464 | tf_op jit(solution)/shard_map/ppermute | solution.py:102
  97.4 13.2 %collective-permute-done.7 = bf16[128,3072]{1,0:T(8,128)(2,1)S(1)} collective-permute-done((bf16[128,3072]{1,0:T(8,128)(2,1)S(1)}, bf16[128,3072]{1,0:T(8,128)(2,1)S(1)}, u32[]{:S(2)}, u32[]{:S(2)}) %collective-permute-start.7) | collective-permute-done | bytes 786464 | tf_op jit(solution)/shard_map/ppermute | solution.py:102
  136.4 8.4 %fusion.55.query_in.key_in.value_in = f32[1024,768]{1,0:T(8,128)} fusion(bf16[1024,2048]{1,0:T(8,128)(2,1)S(1)} %fusion.2, bf16[512,768]{1,0:T(8,128)(2,1)S(1)} %collective-permute-done.13, bf16[512,768]{1,0:T(8,128)(2,1)} %collective-permute-done.12, bf16[512,768]{1,0:T(8,128)(2,1)} %collective-permute-done.11, bf16[512,768]{1,0:T(8,128)(2,1)} %bitcast.7), kind=kOutput, calls=%fused_computation.82 | convolution fusion | flops 3233808384 | bytes 10485760 | tf_op jit(solution)/shard_map/dot_general | solution.py:75
  144.8 8.7 %shard_map.812 = (f32[1024,256]{1,0:T(8,128)S(1)}, bf16[1024,256]{1,0:T(8,128)(2,1)S(1)}, bf16[1024,256]{1,0:T(8,128)(2,1)S(1)}, bf16[1024,256]{1,0:T(8,128)(2,1...) custom-call(f32[1024,768]{1,0:T(8,128)} %fusion.55.query_in.key_in.value_in, ...), custom_call_target="tpu_custom_call" | custom-call | flops 2147483648 | bytes 6291456 | tf_op jit(solution)/shard_map/pallas_call | solution.py:669
  156.1 14.2 %all-to-all-done.1 = bf16[8,64,2048]{2,1,0:T(8,128)(2,1)} async-done(((bf16[8,64,2048]{2,1,0:T(8,128)(2,1)}), bf16[8,64,2048]{2,1,0:T(8,128)(2,1)}, u32[]{:S(2)}, u32[]{:S(2)}) %all-to-all-start.1) | async-done | bytes 2097184 | tf_op jit(solution)/shard_map/all_to_all | solution.py:357
  177.5 27.0 %collective-permute-done.15 = bf16[1024,256]{1,0:T(8,128)(2,1)S(1)} collective-permute-done((bf16[1024,256]{1,0:T(8,128)(2,1)S(1)}, bf16[1024,256]{1,0:T(8,128)(2,1)S(1)}, u32[]{:S(2)}, u32[]{:S(2)}) %collective-permute-start.15) | collective-permute-done | bytes 524320 | tf_op jit(solution)/shard_map/ppermute | solution.py:102
  205.3 7.1 %collective-permute-start.16 = (bf16[1024,256]{1,0:T(8,128)(2,1)}, bf16[1024,256]{1,0:T(8,128)(2,1)}, u32[]{:S(2)}, u32[]{:S(2)}) collective-permute-start(bf16[1024,256]{1,0:T(8,128)(2,1)} %collective-permute-done.14), channel_id=1, source_target_pairs={{0,8},{8,16},{16,24},{24,28},{28,20},{20,12},{12,4},{4,0},{1,9},{9... | collective-permute-start | bytes 1572872 | tf_op jit(solution)/shard_map/ppermute | solution.py:102
  256.4 15.9 %shard_map.813 = (f32[1024,2048]{1,0:T(8,128)}, bf16[1024,2048]{1,0:T(8,128)(2,1)}) custom-call(bf16[1024,2048]{1,0:T(8,128)(2,1)} %maximum_dynamic-update-slice_fusion.refs_0_, bf16[1024,2048]{1,0:T(8,128)(2,1)} %fusion.58.refs_1_, f32[1,2048]{1,0:T(1,128)S(1)} %get-tuple-element.331.refs_2_, bf16[2048,512]{1,0:T(8,128)(2,1)} %maximum_dynamic-update-slice_fusion.9.refs_3_, ...), custom_call_target="tpu_custom_call" | custom-call | flops 8589934592 | bytes 29360128 | tf_op jit(solution)/shard_map/pallas_call | solution.py:530
  278.2 14.3 %shard_map.814 = (f32[1024,1024]{1,0:T(8,128)}, f32[1024,1024]{1,0:T(8,128)}, bf16[1024,1024]{1,0:T(8,128)(2,1)S(1)}) custom-call(bf16[1024,2048]{1,0:T(8,128)(2,1)} %get-tuple-element.107.refs_0_, bf16[512,2048]{1,0:T(8,128)(2,1)} %bitcast.19.refs_1_.refs_5_, bf16[512,2048]{1,0:T(8,128)(2,1)} %collective-permute-done.29.refs_2_.refs_6_, ...), custom_call_target="tpu_custom_call" | custom-call | flops 8589934592 | bytes 23068672 | tf_op jit(solution)/shard_map/pallas_call | solution.py:574
  295.9 8.7 %shard_map.815 = bf16[1024,2048]{1,0:T(8,128)(2,1)} custom-call(bf16[1024,1024]{1,0:T(8,128)(2,1)} %copy-done.8, bf16[512,1024]{1,0:T(8,128)(2,1)S(1)} %bitcast.122, bf16[512,1024]{1,0:T(8,128)(2,1)S(1)} %collective-permute-done.32.refs_2_.refs_4_, bf16[512,1024]{1,0:T(8,128)(2,1)S(1)} %collective-permute-done.33.refs_3_.refs_5_, ...), custom_call_target="tpu_custom_call" | custom-call | flops 4294967296 | bytes 10485760 | tf_op jit(solution)/shard_map/pallas_call | solution.py:646
  311.2 14.3 %collective-permute-done.38 = bf16[128,1024]{1,0:T(8,128)(2,1)S(1)} collective-permute-done((bf16[128,1024]{1,0:T(8,128)(2,1)S(1)}, bf16[128,1024]{1,0:T(8,128)(2,1)S(1)}, u32[]{:S(2)}, u32[]{:S(2)}) %collective-permute-start.38) | collective-permute-done | bytes 262176 | tf_op jit(solution)/shard_map/ppermute | solution.py:102
  327.6 11.0 %shard_map.816.refs_0_ = bf16[1024,2048]{1,0:T(8,128)(2,1)} custom-call(bf16[1024,2048]{1,0:T(8,128)(2,1)} %copy-done.13, f32[1024,1024]{1,0:T(8,128)} %get-tuple-element.116.refs_1_, f32[1024,1024]{1,0:T(8,128)} %get-tuple-element.117.refs_2_, bf16[512,1024]{1,0:T(8,128)(2,1)S(1)} %bitcast.123, ...), custom_call_target="tpu_custom_call" | custom-call | flops 4294967296 | bytes 20971520 | tf_op jit(solution)/shard_map/pallas_call | solution.py:611
  338.7 15.4 %shard_map.817 = bf16[1024,2048]{1,0:T(8,128)(2,1)} custom-call(bf16[1024,2048]{1,0:T(8,128)(2,1)} %shard_map.816.refs_0_, bf16[512,2048]{1,0:T(8,128)(2,1)} %bitcast.19.refs_1_.refs_5_, bf16[512,2048]{1,0:T(8,128)(2,1)} %collective-permute-done.29.refs_2_.refs_6_, bf16[512,2048]{1,0:T(8,128)(2,1)} %collective-permute-done.30.refs_3_.refs_7_, ...), custom_call_target="tpu_custom_call" | custom-call | flops 8589934592 | bytes 16777216 | tf_op jit(solution)/shard_map/pallas_call | solution.py:646
  357.5 10.6 %collective-permute-done.39 = bf16[128,2048]{1,0:T(8,128)(2,1)S(1)} collective-permute-done((bf16[128,2048]{1,0:T(8,128)(2,1)S(1)}, bf16[128,2048]{1,0:T(8,128)(2,1)S(1)}, u32[]{:S(2)}, u32[]{:S(2)}) %collective-permute-start.39) | collective-permute-done | bytes 524320 | tf_op jit(solution)/shard_map/ppermute | solution.py:102
  368.1 6.4 convolution_convert_fusion
  383.5 11.2 %collective-permute-done.41 = bf16[128,2048]{1,0:T(8,128)(2,1)S(1)} collective-permute-done((bf16[128,2048]{1,0:T(8,128)(2,1)S(1)}, bf16[128,2048]{1,0:T(8,128)(2,1)S(1)}, u32[]{:S(2)}, u32[]{:S(2)}) %collective-permute-start.41) | collective-permute-done | bytes 524320 | tf_op jit(solution)/shard_map/ppermute | solution.py:102
  398.1 6.9 %collective-permute-done.42 = bf16[128,2048]{1,0:T(8,128)(2,1)S(1)} collective-permute-done((bf16[128,2048]{1,0:T(8,128)(2,1)S(1)}, bf16[128,2048]{1,0:T(8,128)(2,1)S(1)}, u32[]{:S(2)}, u32[]{:S(2)}) %collective-permute-start.42) | collective-permute-done | bytes 524320 | tf_op jit(solution)/shard_map/ppermute | solution.py:102
  412.3 5.7 fusion.13
  425.2 8.0 %collective-permute-done.51 = bf16[128,2048]{1,0:T(8,128)(2,1)} collective-permute-done((bf16[128,2048]{1,0:T(8,128)(2,1)}, bf16[128,2048]{1,0:T(8,128)(2,1)}, u32[]{:S(2)}, u32[]{:S(2)}) %collective-permute-start.51) | collective-permute-done | bytes 524320 | tf_op jit(solution)/shard_map/ppermute | solution.py:102
  473.3 5.9 fusion.14
  488.1 9.0 %all-to-all-start.4 = ((bf16[8,128,512]{1,2,0:T(8,128)(2,1)}), bf16[8,128,512]{1,2,0:T(8,128)(2,1)}, u32[]{:S(2)}, u32[]{:S(2)}) async-start(bf16[8,128,512]{1,2,0:T(8,128)(2,1)} %maximum_bitcast_fusion), calls=%async_computation.4 | async-start | bytes 2097152 | tf_op jit(solution)/shard_map/all_to_all | solution.py:945
  497.8 8.2 %fusion.12 = bf16[512,2048]{1,0:T(8,128)(2,1)} fusion(f32[1024,2048]{1,0:T(8,128)} %copy-done.12, bf16[512,2048]{1,0:T(8,128)(2,1)} %collective-permute-done.56, bf16[1024,2048]{1,0:T(8,128)(2,1)} %shard_map.816.refs_0_, bf16[1024,2048]{1,0:T(8,128)(2,1)} %get-tuple-element.107.refs_0_), kind=kOutput, calls=%fused_computation.16 | convolution fusion | flops 2151677952 | bytes 13631488 | tf_op jit(solution)/shard_map/dot_general | solution.py:63
  506.0 8.7 %all-to-all-done.4 = bf16[8,128,512]{1,2,0:T(8,128)(2,1)} async-done(((bf16[8,128,512]{1,2,0:T(8,128)(2,1)}), bf16[8,128,512]{1,2,0:T(8,128)(2,1)}, u32[]{:S(2)}, u32[]{:S(2)}) %all-to-all-start.4) | async-done | bytes 1048608 | tf_op jit(solution)/shard_map/all_to_all | solution.py:945
  523.9 8.5 %shard_map.818 = bf16[1024,768]{1,0:T(8,128)(2,1)S(1)} custom-call(bf16[1024,256]{1,0:T(8,128)(2,1)S(1)} %get-tuple-element.128.query_ref, bf16[1024,256]{1,0:T(8,128)(2,1)S(1)} %copy-done.3, bf16[1024,256]{1,0:T(8,128)(2,1)S(1)} %copy-done.5, bf16[1024,256]{1,0:T(8,128)(2,1)S(1)} %slice.420.grad_ref, f32[1024,256]{1,0:T(8,128)S(1)} %copy-done.1, ...), custom_call_target="tpu_custom_call" | custom-call | flops 5368709120 | bytes 4194304 | tf_op jit(solution)/shard_map/pallas_call | solution.py:706
  550.6 15.5 %all-to-all-done.5.gradient_ref = bf16[8,64,2048]{2,1,0:T(8,128)(2,1)} async-done(((bf16[8,64,2048]{2,1,0:T(8,128)(2,1)}), bf16[8,64,2048]{2,1,0:T(8,128)(2,1)}, u32[]{:S(2)}, u32[]{:S(2)}) %all-to-all-start.5) | async-done | bytes 2097184 | tf_op jit(solution)/shard_map/all_to_all | solution.py:364
  566.0 6.6 multiply_reduce_fusion
  577.7 8.1 %shard_map.819 = (f32[64,8192]{1,0:T(8,128)}, f32[64,8192]{1,0:T(8,128)}, f32[64,8192]{1,0:T(8,128)}) custom-call(f32[64,8192]{1,0:T(8,128)} %weight_ref.10, f32[64,8192]{1,0:T(8,128)} %first_ref.4, f32[64,8192]{1,0:T(8,128)} %second_ref.4, bf16[8,64,1024]{2,1,0:T(8,128)(2,1)} %copy-done.18), custom_call_target="tpu_custom_call" | custom-call | flops 7864320 | bytes 13631488 | tf_op jit(solution)/shard_map/pallas_call | solution.py:394
  606.7 15.6 %shard_map.820 = (f32[64,16384]{1,0:T(8,128)}, f32[64,16384]{1,0:T(8,128)}, f32[64,16384]{1,0:T(8,128)}) custom-call(f32[64,16384]{1,0:T(8,128)} %weight_ref.11, f32[64,16384]{1,0:T(8,128)} %first_ref.5, f32[64,16384]{1,0:T(8,128)} %second_ref.5, bf16[8,64,2048]{2,1,0:T(8,128)(2,1)} %all-to-all-done.5.gradient_ref), custom_call_target="tpu_custom_call" | custom-call | flops 15728640 | bytes 27262976 | tf_op jit(solution)/shard_map/pallas_call | solution.py:394
  664.8 6.3 shard_map.821
  (447 shorter events, 319.3 us)
Async XLA Ops:
  5.2 67.9 %all-to-all-start = ((bf16[8,64,768]{2,1,0:T(8,128)(2,1)}), bf16[8,64,768]{2,1,0:T(8,128)(2,1)}, u32[]{:S(2)}, u32[]{:S(2)}) async-start(bf16[8,64,768]{2,1,0:T(8,128)(2,1)} %shard_map.809), calls=%async_computation | async-start | bytes 1572864 | tf_op jit(solution)/shard_map/all_to_all | solution.py:357
  34.6 23.9 %collective-permute-start.3 = (bf16[128,3072]{1,0:T(8,128)(2,1)S(1)}, bf16[128,3072]{1,0:T(8,128)(2,1)}, u32[]{:S(2)}, u32[]{:S(2)}) collective-permute-start(bf16[128,3072]{1,0:T(8,128)(2,1)S(1)} %maximum_maximum_fusion), channel_id=1, source_target_pairs={{0,8},{8,16},{16,24},{24,28},{28,20},{20,12},{12,4},{4,0},{1,9},{9... | collective-permute-start | bytes 2359304 | tf_op jit(solution)/shard_map/ppermute | solution.py:102
  77.8 58.5 %collective-permute-start.12 = (bf16[512,768]{1,0:T(8,128)(2,1)}, bf16[512,768]{1,0:T(8,128)(2,1)}, u32[]{:S(2)}, u32[]{:S(2)}) collective-permute-start(bf16[512,768]{1,0:T(8,128)(2,1)} %bitcast.7), channel_id=1, source_target_pairs={{0,1},{1,0},{2,3},{3,2},{4,5},{5,4},{6,7},{7,6},{8,9},{9,8},{10,11... | collective-permute-start | bytes 2359304 | tf_op jit(solution)/shard_map/ppermute | solution.py:91
  77.8 48.4 %collective-permute-start.11 = (bf16[512,768]{1,0:T(8,128)(2,1)}, bf16[512,768]{1,0:T(8,128)(2,1)}, u32[]{:S(2)}, u32[]{:S(2)}) collective-permute-start(bf16[512,768]{1,0:T(8,128)(2,1)} %bitcast.7), channel_id=1, source_target_pairs={{0,2},{1,3},{2,0},{3,1},{4,6},{5,7},{6,4},{7,5},{8,10},{9,11},{10,... | collective-permute-start | bytes 2359304 | tf_op jit(solution)/shard_map/ppermute | solution.py:91
  121.0 49.4 %all-to-all-start.1 = ((bf16[8,64,2048]{2,1,0:T(8,128)(2,1)}), bf16[8,64,2048]{2,1,0:T(8,128)(2,1)}, u32[]{:S(2)}, u32[]{:S(2)}) async-start(bf16[8,64,2048]{2,1,0:T(8,128)(2,1)} %shard_map.810), calls=%async_computation.1 | async-start | bytes 4194304 | tf_op jit(solution)/shard_map/all_to_all | solution.py:357
  128.5 83.9 %collective-permute-start.22 = (bf16[2048,512]{1,0:T(8,128)(2,1)}, bf16[2048,512]{1,0:T(8,128)(2,1)}, u32[]{:S(2)}, u32[]{:S(2)}) collective-permute-start(bf16[2048,512]{1,0:T(8,128)(2,1)} %maximum_dynamic-update-slice_fusion.9.refs_3_), channel_id=1, source_target_pairs={{0,2},{1,3},{2,0},{3,1},{4,6},{5,7},{6,4},{7,5},{8,10},{9,11},{10,... | collective-permute-start | bytes 6291464 | tf_op jit(solution)/shard_map/ppermute | solution.py:91
  170.3 34.9 %all-to-all-start.2 = ((bf16[8,64,1024]{2,1,0:T(8,128)(2,1)}), bf16[8,64,1024]{2,1,0:T(8,128)(2,1)S(1)}, u32[]{:S(2)}, u32[]{:S(2)}) async-start(bf16[8,64,1024]{2,1,0:T(8,128)(2,1)} %shard_map.811), calls=%async_computation.2 | async-start | bytes 2097152 | tf_op jit(solution)/shard_map/all_to_all | solution.py:357
  173.9 66.5 %collective-permute-start.29 = (bf16[512,2048]{1,0:T(8,128)(2,1)}, bf16[512,2048]{1,0:T(8,128)(2,1)}, u32[]{:S(2)}, u32[]{:S(2)}) collective-permute-start(bf16[512,2048]{1,0:T(8,128)(2,1)} %bitcast.19.refs_1_.refs_5_), channel_id=1, source_target_pairs={{0,2},{1,3},{2,0},{3,1},{4,6},{5,7},{6,4},{7,5},{8,10},{9,11},{10,... | collective-permute-start | bytes 6291464 | tf_op jit(solution)/shard_map/ppermute | solution.py:91
  175.5 29.0 %collective-permute-start.15 = (bf16[1024,256]{1,0:T(8,128)(2,1)S(1)}, bf16[1024,256]{1,0:T(8,128)(2,1)S(1)}, u32[]{:S(2)}, u32[]{:S(2)}) collective-permute-start(bf16[1024,256]{1,0:T(8,128)(2,1)S(1)} %get-tuple-element.101), channel_id=1, source_target_pairs={{0,4},{8,0},{16,8},{24,16},{28,24},{20,28},{12,20},{4,12},{1,5},{9... | collective-permute-start | bytes 1572872 | tf_op jit(solution)/shard_map/ppermute | solution.py:102
  177.3 27.9 %collective-permute-start.14 = (bf16[1024,256]{1,0:T(8,128)(2,1)S(1)}, bf16[1024,256]{1,0:T(8,128)(2,1)}, u32[]{:S(2)}, u32[]{:S(2)}) collective-permute-start(bf16[1024,256]{1,0:T(8,128)(2,1)S(1)} %get-tuple-element.101), channel_id=1, source_target_pairs={{0,8},{8,16},{16,24},{24,28},{28,20},{20,12},{12,4},{4,0},{1,9},{9... | collective-permute-start | bytes 1572872 | tf_op jit(solution)/shard_map/ppermute | solution.py:102
  212.4 41.8 %collective-permute-start.23 = (bf16[2048,512]{1,0:T(8,128)(2,1)}, bf16[2048,512]{1,0:T(8,128)(2,1)}, u32[]{:S(2)}, u32[]{:S(2)}) collective-permute-start(bf16[2048,512]{1,0:T(8,128)(2,1)} %maximum_dynamic-update-slice_fusion.9.refs_3_), channel_id=1, source_target_pairs={{0,1},{1,0},{2,3},{3,2},{4,5},{5,4},{6,7},{7,6},{8,9},{9,8},{10,11... | collective-permute-start | bytes 6291464 | tf_op jit(solution)/shard_map/ppermute | solution.py:91
  212.4 42.4 %collective-permute-start.24 = (bf16[2048,512]{1,0:T(8,128)(2,1)}, bf16[2048,512]{1,0:T(8,128)(2,1)}, u32[]{:S(2)}, u32[]{:S(2)}) collective-permute-start(bf16[2048,512]{1,0:T(8,128)(2,1)} %collective-permute-done.22.refs_4_), channel_id=1, source_target_pairs={{0,1},{1,0},{2,3},{3,2},{4,5},{5,4},{6,7},{7,6},{8,9},{9,8},{10,11... | collective-permute-start | bytes 6291464 | tf_op jit(solution)/shard_map/ppermute | solution.py:91
  240.4 37.5 %collective-permute-start.30 = (bf16[512,2048]{1,0:T(8,128)(2,1)}, bf16[512,2048]{1,0:T(8,128)(2,1)}, u32[]{:S(2)}, u32[]{:S(2)}) collective-permute-start(bf16[512,2048]{1,0:T(8,128)(2,1)} %bitcast.19.refs_1_.refs_5_), channel_id=1, source_target_pairs={{0,1},{1,0},{2,3},{3,2},{4,5},{5,4},{6,7},{7,6},{8,9},{9,8},{10,11... | collective-permute-start | bytes 6291464 | tf_op jit(solution)/shard_map/ppermute | solution.py:91
  240.5 37.8 %collective-permute-start.31 = (bf16[512,2048]{1,0:T(8,128)(2,1)}, bf16[512,2048]{1,0:T(8,128)(2,1)}, u32[]{:S(2)}, u32[]{:S(2)}) collective-permute-start(bf16[512,2048]{1,0:T(8,128)(2,1)} %collective-permute-done.29.refs_2_.refs_6_), channel_id=1, source_target_pairs={{0,1},{1,0},{2,3},{3,2},{4,5},{5,4},{6,7},{7,6},{8,9},{9,8},{10,11... | collective-permute-start | bytes 6291464 | tf_op jit(solution)/shard_map/ppermute | solution.py:91
  251.2 24.3 %collective-permute-start.32 = (bf16[512,1024]{1,0:T(8,128)(2,1)S(1)}, bf16[512,1024]{1,0:T(8,128)(2,1)S(1)}, u32[]{:S(2)}, u32[]{:S(2)}) collective-permute-start(bf16[512,1024]{1,0:T(8,128)(2,1)S(1)} %bitcast.120), channel_id=1, source_target_pairs={{0,2},{1,3},{2,0},{3,1},{4,6},{5,7},{6,4},{7,5},{8,10},{9,11},{10,... | collective-permute-start | bytes 3145736 | tf_op jit(solution)/shard_map/ppermute | solution.py:91
  254.2 21.4 %collective-permute-start.26 = (bf16[128,2048]{1,0:T(8,128)(2,1)S(1)}, bf16[128,2048]{1,0:T(8,128)(2,1)S(1)}, u32[]{:S(2)}, u32[]{:S(2)}) collective-permute-start(bf16[128,2048]{1,0:T(8,128)(2,1)S(1)} %pad_maximum_fusion.8), channel_id=1, source_target_pairs={{0,4},{8,0},{16,8},{24,16},{28,24},{20,28},{12,20},{4,12},{1,5},{9... | collective-permute-start | bytes 1572872 | tf_op jit(solution)/shard_map/ppermute | solution.py:102
  254.8 21.2 %collective-permute-start.25 = (bf16[128,2048]{1,0:T(8,128)(2,1)S(1)}, bf16[128,2048]{1,0:T(8,128)(2,1)S(1)}, u32[]{:S(2)}, u32[]{:S(2)}) collective-permute-start(bf16[128,2048]{1,0:T(8,128)(2,1)S(1)} %pad_maximum_fusion.8), channel_id=1, source_target_pairs={{0,8},{8,16},{16,24},{24,28},{28,20},{20,12},{12,4},{4,0},{1,9},{9... | collective-permute-start | bytes 1572872 | tf_op jit(solution)/shard_map/ppermute | solution.py:102
  306.8 50.7 %collective-permute-start.40 = (bf16[128,2048]{1,0:T(8,128)(2,1)S(1)}, bf16[128,2048]{1,0:T(8,128)(2,1)S(1)}, u32[]{:S(2)}, u32[]{:S(2)}) collective-permute-start(bf16[128,2048]{1,0:T(8,128)(2,1)S(1)} %get-tuple-element.262), channel_id=1, source_target_pairs={{0,4},{8,0},{16,8},{24,16},{28,24},{20,28},{12,20},{4,12},{1,5},{9... | collective-permute-start | bytes 1572872 | tf_op jit(solution)/shard_map/ppermute | solution.py:102
  374.5 36.7 %collective-permute-start.46 = (bf16[1024,2048]{1,0:T(8,128)(2,1)S(1)}, bf16[1024,2048]{1,0:T(8,128)(2,1)S(1)}, u32[]{:S(2)}, u32[]{:S(2)}) collective-permute-start(bf16[1024,2048]{1,0:T(8,128)(2,1)S(1)} %convolution_convert_fusion), channel_id=1, source_target_pairs={{0,1},{1,0},{2,3},{3,2},{4,5},{5,4},{6,7},{7,6},{8,9},{9,8},{10,11... | collective-permute-start | bytes 12582920 | tf_op jit(solution)/shard_map/ppermute | solution.py:91
  377.0 31.4 %collective-permute-start.45 = (bf16[1024,1024]{1,0:T(8,128)(2,1)S(1)}, bf16[1024,1024]{1,0:T(8,128)(2,1)S(1)}, u32[]{:S(2)}, u32[]{:S(2)}) collective-permute-start(bf16[1024,1024]{1,0:T(8,128)(2,1)S(1)} %fusion.25), channel_id=1, source_target_pairs={{0,1},{1,0},{2,3},{3,2},{4,5},{5,4},{6,7},{7,6},{8,9},{9,8},{10,11... | collective-permute-start | bytes 6291464 | tf_op jit(solution)/shard_map/ppermute | solution.py:91
  382.0 23.1 %collective-permute-start.42 = (bf16[128,2048]{1,0:T(8,128)(2,1)S(1)}, bf16[128,2048]{1,0:T(8,128)(2,1)S(1)}, u32[]{:S(2)}, u32[]{:S(2)}) collective-permute-start(bf16[128,2048]{1,0:T(8,128)(2,1)S(1)} %copy-done.35), channel_id=1, source_target_pairs={{0,8},{8,16},{16,24},{24,28},{28,20},{20,12},{12,4},{4,0},{1,9},{9... | collective-permute-start | bytes 1572872 | tf_op jit(solution)/shard_map/ppermute | solution.py:102
  421.6 29.1 %collective-permute-start.55 = (bf16[512,1024]{1,0:T(8,128)(2,1)}, bf16[512,1024]{1,0:T(8,128)(2,1)S(1)}, u32[]{:S(2)}, u32[]{:S(2)}) collective-permute-start(bf16[512,1024]{1,0:T(8,128)(2,1)} %fusion.21), channel_id=1, source_target_pairs={{0,2},{1,3},{2,0},{3,1},{4,6},{5,7},{6,4},{7,5},{8,10},{9,11},{10,... | collective-permute-start | bytes 3145736 | tf_op jit(solution)/shard_map/ppermute | solution.py:91
  423.1 21.2 %collective-permute-start.47 = (bf16[128,2048]{1,0:T(8,128)(2,1)S(1)}, bf16[128,2048]{1,0:T(8,128)(2,1)S(1)}, u32[]{:S(2)}, u32[]{:S(2)}) collective-permute-start(bf16[128,2048]{1,0:T(8,128)(2,1)S(1)} %get-tuple-element.124), channel_id=1, source_target_pairs={{0,8},{8,16},{16,24},{24,28},{28,20},{20,12},{12,4},{4,0},{1,9},{9... | collective-permute-start | bytes 1572872 | tf_op jit(solution)/shard_map/ppermute | solution.py:102
  437.7 22.1 %collective-permute-start.52 = (bf16[128,2048]{1,0:T(8,128)(2,1)}, bf16[128,2048]{1,0:T(8,128)(2,1)S(1)}, u32[]{:S(2)}, u32[]{:S(2)}) collective-permute-start(bf16[128,2048]{1,0:T(8,128)(2,1)} %get-tuple-element.254), channel_id=1, source_target_pairs={{0,8},{8,16},{16,24},{24,28},{28,20},{20,12},{12,4},{4,0},{1,9},{9... | collective-permute-start | bytes 1572872 | tf_op jit(solution)/shard_map/ppermute | solution.py:102
  454.2 34.0 %all-to-all-start.3 = ((bf16[8,64,1024]{2,1,0:T(8,128)(2,1)}), bf16[8,64,1024]{2,1,0:T(8,128)(2,1)S(1)}, u32[]{:S(2)}, u32[]{:S(2)}) async-start(bf16[8,64,1024]{2,1,0:T(8,128)(2,1)} %bitcast.141), calls=%async_computation.3 | async-start | bytes 2097152 | tf_op jit(solution)/shard_map/all_to_all | solution.py:364
  458.2 39.6 %collective-permute-start.56 = (bf16[512,2048]{1,0:T(8,128)(2,1)}, bf16[512,2048]{1,0:T(8,128)(2,1)}, u32[]{:S(2)}, u32[]{:S(2)}) collective-permute-start(bf16[512,2048]{1,0:T(8,128)(2,1)} %fusion.13), channel_id=1, source_target_pairs={{0,2},{1,3},{2,0},{3,1},{4,6},{5,7},{6,4},{7,5},{8,10},{9,11},{10,... | collective-permute-start | bytes 6291464 | tf_op jit(solution)/shard_map/ppermute | solution.py:91
  488.1 26.6 %all-to-all-start.4 = ((bf16[8,128,512]{1,2,0:T(8,128)(2,1)}), bf16[8,128,512]{1,2,0:T(8,128)(2,1)}, u32[]{:S(2)}, u32[]{:S(2)}) async-start(bf16[8,128,512]{1,2,0:T(8,128)(2,1)} %maximum_bitcast_fusion), calls=%async_computation.4 | async-start | bytes 2097152 | tf_op jit(solution)/shard_map/all_to_all | solution.py:945
  518.0 48.0 %all-to-all-start.5 = ((bf16[8,64,2048]{2,1,0:T(8,128)(2,1)}), bf16[8,64,2048]{2,1,0:T(8,128)(2,1)}, u32[]{:S(2)}, u32[]{:S(2)}) async-start(bf16[8,64,2048]{2,1,0:T(8,128)(2,1)} %bitcast.128), calls=%async_computation.5 | async-start | bytes 4194304 | tf_op jit(solution)/shard_map/all_to_all | solution.py:364
  542.8 43.0 %collective-permute-start.74 = (bf16[1,512,256]{2,1,0:T(8,128)(2,1)S(1)}, bf16[1,512,256]{2,1,0:T(8,128)(2,1)S(1)}, u32[]{:S(2)}, u32[]{:S(2)}) collective-permute-start(bf16[1,512,256]{2,1,0:T(8,128)(2,1)S(1)} %slice_bitcast_fusion.2), channel_id=1, source_target_pairs={{0,2},{1,3},{2,0},{3,1},{4,6},{5,7},{6,4},{7,5},{8,10},{9,11},{10,... | collective-permute-start | bytes 786440 | tf_op jit(solution)/shard_map/ppermute | solution.py:91
  550.1 41.3 %collective-permute-start.72 = (bf16[512,768]{1,0:T(8,128)(2,1)}, bf16[512,768]{1,0:T(8,128)(2,1)}, u32[]{:S(2)}, u32[]{:S(2)}) collective-permute-start(bf16[512,768]{1,0:T(8,128)(2,1)} %fusion.33), channel_id=1, source_target_pairs={{0,2},{1,3},{2,0},{3,1},{4,6},{5,7},{6,4},{7,5},{8,10},{9,11},{10,... | collective-permute-start | bytes 2359304 | tf_op jit(solution)/shard_map/ppermute | solution.py:91
  600.8 45.7 %all-to-all-start.6 = ((bf16[8,64,1024]{2,1,0:T(8,128)(2,1)}), bf16[8,64,1024]{2,1,0:T(8,128)(2,1)S(1)}, u32[]{:S(2)}, u32[]{:S(2)}) async-start(bf16[8,64,1024]{2,1,0:T(8,128)(2,1)} %pad_maximum_fusion.2), calls=%async_computation.6 | async-start | bytes 2097152 | tf_op jit(solution)/shard_map/all_to_all | solution.py:364
  647.7 23.5 %all-to-all-start.7 = ((f32[32,2,2048]{2,1,0:T(2,128)}), f32[32,2,2048]{2,1,0:T(2,128)S(1)}, u32[]{:S(2)}, u32[]{:S(2)}) async-start(f32[32,2,2048]{2,1,0:T(2,128)} %broadcast_in_dim.29), calls=%async_computation.7 | async-start | bytes 1048576 | tf_op jit(solution)/shard_map/all_to_all | solution.py:225
  (105 other events, 1556.3 us)

commit v3 on v2

--- a/solution.py
+++ b/solution.py
@@ -104,9 +104,10 @@
 
 def ring_place(offset):
     count = lax.axis_size("seq")
-    order = ring_order(count)
-    table = jnp.array([order[(order.index(own) + offset) % count] for own in range(count)], jnp.int32)
-    return table[lax.axis_index("seq")]
+    own = lax.axis_index("seq")
+    standing = jnp.where(own % 2 == 0, own // 2, count - 1 - own // 2)
+    there = (standing + offset + count) % count
+    return jnp.where(there < count // 2, 2 * there, 2 * (count - 1 - there) + 1)
 
 
 def filled(arrays, filler):
@@ -171,58 +172,45 @@
     return (block.astype(jnp.float32) + got.astype(jnp.float32)).astype(block.dtype)
 
 
-def ring_scatter_sum(parts, fillers=()):
+def ring_scatter_sum(blocks, fillers=()):
     far = lax.axis_size("seq") // 2
-    first, second = parts
-    ahead, behind = [ring_shift(first[far], 1)], [ring_shift(second[far], -1)]
+    middle = blocks[0].shape[1] // 2
+    ahead = ring_shift(blocks[far][:, :middle], 1)
+    behind = ring_shift(blocks[far][:, middle:], -1)
     for turn, step in enumerate(range(far - 1, 0, -1)):
-        onward = [first[step], second[step]]
-        backward = [first[-step], second[-step]]
+        onward, backward = blocks[step], blocks[-step]
         if turn == 0:
-            onward[0] = added(onward[0], ahead[0])
-            backward[1] = added(backward[1], behind[0])
+            onward = jnp.concatenate([added(onward[:, :middle], ahead), onward[:, middle:]], axis=1)
+            backward = jnp.concatenate(
+                [backward[:, :middle], added(backward[:, middle:], behind)], axis=1
+            )
         else:
-            onward = [added(block, got) for block, got in zip(onward, ahead)]
-            backward = [added(block, got) for block, got in zip(backward, behind)]
+            onward, backward = added(onward, ahead), added(backward, behind)
         if turn < len(fillers):
-            needed = fillers[turn]
-            if callable(needed):
-                needed = needed(ahead + behind)
-            moved = after_all(onward + backward, needed)
-            onward, backward = moved[:2], moved[2:]
-        ahead = [ring_shift(block, 1) for block in onward]
-        behind = [ring_shift(block, -1) for block in backward]
+            onward, backward = filled([onward, backward], fillers[turn])
+        ahead, behind = ring_shift(onward, 1), ring_shift(backward, -1)
     if far - 1 < len(fillers):
-        needed = fillers[far - 1]
-        if callable(needed):
-            needed = needed(ahead + behind)
-        moved = after_all(ahead + behind, needed)
-        ahead, behind = moved[:2], moved[2:]
-    return [
-        own.astype(jnp.float32) + left.astype(jnp.float32) + right.astype(jnp.float32)
-        for own, left, right in zip((first[0], second[0]), ahead, behind)
-    ]
-
-
-def ring_scatter_one(whole, fillers=()):
+        ahead, behind = filled([ahead, behind], fillers[far - 1])
+    return blocks[0].astype(jnp.float32) + ahead.astype(jnp.float32) + behind.astype(jnp.float32)
+
+
+def ring_blocks(wholes):
     far = lax.axis_size("seq") // 2
-    middle = whole.shape[1] // 2
-    offsets = [0] + [sign * step for step in range(1, far) for sign in (1, -1)] + [far]
-    blocks = {offset: ring_rows(whole, [offset]) for offset in offsets}
-    halves = ring_scatter_sum(
-        (
-            {offset: block[:, :middle] for offset, block in blocks.items()},
-            {offset: block[:, middle:] for offset, block in blocks.items()},
-        ),
-        fillers,
-    )
-    return jnp.concatenate(halves, axis=1)
-
-
-def sum_everywhere(values):
-    total = lax.axis_size("seq") * lax.axis_size("batch")
-    copies = jnp.broadcast_to(values[None], (total,) + values.shape)
-    return jnp.sum(lax.all_to_all(copies, ("seq", "batch"), 0, 0, tiled=True), axis=0)
+    offsets = [far] + [sign * step for step in range(far - 1, 0, -1) for sign in (1, -1)] + [0]
+    return {
+        offset: jnp.concatenate([ring_rows(whole, [offset]) for whole in wholes], axis=1)
+        for offset in offsets
+    }
+
+
+def butterfly_steps():
+    steps = []
+    for axis in ("batch", "seq"):
+        bit = 1
+        while bit < lax.axis_size(axis):
+            steps.append((axis, bit))
+            bit *= 2
+    return steps
 
 
 def after(value, *others):
@@ -724,7 +712,7 @@
         ],
         compiler_params=pltpu.CompilerParams(vmem_limit_bytes=48 << 20),
         cost_estimate=pl.CostEstimate(
-            flops=20 * work * LANES, bytes_accessed=query.size * 16, transcendentals=2 * work
+            flops=work * LANES, bytes_accessed=query.size * 4, transcendentals=work // 16
         ),
     )(query, key, value, grad, attended, total, cos_table, sin_table, starts)
 
@@ -827,7 +815,6 @@
             axis=1,
         ).astype(jnp.bfloat16)
 
-    far = seq_total // 2
     first_row = lax.axis_index("seq") * local_rows
     gains_here = to_relative(gains, rows_own)
     tokens_here = to_relative(tokens[0], rows_own)
@@ -861,11 +848,11 @@
     out_full = jnp.concatenate(out_pieces, axis=1)
 
     gate_block = after(gate_block, attn_own)
-    down_block = to_column_owners(after(down_low, gate_block))
     attn_own_late = after(attn_own, gate_block)
-    attn_all = stacked_columns(ring_gather([attn_own_late], ((down_block,),))[0])
+    attn_all = stacked_columns(ring_gather([attn_own_late])[0])
+    down_block = to_column_owners(after(down_low, attn_all))
     gate_pieces, down_pieces = gather_pieces(gate_block), gather_pieces(down_block)
-    grads_here_late = after(grads_here, attn_all)
+    grads_here_late = after(grads_here, down_block)
     if in_pairs and length * model_width <= 1 << 21:
         middle_all, act_two = project_rows(attn_all, tokens_all, gains_here[1:], out_pieces)
         gate_part, up_part, hidden_low = hidden_units(act_two, gate_pieces)
@@ -878,7 +865,7 @@
 
         grads_all = ring_gather(
             [grads_here_late],
-            ((act_two,), block_meanwhile, lambda moved: after_all(moved, (late["block"],))),
+            ((hidden_low,), block_meanwhile, lambda moved: after_all(moved, (late["block"],))),
         )
         grads_all, block_part = stacked_rows(grads_all[0]), late["block"]
         grad_gate_up = hidden_back(grads_all, gate_part, up_part, down_pieces)
@@ -902,25 +889,21 @@
         grad_two = contract_cols(grad_gate_up, gate_full).astype(jnp.bfloat16)
         block_part = contract_cols(hidden_low, down_full).astype(jnp.bfloat16)
 
-    offsets = [far] + [sign * step for step in range(far - 1, 0, -1) for sign in (1, -1)] + [0]
     sums = {}
 
-    def weight_sums(arrived):
-        late = after_all((hidden_low, grad_gate_up), arrived)
-        sums["down"] = partial_sum_batch(grads_all, late[0])
-        sums["gate"] = partial_sum_batch(act_two, late[1])
-        return ()
+    def weight_sums(moved):
+        *moved, low, grad = lax.optimization_barrier((*moved, hidden_low, grad_gate_up))
+        sums["down"] = partial_sum_batch(grads_all, low)
+        sums["gate"] = partial_sum_batch(act_two, grad)
+        return moved
 
     def sent(stage):
-        return lambda arrived: (sums["down"][1][stage], sums["gate"][1][stage])
-
-    grad_two, block_rest = ring_scatter_sum(
-        [
-            {offset: ring_rows(whole, [offset]) for offset in offsets}
-            for whole in (grad_two, block_part)
-        ],
-        (weight_sums, lambda arrived: (*sent(0)(arrived), *sent(-1)(arrived))),
-    )
+        return lambda moved: after_all(moved, (sums["down"][1][stage], sums["gate"][1][stage]))
+
+    summed = ring_scatter_sum(
+        ring_blocks([grad_two, block_part]), (weight_sums, sent(0), sent(-1))
+    )
+    grad_two, block_rest = summed[:, :model_width], summed[:, model_width:]
     down_own, gate_own = sums["down"][0], sums["gate"][0]
 
     def own_rows(whole):
@@ -964,30 +947,55 @@
     down_m, down_s, down_w = adam_by_owner(
         down_weight, down_first, down_second, down_grad, 1, rate_down
     )
-    gate_m, gate_s, gate_w = adam_by_owner(
-        gate_up_weight, gate_up_first, gate_up_second, gate_grad, 2, rate_gate
-    )
-
-    def last_transfer(arrived):
-        both = jnp.concatenate([after(qkv_own, gate_grad, *arrived), out_own], axis=1)
-        sums["rest"] = to_row_owners(both)
-        return (gate_m,)
-
-    grad_one = ring_scatter_one(
-        after(grad_one_part.astype(jnp.bfloat16), gate_grad),
-        ((qkv_sends[-1], down_m), last_transfer, (), lambda arrived: (sums["rest"],)),
-    )
-    qkv_grad = sums["rest"]
-    gain_grad = sum_everywhere(after(gain_grad, qkv_grad))
+    steps = butterfly_steps()
+
+    def next_gain_sum():
+        if steps:
+            axis, bit = steps.pop(0)
+            sums["gain"] = sums["gain"] + swapped(sums["gain"], axis, bit)
+
+    def tied(moved, *names):
+        moved = lax.optimization_barrier((*moved, *(sums[name] for name in names)))
+        for name, value in zip(names, moved[len(moved) - len(names) :]):
+            sums[name] = value
+        next_gain_sum()
+        return moved[: len(moved) - len(names)]
+
+    def gate_update(moved):
+        moved = tied(moved, "gain", "gate_grad")
+        sums["gate_new"] = adam_by_owner(
+            gate_up_weight, gate_up_first, gate_up_second, sums["gate_grad"], 2, rate_gate
+        )
+        return moved
+
+    def last_transfer(moved):
+        moved = tied(after_all(moved, (sums["gate_new"][0],)), "gain")
+        return moved
+
+    def last_updates(moved):
+        sums["qkv"] = adam_by_owner(
+            qkv_weight, qkv_first, qkv_second, sums["rest"], 3, rate_qkv
+        )
+        sums["out"] = adam_by_owner(
+            out_weight, out_first, out_second, sums["rest"], 1, rate_out, skipped=3
+        )
+        return tied(after_all(moved, (sums["qkv"][0], sums["out"][0])), "gain")
+
+    sums["gain"], sums["gate_grad"] = gain_grad, gate_grad
+    next_gain_sum()
+    sums["rest"] = to_row_owners(jnp.concatenate([after(qkv_own, gate_grad), out_own], axis=1))
+    grad_one = ring_scatter_sum(
+        ring_blocks([after(grad_one_part.astype(jnp.bfloat16), qkv_sends[-1], down_m)]),
+        (gate_update, last_transfer, lambda moved: tied(moved, "gain"), last_updates),
+    )
+    while steps:
+        next_gain_sum()
+    gain_grad = sums["gain"]
+    (qkv_m, qkv_s, qkv_w), (out_m, out_s, out_w) = sums["qkv"], sums["out"]
+    gate_m, gate_s, gate_w = sums["gate_new"]
     unit_one, scale_one = unit_rows(tokens_here.astype(jnp.float32))
     grad_in_norm = norm_back(grad_one, unit_one, scale_one, gains_here[0])[0]
     input_grad = from_relative(grad_middle + grad_in_norm, rows_own)
-    qkv_m, qkv_s, qkv_w = adam_by_owner(
-        qkv_weight, qkv_first, qkv_second, qkv_grad, 3, rate_qkv
-    )
-    out_m, out_s, out_w = adam_by_owner(
-        out_weight, out_first, out_second, qkv_grad, 1, rate_out, skipped=3
-    )
     gain_m, gain_s, gain_w = adam_update(gains, gain_first, gain_second, gain_grad, rate_gain)
     return (
         block_out[None],

time: 682 us -> 652 us (0.956)
  starting transfers between devices: 118 us -> 106 us
  local copies, waits for them, and re-layouts: 70.2 us -> 58.6 us
  between operations: 11.7 us -> 2.51 us
    ppermute x23 -> x28, waiting for transfers between devices: 5.61 us -> 34.6 us  [swapped(): lax.ppermute(value, axis, [(source, source ^ bit) for source in range(cou...]
    ppermute x52 -> x40, waiting for transfers between devices: 175 us -> 146 us  [ring_shift(): return lax.ppermute(value, 'seq', pairs)]
    all_to_all x3, waiting for transfers between devices: 17.1 us -> 0.01 us  [to_row_owners(): return lax.all_to_all(blocks, 'seq', 0, 0, tiled=True)]
    ppermute x52 -> x40, starting transfers between devices: 62.4 us -> 45.7 us  [ring_shift(): return lax.ppermute(value, 'seq', pairs)]
    all_to_all x1, waiting for transfers between devices: 8.69 us -> 24 us  [on_device(): got = lax.all_to_all(by_owner, 'seq', 0, 0, tiled=True)]
    ppermute x23 -> x28, starting transfers between devices: 15.9 us -> 19.3 us  [swapped(): lax.ppermute(value, axis, [(source, source ^ bit) for source in range(cou...]
    unnamed x112 -> x90, local copies, waits for them, and re-layouts: 14.7 us -> 13.6 us
  transfers between devices with their start and end apart: 83 -> 75, of which waited for: 42 -> 35; matrix products, arithmetic and copies ran while one was open for 24% -> 25% of each run, Pallas kernels for 19% -> 19%
where the time goes in v3:
time: 652 us; the launch traced here: 642 us
  waiting for transfers between devices  224 us (34%)
  Pallas kernels  135 us (21%)
  starting transfers between devices  106 us (16%)
  matrix products  67.6 us (10%)
  local copies, waits for them, and re-layouts  58.6 us (9%)
  other arithmetic  48.6 us (7%)
    ppermute x40, waiting for transfers between devices, ring_shift(): return lax.ppermute(value, 'seq', pairs)  146 us
    ppermute x40, starting transfers between devices, ring_shift(): return lax.ppermute(value, 'seq', pairs)  45.7 us
    dot_general x10, matrix products, contract_rows(): lax.dot_general(left_side, right_side, (((0,), (0,)), ((), ())), preferre...  44.6 us
    ppermute x28, waiting for transfers between devices, swapped(): lax.ppermute(value, axis, [(source, source ^ bit) for source in range(cou...  34.6 us
    pallas_call x4, Pallas kernels, adam_by_owner(): pl.pallas_call(kernel, grid=(groups, steps), in_specs=[whole] * 3 + [pl.B...  32.8 us
    pallas_call x2, Pallas kernels, back_to_model(): pl.pallas_call(lambda *refs: back_kernel(total, *refs), grid=(total * eac...  24 us
    all_to_all x1, waiting for transfers between devices, on_device(): got = lax.all_to_all(by_owner, 'seq', 0, 0, tiled=True)  24 us
    pallas_call x3, Pallas kernels, rounded_by_owner(): pl.pallas_call(kernel, grid=(groups, steps), in_specs=[pl.BlockSpec((rows...  19.6 us
  transfers between devices with their start and end apart: 75, of which 35 were waited for; matrix products, arithmetic and copies ran while one was open for 25% of the time, Pallas kernels for 19%

profile of v3, /device:TPU:0, one launch (start us, length us, event | category | flops | bytes accessed | tf_op | source)
XLA Modules:
  0.0 642.2 jit_solution(7968978548000220594)
XLA Ops:
  5.1 7.3 %all-to-all-start = ((bf16[8,64,768]{2,1,0:T(8,128)(2,1)}), bf16[8,64,768]{2,1,0:T(8,128)(2,1)}, u32[]{:S(2)}, u32[]{:S(2)}) async-start(bf16[8,64,768]{2,1,0:T(8,128)(2,1)} %shard_map.305), calls=%async_computation | async-start | bytes 1572864 | tf_op jit(solution)/shard_map/all_to_all | solution.py:345
  30.9 9.8 %shard_map.306 = bf16[8,64,2048]{2,1,0:T(8,128)(2,1)} custom-call(f32[64,16384]{1,0:T(8,128)} %weight_ref.11), custom_call_target="tpu_custom_call" | custom-call | bytes 6291456 | tf_op jit(solution)/shard_map/pallas_call | solution.py:332
  48.1 12.3 %collective-permute-done.4 = bf16[128,3072]{1,0:T(8,128)(2,1)S(1)} collective-permute-done((bf16[128,3072]{1,0:T(8,128)(2,1)S(1)}, bf16[128,3072]{1,0:T(8,128)(2,1)S(1)}, u32[]{:S(2)}, u32[]{:S(2)}) %collective-permute-start.4) | collective-permute-done | bytes 786464 | tf_op jit(solution)/shard_map/ppermute | solution.py:102
  67.4 12.9 %collective-permute-done.5 = bf16[128,3072]{1,0:T(8,128)(2,1)S(1)} collective-permute-done((bf16[128,3072]{1,0:T(8,128)(2,1)}, bf16[128,3072]{1,0:T(8,128)(2,1)S(1)}, u32[]{:S(2)}, u32[]{:S(2)}) %collective-permute-start.5) | collective-permute-done | bytes 786464 | tf_op jit(solution)/shard_map/ppermute | solution.py:102
  85.8 13.4 %collective-permute-done.7 = bf16[128,3072]{1,0:T(8,128)(2,1)S(1)} collective-permute-done((bf16[128,3072]{1,0:T(8,128)(2,1)S(1)}, bf16[128,3072]{1,0:T(8,128)(2,1)S(1)}, u32[]{:S(2)}, u32[]{:S(2)}) %collective-permute-start.7) | collective-permute-done | bytes 786464 | tf_op jit(solution)/shard_map/ppermute | solution.py:102
  125.7 8.4 %fusion.56.query_in.key_in.value_in = f32[1024,768]{1,0:T(8,128)} fusion(bf16[1024,2048]{1,0:T(8,128)(2,1)S(1)} %fusion.2, bf16[512,768]{1,0:T(8,128)(2,1)S(1)} %collective-permute-done.13, bf16[512,768]{1,0:T(8,128)(2,1)} %collective-permute-done.12, bf16[512,768]{1,0:T(8,128)(2,1)} %collective-permute-done.11, bf16[512,768]{1,0:T(8,128)(2,1)} %bitcast.5), kind=kOutput, calls=%fused_computation.86 | convolution fusion | flops 3233808384 | bytes 10485760 | tf_op jit(solution)/shard_map/dot_general | solution.py:75
  134.1 8.7 %shard_map.308 = (f32[1024,256]{1,0:T(8,128)S(1)}, bf16[1024,256]{1,0:T(8,128)(2,1)S(1)}, bf16[1024,256]{1,0:T(8,128)(2,1)S(1)}, bf16[1024,256]{1,0:T(8,128)(2,1...) custom-call(f32[1024,768]{1,0:T(8,128)} %fusion.56.query_in.key_in.value_in, ...), custom_call_target="tpu_custom_call" | custom-call | flops 2147483648 | bytes 6291456 | tf_op jit(solution)/shard_map/pallas_call | solution.py:657
  145.4 14.0 %all-to-all-done.1 = bf16[8,64,2048]{2,1,0:T(8,128)(2,1)} async-done(((bf16[8,64,2048]{2,1,0:T(8,128)(2,1)}), bf16[8,64,2048]{2,1,0:T(8,128)(2,1)}, u32[]{:S(2)}, u32[]{:S(2)}) %all-to-all-start.1) | async-done | bytes 2097184 | tf_op jit(solution)/shard_map/all_to_all | solution.py:345
  164.4 8.0 %collective-permute-done.15 = bf16[1024,256]{1,0:T(8,128)(2,1)S(1)} collective-permute-done((bf16[1024,256]{1,0:T(8,128)(2,1)S(1)}, bf16[1024,256]{1,0:T(8,128)(2,1)S(1)}, u32[]{:S(2)}, u32[]{:S(2)}) %collective-permute-start.15) | collective-permute-done | bytes 524320 | tf_op jit(solution)/shard_map/ppermute | solution.py:102
  174.9 9.5 %collective-permute-done.17 = bf16[1024,256]{1,0:T(8,128)(2,1)S(1)} collective-permute-done((bf16[1024,256]{1,0:T(8,128)(2,1)S(1)}, bf16[1024,256]{1,0:T(8,128)(2,1)S(1)}, u32[]{:S(2)}, u32[]{:S(2)}) %collective-permute-start.17) | collective-permute-done | bytes 524320 | tf_op jit(solution)/shard_map/ppermute | solution.py:102
  202.6 8.2 %collective-permute-done.27.refs_2_.refs_6_ = bf16[512,2048]{1,0:T(8,128)(2,1)} collective-permute-done((bf16[512,2048]{1,0:T(8,128)(2,1)}, bf16[512,2048]{1,0:T(8,128)(2,1)}, u32[]{:S(2)}, u32[]{:S(2)}) %collective-permute-start.27) | collective-permute-done | bytes 2097184 | tf_op jit(solution)/shard_map/ppermute | solution.py:91
  224.7 15.9 %shard_map.309 = (f32[1024,2048]{1,0:T(8,128)}, bf16[1024,2048]{1,0:T(8,128)(2,1)}) custom-call(bf16[1024,2048]{1,0:T(8,128)(2,1)} %maximum_dynamic-update-slice_fusion.refs_0_, bf16[1024,2048]{1,0:T(8,128)(2,1)} %fusion.59.refs_1_, f32[1,2048]{1,0:T(1,128)S(1)} %get-tuple-element.302.refs_2_, bf16[2048,512]{1,0:T(8,128)(2,1)} %maximum_dynamic-update-slice_fusion.9.refs_3_, ...), custom_call_target="tpu_custom_call" | custom-call | flops 8589934592 | bytes 29360128 | tf_op jit(solution)/shard_map/pallas_call | solution.py:518
  249.7 14.3 %shard_map.310 = (f32[1024,1024]{1,0:T(8,128)}, f32[1024,1024]{1,0:T(8,128)}, bf16[1024,1024]{1,0:T(8,128)(2,1)S(1)}) custom-call(bf16[1024,2048]{1,0:T(8,128)(2,1)} %get-tuple-element.101.refs_0_, bf16[512,2048]{1,0:T(8,128)(2,1)} %bitcast.12.refs_1_.refs_5_, bf16[512,2048]{1,0:T(8,128)(2,1)} %collective-permute-done.27.refs_2_.refs_6_, ...), custom_call_target="tpu_custom_call" | custom-call | flops 8589934592 | bytes 23068672 | tf_op jit(solution)/shard_map/pallas_call | solution.py:562
  279.0 9.4 %collective-permute-done.32 = bf16[128,2048]{1,0:T(8,128)(2,1)S(1)} collective-permute-done((bf16[128,2048]{1,0:T(8,128)(2,1)S(1)}, bf16[128,2048]{1,0:T(8,128)(2,1)S(1)}, u32[]{:S(2)}, u32[]{:S(2)}) %collective-permute-start.32) | collective-permute-done | bytes 524320 | tf_op jit(solution)/shard_map/ppermute | solution.py:102
  290.5 8.8 %shard_map.311 = bf16[1024,2048]{1,0:T(8,128)(2,1)} custom-call(bf16[1024,1024]{1,0:T(8,128)(2,1)} %copy-done.6, bf16[512,1024]{1,0:T(8,128)(2,1)S(1)} %bitcast.104, bf16[512,1024]{1,0:T(8,128)(2,1)S(1)} %collective-permute-done.34.refs_2_.refs_4_, bf16[512,1024]{1,0:T(8,128)(2,1)S(1)} %collective-permute-done.35.refs_3_.refs_5_, ...), custom_call_target="tpu_custom_call" | custom-call | flops 4294967296 | bytes 10485760 | tf_op jit(solution)/shard_map/pallas_call | solution.py:634
  310.3 11.1 %shard_map.312.refs_0_ = bf16[1024,2048]{1,0:T(8,128)(2,1)} custom-call(bf16[1024,2048]{1,0:T(8,128)(2,1)} %copy-done.10, f32[1024,1024]{1,0:T(8,128)} %get-tuple-element.110.refs_1_, f32[1024,1024]{1,0:T(8,128)} %get-tuple-element.111.refs_2_, bf16[512,1024]{1,0:T(8,128)(2,1)S(1)} %bitcast.105, ...), custom_call_target="tpu_custom_call" | custom-call | flops 4294967296 | bytes 20971520 | tf_op jit(solution)/shard_map/pallas_call | solution.py:599
  321.3 15.3 %shard_map.313 = bf16[1024,2048]{1,0:T(8,128)(2,1)} custom-call(bf16[1024,2048]{1,0:T(8,128)(2,1)} %shard_map.312.refs_0_, bf16[512,2048]{1,0:T(8,128)(2,1)} %bitcast.12.refs_1_.refs_5_, bf16[512,2048]{1,0:T(8,128)(2,1)} %collective-permute-done.27.refs_2_.refs_6_, bf16[512,2048]{1,0:T(8,128)(2,1)} %collective-permute-done.28.refs_3_.refs_7_, ...), custom_call_target="tpu_custom_call" | custom-call | flops 8589934592 | bytes 16777216 | tf_op jit(solution)/shard_map/pallas_call | solution.py:634
  342.8 9.7 %collective-permute-done.39 = bf16[128,2048]{1,0:T(8,128)(2,1)S(1)} collective-permute-done((bf16[128,2048]{1,0:T(8,128)(2,1)S(1)}, bf16[128,2048]{1,0:T(8,128)(2,1)S(1)}, u32[]{:S(2)}, u32[]{:S(2)}) %collective-permute-start.39) | collective-permute-done | bytes 524320 | tf_op jit(solution)/shard_map/ppermute | solution.py:102
  359.6 6.3 convolution_convert_fusion
  366.4 6.8 %collective-permute-done.41 = bf16[128,4096]{1,0:T(8,128)(2,1)S(1)} collective-permute-done((bf16[128,4096]{1,0:T(8,128)(2,1)S(1)}, bf16[128,4096]{1,0:T(8,128)(2,1)S(1)}, u32[]{:S(2)}, u32[]{:S(2)}) %collective-permute-start.41) | collective-permute-done | bytes 1048608 | tf_op jit(solution)/shard_map/ppermute | solution.py:102
  379.0 14.8 %collective-permute-done.43 = bf16[128,4096]{1,0:T(8,128)(2,1)S(1)} collective-permute-done((bf16[128,4096]{1,0:T(8,128)(2,1)S(1)}, bf16[128,4096]{1,0:T(8,128)(2,1)S(1)}, u32[]{:S(2)}, u32[]{:S(2)}) %collective-permute-start.43) | collective-permute-done | bytes 1048608 | tf_op jit(solution)/shard_map/ppermute | solution.py:102
  415.7 13.1 %collective-permute-done.47 = bf16[128,4096]{1,0:T(8,128)(2,1)} collective-permute-done((bf16[128,4096]{1,0:T(8,128)(2,1)}, bf16[128,4096]{1,0:T(8,128)(2,1)}, u32[]{:S(2)}, u32[]{:S(2)}) %collective-permute-start.47) | collective-permute-done | bytes 1048608 | tf_op jit(solution)/shard_map/ppermute | solution.py:102
  452.1 10.4 %all-to-all-start.4 = ((bf16[8,128,512]{1,2,0:T(8,128)(2,1)}), bf16[8,128,512]{1,2,0:T(8,128)(2,1)}, u32[]{:S(2)}, u32[]{:S(2)}) async-start(bf16[8,128,512]{1,2,0:T(8,128)(2,1)} %maximum_bitcast_fusion), calls=%async_computation.4 | async-start | bytes 2097152 | tf_op jit(solution)/shard_map/all_to_all | solution.py:928
  462.5 8.2 %fusion.12 = bf16[512,2048]{1,0:T(8,128)(2,1)} fusion(f32[1024,2048]{1,0:T(8,128)} %copy-done.9, bf16[512,2048]{1,0:T(8,128)(2,1)} %collective-permute-done.50, bf16[1024,2048]{1,0:T(8,128)(2,1)} %shard_map.312.refs_0_, bf16[1024,2048]{1,0:T(8,128)(2,1)} %get-tuple-element.101.refs_0_), kind=kOutput, calls=%fused_computation.16 | convolution fusion | flops 2151677952 | bytes 13631488 | tf_op jit(solution)/shard_map/dot_general | solution.py:63
  470.7 24.0 %all-to-all-done.4 = bf16[8,128,512]{1,2,0:T(8,128)(2,1)} async-done(((bf16[8,128,512]{1,2,0:T(8,128)(2,1)}), bf16[8,128,512]{1,2,0:T(8,128)(2,1)}, u32[]{:S(2)}, u32[]{:S(2)}) %all-to-all-start.4) | async-done | bytes 1048608 | tf_op jit(solution)/shard_map/all_to_all | solution.py:928
  504.1 8.5 %shard_map.314 = bf16[1024,768]{1,0:T(8,128)(2,1)S(1)} custom-call(bf16[1024,256]{1,0:T(8,128)(2,1)S(1)} %get-tuple-element.120.query_ref, bf16[1024,256]{1,0:T(8,128)(2,1)S(1)} %copy-done.3, bf16[1024,256]{1,0:T(8,128)(2,1)S(1)} %copy-done.5, bf16[1024,256]{1,0:T(8,128)(2,1)S(1)} %slice.390.grad_ref, f32[1024,256]{1,0:T(8,128)S(1)} %copy-done.1, ...), custom_call_target="tpu_custom_call" | custom-call | flops 268435456 | bytes 1048576 | tf_op jit(solution)/shard_map/pallas_call | solution.py:694
  520.2 8.3 %shard_map.315 = (f32[64,8192]{1,0:T(8,128)}, f32[64,8192]{1,0:T(8,128)}, f32[64,8192]{1,0:T(8,128)}) custom-call(f32[64,8192]{1,0:T(8,128)} %weight_ref.10, f32[64,8192]{1,0:T(8,128)} %first_ref.4, f32[64,8192]{1,0:T(8,128)} %second_ref.4, bf16[8,64,1024]{2,1,0:T(8,128)(2,1)} %copy-done.16), custom_call_target="tpu_custom_call" | custom-call | flops 7864320 | bytes 13631488 | tf_op jit(solution)/shard_map/pallas_call | solution.py:382
  537.5 8.7 %multiply_reduce_fusion = (f32[2048]{0:T(1024)S(1)}, bf16[1024,2048]{1,0:T(8,128)(2,1)}) fusion(bf16[1024,2048]{1,0:T(8,128)(2,1)} %copy-done.18, bf16[1024,768]{1,0:T(8,128)(2,1)S(1)} %shard_map.314, bf16[512,768]{1,0:T(8,128)(2,1)} %copy-done.41, bf16[512,768]{1,0:T(8,128)(2,1)} %collective-permute-done.12, bf16[512,768]{1,0:T(8,128)(2,1)} %collective-permute-done.11, ...), kind=kOutput, calls=%fused_computation.13 | convolution fusion | flops 3242194944 | bytes 13115392 | tf_op jit(solution)/shard_map/dot_general | solution.py:69
  571.3 15.6 %shard_map.316 = (f32[64,16384]{1,0:T(8,128)}, f32[64,16384]{1,0:T(8,128)}, f32[64,16384]{1,0:T(8,128)}) custom-call(f32[64,16384]{1,0:T(8,128)} %weight_ref.11, f32[64,16384]{1,0:T(8,128)} %first_ref.5, f32[64,16384]{1,0:T(8,128)} %second_ref.5, bf16[8,64,2048]{2,1,0:T(8,128)(2,1)} %all-to-all-done.5.gradient_ref), custom_call_target="tpu_custom_call" | custom-call | flops 15728640 | bytes 27262976 | tf_op jit(solution)/shard_map/pallas_call | solution.py:382
  592.9 8.7 %collective-permute-done.60 = f32[2,2048]{1,0:T(2,128)S(1)} collective-permute-done((f32[2,2048]{1,0:T(2,128)S(1)}, f32[2,2048]{1,0:T(2,128)S(1)}, u32[]{:S(2)}, u32[]{:S(2)}) %collective-permute-start.60) | collective-permute-done | bytes 16416 | tf_op jit(solution)/shard_map/ppermute | solution.py:91
  615.6 7.4 %collective-permute-done.66 = f32[2,2048]{1,0:T(2,128)S(1)} collective-permute-done((f32[2,2048]{1,0:T(2,128)S(1)}, f32[2,2048]{1,0:T(2,128)S(1)}, u32[]{:S(2)}, u32[]{:S(2)}) %collective-permute-start.66) | collective-permute-done | bytes 16416 | tf_op jit(solution)/shard_map/ppermute | solution.py:91
  626.5 6.4 shard_map.317
  (408 shorter events, 295.6 us)
Async XLA Ops:
  5.1 56.1 %all-to-all-start = ((bf16[8,64,768]{2,1,0:T(8,128)(2,1)}), bf16[8,64,768]{2,1,0:T(8,128)(2,1)}, u32[]{:S(2)}, u32[]{:S(2)}) async-start(bf16[8,64,768]{2,1,0:T(8,128)(2,1)} %shard_map.305), calls=%async_computation | async-start | bytes 1572864 | tf_op jit(solution)/shard_map/all_to_all | solution.py:345
  22.5 23.9 %collective-permute-start.3 = (bf16[128,3072]{1,0:T(8,128)(2,1)S(1)}, bf16[128,3072]{1,0:T(8,128)(2,1)}, u32[]{:S(2)}, u32[]{:S(2)}) collective-permute-start(bf16[128,3072]{1,0:T(8,128)(2,1)S(1)} %maximum_maximum_fusion), channel_id=1, source_target_pairs={{0,8},{8,16},{16,24},{24,28},{28,20},{20,12},{12,4},{4,0},{1,9},{9... | collective-permute-start | bytes 2359304 | tf_op jit(solution)/shard_map/ppermute | solution.py:102
  65.9 59.7 %collective-permute-start.12 = (bf16[512,768]{1,0:T(8,128)(2,1)}, bf16[512,768]{1,0:T(8,128)(2,1)}, u32[]{:S(2)}, u32[]{:S(2)}) collective-permute-start(bf16[512,768]{1,0:T(8,128)(2,1)} %bitcast.5), channel_id=1, source_target_pairs={{0,1},{1,0},{2,3},{3,2},{4,5},{5,4},{6,7},{7,6},{8,9},{9,8},{10,11... | collective-permute-start | bytes 2359304 | tf_op jit(solution)/shard_map/ppermute | solution.py:91
  65.9 49.1 %collective-permute-start.11 = (bf16[512,768]{1,0:T(8,128)(2,1)}, bf16[512,768]{1,0:T(8,128)(2,1)}, u32[]{:S(2)}, u32[]{:S(2)}) collective-permute-start(bf16[512,768]{1,0:T(8,128)(2,1)} %bitcast.5), channel_id=1, source_target_pairs={{0,2},{1,3},{2,0},{3,1},{4,6},{5,7},{6,4},{7,5},{8,10},{9,11},{10,... | collective-permute-start | bytes 2359304 | tf_op jit(solution)/shard_map/ppermute | solution.py:91
  109.8 49.6 %all-to-all-start.1 = ((bf16[8,64,2048]{2,1,0:T(8,128)(2,1)}), bf16[8,64,2048]{2,1,0:T(8,128)(2,1)}, u32[]{:S(2)}, u32[]{:S(2)}) async-start(bf16[8,64,2048]{2,1,0:T(8,128)(2,1)} %shard_map.306), calls=%async_computation.1 | async-start | bytes 4194304 | tf_op jit(solution)/shard_map/all_to_all | solution.py:345
  117.3 69.5 %collective-permute-start.22 = (bf16[2048,512]{1,0:T(8,128)(2,1)}, bf16[2048,512]{1,0:T(8,128)(2,1)}, u32[]{:S(2)}, u32[]{:S(2)}) collective-permute-start(bf16[2048,512]{1,0:T(8,128)(2,1)} %maximum_dynamic-update-slice_fusion.9.refs_3_), channel_id=1, source_target_pairs={{0,2},{1,3},{2,0},{3,1},{4,6},{5,7},{6,4},{7,5},{8,10},{9,11},{10,... | collective-permute-start | bytes 6291464 | tf_op jit(solution)/shard_map/ppermute | solution.py:91
  159.4 51.4 %collective-permute-start.27 = (bf16[512,2048]{1,0:T(8,128)(2,1)}, bf16[512,2048]{1,0:T(8,128)(2,1)}, u32[]{:S(2)}, u32[]{:S(2)}) collective-permute-start(bf16[512,2048]{1,0:T(8,128)(2,1)} %bitcast.12.refs_1_.refs_5_), channel_id=1, source_target_pairs={{0,2},{1,3},{2,0},{3,1},{4,6},{5,7},{6,4},{7,5},{8,10},{9,11},{10,... | collective-permute-start | bytes 6291464 | tf_op jit(solution)/shard_map/ppermute | solution.py:91
  186.8 37.9 %collective-permute-start.23 = (bf16[2048,512]{1,0:T(8,128)(2,1)}, bf16[2048,512]{1,0:T(8,128)(2,1)}, u32[]{:S(2)}, u32[]{:S(2)}) collective-permute-start(bf16[2048,512]{1,0:T(8,128)(2,1)} %maximum_dynamic-update-slice_fusion.9.refs_3_), channel_id=1, source_target_pairs={{0,1},{1,0},{2,3},{3,2},{4,5},{5,4},{6,7},{7,6},{8,9},{9,8},{10,11... | collective-permute-start | bytes 6291464 | tf_op jit(solution)/shard_map/ppermute | solution.py:91
  186.9 37.9 %collective-permute-start.24 = (bf16[2048,512]{1,0:T(8,128)(2,1)}, bf16[2048,512]{1,0:T(8,128)(2,1)}, u32[]{:S(2)}, u32[]{:S(2)}) collective-permute-start(bf16[2048,512]{1,0:T(8,128)(2,1)} %collective-permute-done.22.refs_4_), channel_id=1, source_target_pairs={{0,1},{1,0},{2,3},{3,2},{4,5},{5,4},{6,7},{7,6},{8,9},{9,8},{10,11... | collective-permute-start | bytes 6291464 | tf_op jit(solution)/shard_map/ppermute | solution.py:91
  202.6 47.1 %collective-permute-start.28 = (bf16[512,2048]{1,0:T(8,128)(2,1)}, bf16[512,2048]{1,0:T(8,128)(2,1)}, u32[]{:S(2)}, u32[]{:S(2)}) collective-permute-start(bf16[512,2048]{1,0:T(8,128)(2,1)} %bitcast.12.refs_1_.refs_5_), channel_id=1, source_target_pairs={{0,1},{1,0},{2,3},{3,2},{4,5},{5,4},{6,7},{7,6},{8,9},{9,8},{10,11... | collective-permute-start | bytes 6291464 | tf_op jit(solution)/shard_map/ppermute | solution.py:91
  210.9 38.9 %collective-permute-start.29 = (bf16[512,2048]{1,0:T(8,128)(2,1)}, bf16[512,2048]{1,0:T(8,128)(2,1)}, u32[]{:S(2)}, u32[]{:S(2)}) collective-permute-start(bf16[512,2048]{1,0:T(8,128)(2,1)} %collective-permute-done.27.refs_2_.refs_6_), channel_id=1, source_target_pairs={{0,1},{1,0},{2,3},{3,2},{4,5},{5,4},{6,7},{7,6},{8,9},{9,8},{10,11... | collective-permute-start | bytes 6291464 | tf_op jit(solution)/shard_map/ppermute | solution.py:91
  213.4 32.6 %all-to-all-start.2 = ((bf16[8,64,1024]{2,1,0:T(8,128)(2,1)}), bf16[8,64,1024]{2,1,0:T(8,128)(2,1)S(1)}, u32[]{:S(2)}, u32[]{:S(2)}) async-start(bf16[8,64,1024]{2,1,0:T(8,128)(2,1)} %shard_map.307), calls=%async_computation.2 | async-start | bytes 2097152 | tf_op jit(solution)/shard_map/all_to_all | solution.py:345
  248.0 23.9 %collective-permute-start.34 = (bf16[512,1024]{1,0:T(8,128)(2,1)S(1)}, bf16[512,1024]{1,0:T(8,128)(2,1)S(1)}, u32[]{:S(2)}, u32[]{:S(2)}) collective-permute-start(bf16[512,1024]{1,0:T(8,128)(2,1)S(1)} %bitcast.102), channel_id=1, source_target_pairs={{0,2},{1,3},{2,0},{3,1},{4,6},{5,7},{6,4},{7,5},{8,10},{9,11},{10,... | collective-permute-start | bytes 3145736 | tf_op jit(solution)/shard_map/ppermute | solution.py:91
  266.1 24.4 %collective-permute-start.35 = (bf16[512,1024]{1,0:T(8,128)(2,1)S(1)}, bf16[512,1024]{1,0:T(8,128)(2,1)S(1)}, u32[]{:S(2)}, u32[]{:S(2)}) collective-permute-start(bf16[512,1024]{1,0:T(8,128)(2,1)S(1)} %bitcast.103), channel_id=1, source_target_pairs={{0,1},{1,0},{2,3},{3,2},{4,5},{5,4},{6,7},{7,6},{8,9},{9,8},{10,11... | collective-permute-start | bytes 3145736 | tf_op jit(solution)/shard_map/ppermute | solution.py:91
  303.8 37.6 %collective-permute-start.40 = (bf16[128,2048]{1,0:T(8,128)(2,1)S(1)}, bf16[128,2048]{1,0:T(8,128)(2,1)S(1)}, u32[]{:S(2)}, u32[]{:S(2)}) collective-permute-start(bf16[128,2048]{1,0:T(8,128)(2,1)S(1)} %get-tuple-element.233), channel_id=1, source_target_pairs={{0,4},{8,0},{16,8},{24,16},{28,24},{20,28},{12,20},{4,12},{1,5},{9... | collective-permute-start | bytes 1572872 | tf_op jit(solution)/shard_map/ppermute | solution.py:102
  365.9 30.4 %collective-permute-start.46 = (bf16[1024,2048]{1,0:T(8,128)(2,1)}, bf16[1024,2048]{1,0:T(8,128)(2,1)S(1)}, u32[]{:S(2)}, u32[]{:S(2)}) collective-permute-start(bf16[1024,2048]{1,0:T(8,128)(2,1)} %convolution_convert_fusion), channel_id=1, source_target_pairs={{0,1},{1,0},{2,3},{3,2},{4,5},{5,4},{6,7},{7,6},{8,9},{9,8},{10,11... | collective-permute-start | bytes 12582920 | tf_op jit(solution)/shard_map/ppermute | solution.py:91
  373.6 20.2 %collective-permute-start.43 = (bf16[128,4096]{1,0:T(8,128)(2,1)S(1)}, bf16[128,4096]{1,0:T(8,128)(2,1)S(1)}, u32[]{:S(2)}, u32[]{:S(2)}) collective-permute-start(bf16[128,4096]{1,0:T(8,128)(2,1)S(1)} %add_convert_fusion.3), channel_id=1, source_target_pairs={{0,8},{8,16},{16,24},{24,28},{28,20},{20,12},{12,4},{4,0},{1,9},{9... | collective-permute-start | bytes 3145736 | tf_op jit(solution)/shard_map/ppermute | solution.py:102
  378.7 28.0 %collective-permute-start.49 = (bf16[512,1024]{1,0:T(8,128)(2,1)}, bf16[512,1024]{1,0:T(8,128)(2,1)}, u32[]{:S(2)}, u32[]{:S(2)}) collective-permute-start(bf16[512,1024]{1,0:T(8,128)(2,1)} %fusion.21), channel_id=1, source_target_pairs={{0,2},{1,3},{2,0},{3,1},{4,6},{5,7},{6,4},{7,5},{8,10},{9,11},{10,... | collective-permute-start | bytes 3145736 | tf_op jit(solution)/shard_map/ppermute | solution.py:91
  403.3 25.6 %collective-permute-start.47 = (bf16[128,4096]{1,0:T(8,128)(2,1)}, bf16[128,4096]{1,0:T(8,128)(2,1)}, u32[]{:S(2)}, u32[]{:S(2)}) collective-permute-start(bf16[128,4096]{1,0:T(8,128)(2,1)} %add_convert_fusion.1), channel_id=1, source_target_pairs={{0,8},{8,16},{16,24},{24,28},{28,20},{20,12},{12,4},{4,0},{1,9},{9... | collective-permute-start | bytes 3145736 | tf_op jit(solution)/shard_map/ppermute | solution.py:102
  405.0 27.4 %collective-permute-start.48 = (bf16[128,4096]{1,0:T(8,128)(2,1)}, bf16[128,4096]{1,0:T(8,128)(2,1)}, u32[]{:S(2)}, u32[]{:S(2)}) collective-permute-start(bf16[128,4096]{1,0:T(8,128)(2,1)} %add_convert_fusion), channel_id=1, source_target_pairs={{0,4},{8,0},{16,8},{24,16},{28,24},{20,28},{12,20},{4,12},{1,5},{9... | collective-permute-start | bytes 3145736 | tf_op jit(solution)/shard_map/ppermute | solution.py:102
  411.7 40.4 %all-to-all-start.3 = ((bf16[8,64,1024]{2,1,0:T(8,128)(2,1)}), bf16[8,64,1024]{2,1,0:T(8,128)(2,1)S(1)}, u32[]{:S(2)}, u32[]{:S(2)}) async-start(bf16[8,64,1024]{2,1,0:T(8,128)(2,1)} %bitcast.123), calls=%async_computation.3 | async-start | bytes 2097152 | tf_op jit(solution)/shard_map/all_to_all | solution.py:352
  415.3 47.2 %collective-permute-start.50 = (bf16[512,2048]{1,0:T(8,128)(2,1)}, bf16[512,2048]{1,0:T(8,128)(2,1)}, u32[]{:S(2)}, u32[]{:S(2)}) collective-permute-start(bf16[512,2048]{1,0:T(8,128)(2,1)} %fusion.13), channel_id=1, source_target_pairs={{0,2},{1,3},{2,0},{3,1},{4,6},{5,7},{6,4},{7,5},{8,10},{9,11},{10,... | collective-permute-start | bytes 6291464 | tf_op jit(solution)/shard_map/ppermute | solution.py:91
  452.1 42.5 %all-to-all-start.4 = ((bf16[8,128,512]{1,2,0:T(8,128)(2,1)}), bf16[8,128,512]{1,2,0:T(8,128)(2,1)}, u32[]{:S(2)}, u32[]{:S(2)}) async-start(bf16[8,128,512]{1,2,0:T(8,128)(2,1)} %maximum_bitcast_fusion), calls=%async_computation.4 | async-start | bytes 2097152 | tf_op jit(solution)/shard_map/all_to_all | solution.py:928
  496.2 41.4 %all-to-all-start.5 = ((bf16[8,64,2048]{2,1,0:T(8,128)(2,1)}), bf16[8,64,2048]{2,1,0:T(8,128)(2,1)}, u32[]{:S(2)}, u32[]{:S(2)}) async-start(bf16[8,64,2048]{2,1,0:T(8,128)(2,1)} %bitcast.110), calls=%async_computation.5 | async-start | bytes 4194304 | tf_op jit(solution)/shard_map/all_to_all | solution.py:352
  529.8 21.1 %collective-permute-start.65 = (bf16[1,512,256]{2,1,0:T(8,128)(2,1)S(1)}, bf16[1,512,256]{2,1,0:T(8,128)(2,1)S(1)}, u32[]{:S(2)}, u32[]{:S(2)}) collective-permute-start(bf16[1,512,256]{2,1,0:T(8,128)(2,1)S(1)} %slice_bitcast_fusion.2), channel_id=1, source_target_pairs={{0,2},{1,3},{2,0},{3,1},{4,6},{5,7},{6,4},{7,5},{8,10},{9,11},{10,... | collective-permute-start | bytes 786440 | tf_op jit(solution)/shard_map/ppermute | solution.py:91
  535.7 27.1 %collective-permute-start.63 = (bf16[512,768]{1,0:T(8,128)(2,1)}, bf16[512,768]{1,0:T(8,128)(2,1)}, u32[]{:S(2)}, u32[]{:S(2)}) collective-permute-start(bf16[512,768]{1,0:T(8,128)(2,1)} %fusion.33), channel_id=1, source_target_pairs={{0,2},{1,3},{2,0},{3,1},{4,6},{5,7},{6,4},{7,5},{8,10},{9,11},{10,... | collective-permute-start | bytes 2359304 | tf_op jit(solution)/shard_map/ppermute | solution.py:91
  560.7 26.2 %collective-permute-start.55 = (bf16[128,2048]{1,0:T(8,128)(2,1)}, bf16[128,2048]{1,0:T(8,128)(2,1)S(1)}, u32[]{:S(2)}, u32[]{:S(2)}) collective-permute-start(bf16[128,2048]{1,0:T(8,128)(2,1)} %get-tuple-element.130), channel_id=1, source_target_pairs={{0,8},{8,16},{16,24},{24,28},{28,20},{20,12},{12,4},{4,0},{1,9},{9... | collective-permute-start | bytes 1572872 | tf_op jit(solution)/shard_map/ppermute | solution.py:102
  562.2 24.8 %collective-permute-start.56 = (bf16[128,2048]{1,0:T(8,128)(2,1)}, bf16[128,2048]{1,0:T(8,128)(2,1)}, u32[]{:S(2)}, u32[]{:S(2)}) collective-permute-start(bf16[128,2048]{1,0:T(8,128)(2,1)} %get-tuple-element.131), channel_id=1, source_target_pairs={{0,4},{8,0},{16,8},{24,16},{28,24},{20,28},{12,20},{4,12},{1,5},{9... | collective-permute-start | bytes 1572872 | tf_op jit(solution)/shard_map/ppermute | solution.py:102
  565.3 21.6 %collective-permute-start.57 = (f32[2,2048]{1,0:T(2,128)S(1)}, f32[2,2048]{1,0:T(2,128)S(1)}, u32[]{:S(2)}, u32[]{:S(2)}) collective-permute-start(f32[2,2048]{1,0:T(2,128)S(1)} %add.642), channel_id=1, source_target_pairs={{0,2},{1,3},{2,0},{3,1},{4,6},{5,7},{6,4},{7,5},{8,10},{9,11},{10,... | collective-permute-start | bytes 49160 | tf_op jit(solution)/shard_map/ppermute | solution.py:91
  566.8 56.2 %all-to-all-start.6 = ((bf16[8,64,1024]{2,1,0:T(8,128)(2,1)}), bf16[8,64,1024]{2,1,0:T(8,128)(2,1)S(1)}, u32[]{:S(2)}, u32[]{:S(2)}) async-start(bf16[8,64,1024]{2,1,0:T(8,128)(2,1)} %pad_maximum_fusion.4), calls=%async_computation.6 | async-start | bytes 2097152 | tf_op jit(solution)/shard_map/all_to_all | solution.py:352
  607.5 25.4 %collective-permute-start.61 = (bf16[128,2048]{1,0:T(8,128)(2,1)}, bf16[128,2048]{1,0:T(8,128)(2,1)S(1)}, u32[]{:S(2)}, u32[]{:S(2)}) collective-permute-start(bf16[128,2048]{1,0:T(8,128)(2,1)} %get-tuple-element.140), channel_id=1, source_target_pairs={{0,8},{8,16},{16,24},{24,28},{28,20},{20,12},{12,4},{4,0},{1,9},{9... | collective-permute-start | bytes 1572872 | tf_op jit(solution)/shard_map/ppermute | solution.py:102
  611.8 21.1 %collective-permute-start.62 = (bf16[128,2048]{1,0:T(8,128)(2,1)S(1)}, bf16[128,2048]{1,0:T(8,128)(2,1)S(1)}, u32[]{:S(2)}, u32[]{:S(2)}) collective-permute-start(bf16[128,2048]{1,0:T(8,128)(2,1)S(1)} %get-tuple-element.141), channel_id=1, source_target_pairs={{0,4},{8,0},{16,8},{24,16},{28,24},{20,28},{12,20},{4,12},{1,5},{9... | collective-permute-start | bytes 1572872 | tf_op jit(solution)/shard_map/ppermute | solution.py:102
  (86 other events, 1004.5 us)

commit v4 on v3

--- a/solution.py
+++ b/solution.py
@@ -197,10 +197,11 @@
 def ring_blocks(wholes):
     far = lax.axis_size("seq") // 2
     offsets = [far] + [sign * step for step in range(far - 1, 0, -1) for sign in (1, -1)] + [0]
-    return {
-        offset: jnp.concatenate([ring_rows(whole, [offset]) for whole in wholes], axis=1)
-        for offset in offsets
-    }
+    blocks = {far: jnp.concatenate([ring_rows(whole, [far]) for whole in wholes], axis=1)}
+    wholes = after_all(wholes, (blocks[far],))
+    for offset in offsets[1:]:
+        blocks[offset] = jnp.concatenate([ring_rows(whole, [offset]) for whole in wholes], axis=1)
+    return blocks
 
 
 def butterfly_steps():
@@ -945,7 +946,7 @@
     gain_grad = jnp.stack([gain_one_part / gains_here[0], gain_two_grad])
     gain_grad = from_relative(gain_grad, rows_own)
     down_m, down_s, down_w = adam_by_owner(
-        down_weight, down_first, down_second, down_grad, 1, rate_down
+        down_weight, down_first, down_second, after(down_grad, qkv_sends[-1]), 1, rate_down
     )
     steps = butterfly_steps()
 
@@ -985,7 +986,7 @@
     next_gain_sum()
     sums["rest"] = to_row_owners(jnp.concatenate([after(qkv_own, gate_grad), out_own], axis=1))
     grad_one = ring_scatter_sum(
-        ring_blocks([after(grad_one_part.astype(jnp.bfloat16), qkv_sends[-1], down_m)]),
+        ring_blocks([after(grad_one_part.astype(jnp.bfloat16), qkv_own, down_m)]),
         (gate_update, last_transfer, lambda moved: tied(moved, "gain"), last_updates),
     )
     while steps:

time: 652 us -> 649 us (level)
  matrix products: 67.6 us -> 60.2 us
  starting transfers between devices: 106 us -> 113 us
    ppermute x40, waiting for transfers between devices: 146 us -> 133 us  [ring_shift(): return lax.ppermute(value, 'seq', pairs)]
    ppermute x28, waiting for transfers between devices: 34.6 us -> 44.8 us  [swapped(): lax.ppermute(value, axis, [(source, source ^ bit) for source in range(cou...]
    unnamed x90 -> x94, local copies, waits for them, and re-layouts: 13.6 us -> 16.2 us
  transfers between devices with their start and end apart: 75 -> 75, of which waited for: 35 -> 31; matrix products, arithmetic and copies ran while one was open for 25% -> 23% of each run, Pallas kernels for 19% -> 20%
where the time goes in v4:
time: 649 us; the launch traced here: 639 us
  waiting for transfers between devices  221 us (34%)
  Pallas kernels  135 us (21%)
  starting transfers between devices  113 us (17%)
  local copies, waits for them, and re-layouts  61.1 us (9%)
  matrix products  60.2 us (9%)
  other arithmetic  46.3 us (7%)
    ppermute x40, waiting for transfers between devices, ring_shift(): return lax.ppermute(value, 'seq', pairs)  133 us
    ppermute x40, starting transfers between devices, ring_shift(): return lax.ppermute(value, 'seq', pairs)  48.8 us
    ppermute x28, waiting for transfers between devices, swapped(): lax.ppermute(value, axis, [(source, source ^ bit) for source in range(cou...  44.8 us
    dot_general x10, matrix products, contract_rows(): lax.dot_general(left_side, right_side, (((0,), (0,)), ((), ())), preferre...  39.2 us
    pallas_call x4, Pallas kernels, adam_by_owner(): pl.pallas_call(kernel, grid=(groups, steps), in_specs=[whole] * 3 + [pl.B...  32.8 us
    all_to_all x1, waiting for transfers between devices, on_device(): got = lax.all_to_all(by_owner, 'seq', 0, 0, tiled=True)  24.7 us
    pallas_call x2, Pallas kernels, back_to_model(): pl.pallas_call(lambda *refs: back_kernel(total, *refs), grid=(total * eac...  24.2 us
    pallas_call x3, Pallas kernels, rounded_by_owner(): pl.pallas_call(kernel, grid=(groups, steps), in_specs=[pl.BlockSpec((rows...  19.8 us
  transfers between devices with their start and end apart: 75, of which 31 were waited for; matrix products, arithmetic and copies ran while one was open for 23% of the time, Pallas kernels for 20%

profile of v4, /device:TPU:0, one launch (start us, length us, event | category | flops | bytes accessed | tf_op | source)
XLA Modules:
  0.0 639.3 jit_solution(14881918961531214698)
XLA Ops:
  5.1 7.3 %all-to-all-start = ((bf16[8,64,768]{2,1,0:T(8,128)(2,1)}), bf16[8,64,768]{2,1,0:T(8,128)(2,1)}, u32[]{:S(2)}, u32[]{:S(2)}) async-start(bf16[8,64,768]{2,1,0:T(8,128)(2,1)} %shard_map.305), calls=%async_computation | async-start | bytes 1572864 | tf_op jit(solution)/shard_map/all_to_all | solution.py:346
  27.1 10.0 %shard_map.306 = bf16[8,64,2048]{2,1,0:T(8,128)(2,1)} custom-call(f32[64,16384]{1,0:T(8,128)} %weight_ref.11), custom_call_target="tpu_custom_call" | custom-call | bytes 6291456 | tf_op jit(solution)/shard_map/pallas_call | solution.py:333
  46.2 10.9 %collective-permute-done.3 = bf16[128,3072]{1,0:T(8,128)(2,1)} collective-permute-done((bf16[128,3072]{1,0:T(8,128)(2,1)S(1)}, bf16[128,3072]{1,0:T(8,128)(2,1)}, u32[]{:S(2)}, u32[]{:S(2)}) %collective-permute-start.3) | collective-permute-done | bytes 786464 | tf_op jit(solution)/shard_map/ppermute | solution.py:102
  66.7 12.3 %collective-permute-done.5 = bf16[128,3072]{1,0:T(8,128)(2,1)S(1)} collective-permute-done((bf16[128,3072]{1,0:T(8,128)(2,1)}, bf16[128,3072]{1,0:T(8,128)(2,1)S(1)}, u32[]{:S(2)}, u32[]{:S(2)}) %collective-permute-start.5) | collective-permute-done | bytes 786464 | tf_op jit(solution)/shard_map/ppermute | solution.py:102
  84.4 14.6 %collective-permute-done.8 = bf16[128,3072]{1,0:T(8,128)(2,1)S(1)} collective-permute-done((bf16[128,3072]{1,0:T(8,128)(2,1)S(1)}, bf16[128,3072]{1,0:T(8,128)(2,1)S(1)}, u32[]{:S(2)}, u32[]{:S(2)}) %collective-permute-start.8) | collective-permute-done | bytes 786464 | tf_op jit(solution)/shard_map/ppermute | solution.py:102
  123.7 8.4 %fusion.56.query_in.key_in.value_in = f32[1024,768]{1,0:T(8,128)} fusion(bf16[1024,2048]{1,0:T(8,128)(2,1)S(1)} %fusion.2, bf16[512,768]{1,0:T(8,128)(2,1)S(1)} %collective-permute-done.13, bf16[512,768]{1,0:T(8,128)(2,1)} %collective-permute-done.12, bf16[512,768]{1,0:T(8,128)(2,1)} %collective-permute-done.11, bf16[512,768]{1,0:T(8,128)(2,1)} %bitcast.5), kind=kOutput, calls=%fused_computation.86 | convolution fusion | flops 3233808384 | bytes 10485760 | tf_op jit(solution)/shard_map/dot_general | solution.py:75
  132.2 8.7 %shard_map.308 = (f32[1024,256]{1,0:T(8,128)S(1)}, bf16[1024,256]{1,0:T(8,128)(2,1)S(1)}, bf16[1024,256]{1,0:T(8,128)(2,1)S(1)}, bf16[1024,256]{1,0:T(8,128)(2,1...) custom-call(f32[1024,768]{1,0:T(8,128)} %fusion.56.query_in.key_in.value_in, ...), custom_call_target="tpu_custom_call" | custom-call | flops 2147483648 | bytes 6291456 | tf_op jit(solution)/shard_map/pallas_call | solution.py:658
  143.4 13.8 %all-to-all-done.1 = bf16[8,64,2048]{2,1,0:T(8,128)(2,1)} async-done(((bf16[8,64,2048]{2,1,0:T(8,128)(2,1)}), bf16[8,64,2048]{2,1,0:T(8,128)(2,1)}, u32[]{:S(2)}, u32[]{:S(2)}) %all-to-all-start.1) | async-done | bytes 2097184 | tf_op jit(solution)/shard_map/all_to_all | solution.py:346
  161.4 8.4 %collective-permute-done.15 = bf16[1024,256]{1,0:T(8,128)(2,1)S(1)} collective-permute-done((bf16[1024,256]{1,0:T(8,128)(2,1)S(1)}, bf16[1024,256]{1,0:T(8,128)(2,1)S(1)}, u32[]{:S(2)}, u32[]{:S(2)}) %collective-permute-start.15) | collective-permute-done | bytes 524320 | tf_op jit(solution)/shard_map/ppermute | solution.py:102
  172.0 9.5 %collective-permute-done.17 = bf16[1024,256]{1,0:T(8,128)(2,1)S(1)} collective-permute-done((bf16[1024,256]{1,0:T(8,128)(2,1)S(1)}, bf16[1024,256]{1,0:T(8,128)(2,1)S(1)}, u32[]{:S(2)}, u32[]{:S(2)}) %collective-permute-start.17) | collective-permute-done | bytes 524320 | tf_op jit(solution)/shard_map/ppermute | solution.py:102
  199.5 9.6 %collective-permute-done.27.refs_2_.refs_6_ = bf16[512,2048]{1,0:T(8,128)(2,1)} collective-permute-done((bf16[512,2048]{1,0:T(8,128)(2,1)}, bf16[512,2048]{1,0:T(8,128)(2,1)}, u32[]{:S(2)}, u32[]{:S(2)}) %collective-permute-start.27) | collective-permute-done | bytes 2097184 | tf_op jit(solution)/shard_map/ppermute | solution.py:91
  223.0 15.9 %shard_map.309 = (f32[1024,2048]{1,0:T(8,128)}, bf16[1024,2048]{1,0:T(8,128)(2,1)}) custom-call(bf16[1024,2048]{1,0:T(8,128)(2,1)} %maximum_dynamic-update-slice_fusion.refs_0_, bf16[1024,2048]{1,0:T(8,128)(2,1)} %fusion.59.refs_1_, f32[1,2048]{1,0:T(1,128)S(1)} %get-tuple-element.308.refs_2_, bf16[2048,512]{1,0:T(8,128)(2,1)} %maximum_dynamic-update-slice_fusion.9.refs_3_, ...), custom_call_target="tpu_custom_call" | custom-call | flops 8589934592 | bytes 29360128 | tf_op jit(solution)/shard_map/pallas_call | solution.py:519
  247.8 14.3 %shard_map.310 = (f32[1024,1024]{1,0:T(8,128)}, f32[1024,1024]{1,0:T(8,128)}, bf16[1024,1024]{1,0:T(8,128)(2,1)S(1)}) custom-call(bf16[1024,2048]{1,0:T(8,128)(2,1)} %get-tuple-element.105.refs_0_, bf16[512,2048]{1,0:T(8,128)(2,1)} %bitcast.12.refs_1_.refs_5_, bf16[512,2048]{1,0:T(8,128)(2,1)} %collective-permute-done.27.refs_2_.refs_6_, ...), custom_call_target="tpu_custom_call" | custom-call | flops 8589934592 | bytes 23068672 | tf_op jit(solution)/shard_map/pallas_call | solution.py:563
  277.1 9.4 %collective-permute-done.32 = bf16[128,2048]{1,0:T(8,128)(2,1)S(1)} collective-permute-done((bf16[128,2048]{1,0:T(8,128)(2,1)S(1)}, bf16[128,2048]{1,0:T(8,128)(2,1)S(1)}, u32[]{:S(2)}, u32[]{:S(2)}) %collective-permute-start.32) | collective-permute-done | bytes 524320 | tf_op jit(solution)/shard_map/ppermute | solution.py:102
  286.6 8.8 %shard_map.311 = bf16[1024,2048]{1,0:T(8,128)(2,1)} custom-call(bf16[1024,1024]{1,0:T(8,128)(2,1)} %copy-done.6, bf16[512,1024]{1,0:T(8,128)(2,1)S(1)} %bitcast.104, bf16[512,1024]{1,0:T(8,128)(2,1)S(1)} %collective-permute-done.34.refs_2_.refs_4_, bf16[512,1024]{1,0:T(8,128)(2,1)S(1)} %collective-permute-done.35.refs_3_.refs_5_, ...), custom_call_target="tpu_custom_call" | custom-call | flops 4294967296 | bytes 10485760 | tf_op jit(solution)/shard_map/pallas_call | solution.py:635
  306.2 11.1 %shard_map.312.refs_0_ = bf16[1024,2048]{1,0:T(8,128)(2,1)} custom-call(bf16[1024,2048]{1,0:T(8,128)(2,1)} %copy-done.10, f32[1024,1024]{1,0:T(8,128)} %get-tuple-element.114.refs_1_, f32[1024,1024]{1,0:T(8,128)} %get-tuple-element.115.refs_2_, bf16[512,1024]{1,0:T(8,128)(2,1)S(1)} %bitcast.105, ...), custom_call_target="tpu_custom_call" | custom-call | flops 4294967296 | bytes 20971520 | tf_op jit(solution)/shard_map/pallas_call | solution.py:600
  317.2 15.4 %shard_map.313 = bf16[1024,2048]{1,0:T(8,128)(2,1)} custom-call(bf16[1024,2048]{1,0:T(8,128)(2,1)} %shard_map.312.refs_0_, bf16[512,2048]{1,0:T(8,128)(2,1)} %bitcast.12.refs_1_.refs_5_, bf16[512,2048]{1,0:T(8,128)(2,1)} %collective-permute-done.27.refs_2_.refs_6_, bf16[512,2048]{1,0:T(8,128)(2,1)} %collective-permute-done.28.refs_3_.refs_7_, ...), custom_call_target="tpu_custom_call" | custom-call | flops 8589934592 | bytes 16777216 | tf_op jit(solution)/shard_map/pallas_call | solution.py:635
  339.3 8.0 %collective-permute-done.39 = bf16[128,2048]{1,0:T(8,128)(2,1)S(1)} collective-permute-done((bf16[128,2048]{1,0:T(8,128)(2,1)S(1)}, bf16[128,2048]{1,0:T(8,128)(2,1)S(1)}, u32[]{:S(2)}, u32[]{:S(2)}) %collective-permute-start.39) | collective-permute-done | bytes 524320 | tf_op jit(solution)/shard_map/ppermute | solution.py:102
  358.1 11.8 %collective-permute-done.41 = bf16[128,4096]{1,0:T(8,128)(2,1)S(1)} collective-permute-done((bf16[128,4096]{1,0:T(8,128)(2,1)S(1)}, bf16[128,4096]{1,0:T(8,128)(2,1)S(1)}, u32[]{:S(2)}, u32[]{:S(2)}) %collective-permute-start.41) | collective-permute-done | bytes 1048608 | tf_op jit(solution)/shard_map/ppermute | solution.py:102
  376.5 11.5 %collective-permute-done.43 = bf16[128,4096]{1,0:T(8,128)(2,1)S(1)} collective-permute-done((bf16[128,4096]{1,0:T(8,128)(2,1)S(1)}, bf16[128,4096]{1,0:T(8,128)(2,1)S(1)}, u32[]{:S(2)}, u32[]{:S(2)}) %collective-permute-start.43) | collective-permute-done | bytes 1048608 | tf_op jit(solution)/shard_map/ppermute | solution.py:102
  411.4 11.9 %collective-permute-done.48 = bf16[128,4096]{1,0:T(8,128)(2,1)} collective-permute-done((bf16[128,4096]{1,0:T(8,128)(2,1)}, bf16[128,4096]{1,0:T(8,128)(2,1)}, u32[]{:S(2)}, u32[]{:S(2)}) %collective-permute-start.48) | collective-permute-done | bytes 1048608 | tf_op jit(solution)/shard_map/ppermute | solution.py:102
  446.1 12.9 %all-to-all-start.4 = ((bf16[8,128,512]{1,2,0:T(8,128)(2,1)}), bf16[8,128,512]{1,2,0:T(8,128)(2,1)}, u32[]{:S(2)}, u32[]{:S(2)}) async-start(bf16[8,128,512]{1,2,0:T(8,128)(2,1)} %maximum_bitcast_fusion), calls=%async_computation.4 | async-start | bytes 2097152 | tf_op jit(solution)/shard_map/all_to_all | solution.py:929
  458.9 8.2 %fusion.12 = bf16[512,2048]{1,0:T(8,128)(2,1)} fusion(f32[1024,2048]{1,0:T(8,128)} %copy-done.9, bf16[512,2048]{1,0:T(8,128)(2,1)} %collective-permute-done.50, bf16[1024,2048]{1,0:T(8,128)(2,1)} %shard_map.312.refs_0_, bf16[1024,2048]{1,0:T(8,128)(2,1)} %get-tuple-element.105.refs_0_), kind=kOutput, calls=%fused_computation.16 | convolution fusion | flops 2151677952 | bytes 13631488 | tf_op jit(solution)/shard_map/dot_general | solution.py:63
  467.2 24.7 %all-to-all-done.4 = bf16[8,128,512]{1,2,0:T(8,128)(2,1)} async-done(((bf16[8,128,512]{1,2,0:T(8,128)(2,1)}), bf16[8,128,512]{1,2,0:T(8,128)(2,1)}, u32[]{:S(2)}, u32[]{:S(2)}) %all-to-all-start.4) | async-done | bytes 1048608 | tf_op jit(solution)/shard_map/all_to_all | solution.py:929
  501.3 8.4 %shard_map.314 = bf16[1024,768]{1,0:T(8,128)(2,1)S(1)} custom-call(bf16[1024,256]{1,0:T(8,128)(2,1)S(1)} %get-tuple-element.126.query_ref, bf16[1024,256]{1,0:T(8,128)(2,1)S(1)} %copy-done.3, bf16[1024,256]{1,0:T(8,128)(2,1)S(1)} %copy-done.5, bf16[1024,256]{1,0:T(8,128)(2,1)S(1)} %slice.390.grad_ref, f32[1024,256]{1,0:T(8,128)S(1)} %copy-done.1, ...), custom_call_target="tpu_custom_call" | custom-call | flops 268435456 | bytes 1048576 | tf_op jit(solution)/shard_map/pallas_call | solution.py:695
  521.7 8.3 %shard_map.315 = (f32[64,8192]{1,0:T(8,128)}, f32[64,8192]{1,0:T(8,128)}, f32[64,8192]{1,0:T(8,128)}) custom-call(f32[64,8192]{1,0:T(8,128)} %weight_ref.10, f32[64,8192]{1,0:T(8,128)} %first_ref.4, f32[64,8192]{1,0:T(8,128)} %second_ref.4, bf16[8,64,1024]{2,1,0:T(8,128)(2,1)} %copy-done.17), custom_call_target="tpu_custom_call" | custom-call | flops 7864320 | bytes 13631488 | tf_op jit(solution)/shard_map/pallas_call | solution.py:383
  530.0 9.1 %collective-permute-done.52 = bf16[512,768]{1,0:T(8,128)(2,1)} collective-permute-done((bf16[512,768]{1,0:T(8,128)(2,1)}, bf16[512,768]{1,0:T(8,128)(2,1)}, u32[]{:S(2)}, u32[]{:S(2)}) %collective-permute-start.52) | collective-permute-done | bytes 786464 | tf_op jit(solution)/shard_map/ppermute | solution.py:91
  542.1 6.7 %multiply_reduce_fusion = (f32[2048]{0:T(1024)S(1)}, bf16[1024,2048]{1,0:T(8,128)(2,1)S(1)}) fusion(bf16[1024,2048]{1,0:T(8,128)(2,1)} %copy-done.21, bf16[1024,768]{1,0:T(8,128)(2,1)S(1)} %shard_map.314, bf16[512,768]{1,0:T(8,128)(2,1)} %copy-done.43, bf16[512,768]{1,0:T(8,128)(2,1)} %collective-permute-done.12, ...), kind=kOutput, calls=%fused_computation.13 | convolution fusion | flops 3242194944 | bytes 13115392 | tf_op jit(solution)/shard_map/dot_general | solution.py:69
  569.0 15.6 %shard_map.316 = (f32[64,16384]{1,0:T(8,128)}, f32[64,16384]{1,0:T(8,128)}, f32[64,16384]{1,0:T(8,128)}) custom-call(f32[64,16384]{1,0:T(8,128)} %weight_ref.11, f32[64,16384]{1,0:T(8,128)} %first_ref.5, f32[64,16384]{1,0:T(8,128)} %second_ref.5, bf16[8,64,2048]{2,1,0:T(8,128)(2,1)} %all-to-all-done.5.gradient_ref), custom_call_target="tpu_custom_call" | custom-call | flops 15728640 | bytes 27262976 | tf_op jit(solution)/shard_map/pallas_call | solution.py:383
  590.5 10.5 %collective-permute-done.61 = f32[2,2048]{1,0:T(2,128)S(1)} collective-permute-done((f32[2,2048]{1,0:T(2,128)S(1)}, f32[2,2048]{1,0:T(2,128)S(1)}, u32[]{:S(2)}, u32[]{:S(2)}) %collective-permute-start.61) | collective-permute-done | bytes 16416 | tf_op jit(solution)/shard_map/ppermute | solution.py:91
  612.2 7.4 %collective-permute-done.66 = f32[2,2048]{1,0:T(2,128)S(1)} collective-permute-done((f32[2,2048]{1,0:T(2,128)S(1)}, f32[2,2048]{1,0:T(2,128)S(1)}, u32[]{:S(2)}, u32[]{:S(2)}) %collective-permute-start.66) | collective-permute-done | bytes 16416 | tf_op jit(solution)/shard_map/ppermute | solution.py:91
  623.2 6.4 %shard_map.317 = (f32[64,6144]{1,0:T(8,128)}, f32[64,6144]{1,0:T(8,128)}, f32[64,6144]{1,0:T(8,128)}) custom-call(f32[64,6144]{1,0:T(8,128)} %weight_ref.12, f32[64,6144]{1,0:T(8,128)} %first_ref.6, f32[64,6144]{1,0:T(8,128)} %second_ref.6, bf16[8,64,1024]{2,1,0:T(8,128)(2,1)} %copy-done.14), custom_call_target="tpu_custom_call" | custom-call | flops 5898240 | bytes 10223616 | tf_op jit(solution)/shard_map/pallas_call | solution.py:383
  (415 shorter events, 286.9 us)
Async XLA Ops:
  5.1 55.3 %all-to-all-start = ((bf16[8,64,768]{2,1,0:T(8,128)(2,1)}), bf16[8,64,768]{2,1,0:T(8,128)(2,1)}, u32[]{:S(2)}, u32[]{:S(2)}) async-start(bf16[8,64,768]{2,1,0:T(8,128)(2,1)} %shard_map.305), calls=%async_computation | async-start | bytes 1572864 | tf_op jit(solution)/shard_map/all_to_all | solution.py:346
  16.6 20.4 %collective-permute-start.1 = (bf16[64,512]{1,0:T(8,128)(2,1)S(1)}, bf16[64,512]{1,0:T(8,128)(2,1)S(1)}, u32[]{:S(2)}, u32[]{:S(2)}) collective-permute-start(bf16[64,512]{1,0:T(8,128)(2,1)S(1)} %get-tuple-element.297), channel_id=1, source_target_pairs={{0,2},{1,3},{2,0},{3,1},{4,6},{5,7},{6,4},{7,5},{8,10},{9,11},{10,... | collective-permute-start | bytes 196616 | tf_op jit(solution)/shard_map/ppermute | solution.py:91
  65.2 48.4 %collective-permute-start.11 = (bf16[512,768]{1,0:T(8,128)(2,1)}, bf16[512,768]{1,0:T(8,128)(2,1)}, u32[]{:S(2)}, u32[]{:S(2)}) collective-permute-start(bf16[512,768]{1,0:T(8,128)(2,1)} %bitcast.5), channel_id=1, source_target_pairs={{0,2},{1,3},{2,0},{3,1},{4,6},{5,7},{6,4},{7,5},{8,10},{9,11},{10,... | collective-permute-start | bytes 2359304 | tf_op jit(solution)/shard_map/ppermute | solution.py:91
  66.6 57.0 %collective-permute-start.12 = (bf16[512,768]{1,0:T(8,128)(2,1)}, bf16[512,768]{1,0:T(8,128)(2,1)}, u32[]{:S(2)}, u32[]{:S(2)}) collective-permute-start(bf16[512,768]{1,0:T(8,128)(2,1)} %bitcast.5), channel_id=1, source_target_pairs={{0,1},{1,0},{2,3},{3,2},{4,5},{5,4},{6,7},{7,6},{8,9},{9,8},{10,11... | collective-permute-start | bytes 2359304 | tf_op jit(solution)/shard_map/ppermute | solution.py:91
  108.3 48.9 %all-to-all-start.1 = ((bf16[8,64,2048]{2,1,0:T(8,128)(2,1)}), bf16[8,64,2048]{2,1,0:T(8,128)(2,1)}, u32[]{:S(2)}, u32[]{:S(2)}) async-start(bf16[8,64,2048]{2,1,0:T(8,128)(2,1)} %shard_map.306), calls=%async_computation.1 | async-start | bytes 4194304 | tf_op jit(solution)/shard_map/all_to_all | solution.py:346
  115.9 68.1 %collective-permute-start.22 = (bf16[2048,512]{1,0:T(8,128)(2,1)}, bf16[2048,512]{1,0:T(8,128)(2,1)}, u32[]{:S(2)}, u32[]{:S(2)}) collective-permute-start(bf16[2048,512]{1,0:T(8,128)(2,1)} %maximum_dynamic-update-slice_fusion.9.refs_3_), channel_id=1, source_target_pairs={{0,2},{1,3},{2,0},{3,1},{4,6},{5,7},{6,4},{7,5},{8,10},{9,11},{10,... | collective-permute-start | bytes 6291464 | tf_op jit(solution)/shard_map/ppermute | solution.py:91
  157.3 51.9 %collective-permute-start.27 = (bf16[512,2048]{1,0:T(8,128)(2,1)}, bf16[512,2048]{1,0:T(8,128)(2,1)}, u32[]{:S(2)}, u32[]{:S(2)}) collective-permute-start(bf16[512,2048]{1,0:T(8,128)(2,1)} %bitcast.12.refs_1_.refs_5_), channel_id=1, source_target_pairs={{0,2},{1,3},{2,0},{3,1},{4,6},{5,7},{6,4},{7,5},{8,10},{9,11},{10,... | collective-permute-start | bytes 6291464 | tf_op jit(solution)/shard_map/ppermute | solution.py:91
  183.9 39.1 %collective-permute-start.23 = (bf16[2048,512]{1,0:T(8,128)(2,1)}, bf16[2048,512]{1,0:T(8,128)(2,1)}, u32[]{:S(2)}, u32[]{:S(2)}) collective-permute-start(bf16[2048,512]{1,0:T(8,128)(2,1)} %maximum_dynamic-update-slice_fusion.9.refs_3_), channel_id=1, source_target_pairs={{0,1},{1,0},{2,3},{3,2},{4,5},{5,4},{6,7},{7,6},{8,9},{9,8},{10,11... | collective-permute-start | bytes 6291464 | tf_op jit(solution)/shard_map/ppermute | solution.py:91
  183.9 39.1 %collective-permute-start.24 = (bf16[2048,512]{1,0:T(8,128)(2,1)}, bf16[2048,512]{1,0:T(8,128)(2,1)}, u32[]{:S(2)}, u32[]{:S(2)}) collective-permute-start(bf16[2048,512]{1,0:T(8,128)(2,1)} %collective-permute-done.22.refs_4_), channel_id=1, source_target_pairs={{0,1},{1,0},{2,3},{3,2},{4,5},{5,4},{6,7},{7,6},{8,9},{9,8},{10,11... | collective-permute-start | bytes 6291464 | tf_op jit(solution)/shard_map/ppermute | solution.py:91
  199.5 48.3 %collective-permute-start.28 = (bf16[512,2048]{1,0:T(8,128)(2,1)}, bf16[512,2048]{1,0:T(8,128)(2,1)}, u32[]{:S(2)}, u32[]{:S(2)}) collective-permute-start(bf16[512,2048]{1,0:T(8,128)(2,1)} %bitcast.12.refs_1_.refs_5_), channel_id=1, source_target_pairs={{0,1},{1,0},{2,3},{3,2},{4,5},{5,4},{6,7},{7,6},{8,9},{9,8},{10,11... | collective-permute-start | bytes 6291464 | tf_op jit(solution)/shard_map/ppermute | solution.py:91
  209.2 38.6 %collective-permute-start.29 = (bf16[512,2048]{1,0:T(8,128)(2,1)}, bf16[512,2048]{1,0:T(8,128)(2,1)}, u32[]{:S(2)}, u32[]{:S(2)}) collective-permute-start(bf16[512,2048]{1,0:T(8,128)(2,1)} %collective-permute-done.27.refs_2_.refs_6_), channel_id=1, source_target_pairs={{0,1},{1,0},{2,3},{3,2},{4,5},{5,4},{6,7},{7,6},{8,9},{9,8},{10,11... | collective-permute-start | bytes 6291464 | tf_op jit(solution)/shard_map/ppermute | solution.py:91
  211.7 32.6 %all-to-all-start.2 = ((bf16[8,64,1024]{2,1,0:T(8,128)(2,1)}), bf16[8,64,1024]{2,1,0:T(8,128)(2,1)S(1)}, u32[]{:S(2)}, u32[]{:S(2)}) async-start(bf16[8,64,1024]{2,1,0:T(8,128)(2,1)} %shard_map.307), calls=%async_computation.2 | async-start | bytes 2097152 | tf_op jit(solution)/shard_map/all_to_all | solution.py:346
  246.3 23.9 %collective-permute-start.34 = (bf16[512,1024]{1,0:T(8,128)(2,1)S(1)}, bf16[512,1024]{1,0:T(8,128)(2,1)S(1)}, u32[]{:S(2)}, u32[]{:S(2)}) collective-permute-start(bf16[512,1024]{1,0:T(8,128)(2,1)S(1)} %bitcast.102), channel_id=1, source_target_pairs={{0,2},{1,3},{2,0},{3,1},{4,6},{5,7},{6,4},{7,5},{8,10},{9,11},{10,... | collective-permute-start | bytes 3145736 | tf_op jit(solution)/shard_map/ppermute | solution.py:91
  264.2 22.3 %collective-permute-start.35 = (bf16[512,1024]{1,0:T(8,128)(2,1)S(1)}, bf16[512,1024]{1,0:T(8,128)(2,1)S(1)}, u32[]{:S(2)}, u32[]{:S(2)}) collective-permute-start(bf16[512,1024]{1,0:T(8,128)(2,1)S(1)} %bitcast.103), channel_id=1, source_target_pairs={{0,1},{1,0},{2,3},{3,2},{4,5},{5,4},{6,7},{7,6},{8,9},{9,8},{10,11... | collective-permute-start | bytes 3145736 | tf_op jit(solution)/shard_map/ppermute | solution.py:91
  299.7 38.0 %collective-permute-start.40 = (bf16[128,2048]{1,0:T(8,128)(2,1)}, bf16[128,2048]{1,0:T(8,128)(2,1)}, u32[]{:S(2)}, u32[]{:S(2)}) collective-permute-start(bf16[128,2048]{1,0:T(8,128)(2,1)} %constant_dynamic-slice_fusion.7), channel_id=1, source_target_pairs={{0,4},{8,0},{16,8},{24,16},{28,24},{20,28},{12,20},{4,12},{1,5},{9... | collective-permute-start | bytes 1572872 | tf_op jit(solution)/shard_map/ppermute | solution.py:102
  347.6 22.4 %collective-permute-start.41 = (bf16[128,4096]{1,0:T(8,128)(2,1)S(1)}, bf16[128,4096]{1,0:T(8,128)(2,1)S(1)}, u32[]{:S(2)}, u32[]{:S(2)}) collective-permute-start(bf16[128,4096]{1,0:T(8,128)(2,1)S(1)} %pad_maximum_fusion.1), channel_id=1, source_target_pairs={{0,8},{8,16},{16,24},{24,28},{28,20},{20,12},{12,4},{4,0},{1,9},{9... | collective-permute-start | bytes 3145736 | tf_op jit(solution)/shard_map/ppermute | solution.py:102
  357.6 32.9 %collective-permute-start.46 = (bf16[1024,2048]{1,0:T(8,128)(2,1)S(1)}, bf16[1024,2048]{1,0:T(8,128)(2,1)S(1)}, u32[]{:S(2)}, u32[]{:S(2)}) collective-permute-start(bf16[1024,2048]{1,0:T(8,128)(2,1)S(1)} %convolution_convert_fusion), channel_id=1, source_target_pairs={{0,1},{1,0},{2,3},{3,2},{4,5},{5,4},{6,7},{7,6},{8,9},{9,8},{10,11... | collective-permute-start | bytes 12582920 | tf_op jit(solution)/shard_map/ppermute | solution.py:91
  376.0 25.2 %collective-permute-start.49 = (bf16[512,1024]{1,0:T(8,128)(2,1)}, bf16[512,1024]{1,0:T(8,128)(2,1)}, u32[]{:S(2)}, u32[]{:S(2)}) collective-permute-start(bf16[512,1024]{1,0:T(8,128)(2,1)} %fusion.21), channel_id=1, source_target_pairs={{0,2},{1,3},{2,0},{3,1},{4,6},{5,7},{6,4},{7,5},{8,10},{9,11},{10,... | collective-permute-start | bytes 3145736 | tf_op jit(solution)/shard_map/ppermute | solution.py:91
  397.5 25.8 %collective-permute-start.48 = (bf16[128,4096]{1,0:T(8,128)(2,1)}, bf16[128,4096]{1,0:T(8,128)(2,1)}, u32[]{:S(2)}, u32[]{:S(2)}) collective-permute-start(bf16[128,4096]{1,0:T(8,128)(2,1)} %add_convert_fusion), channel_id=1, source_target_pairs={{0,4},{8,0},{16,8},{24,16},{28,24},{20,28},{12,20},{4,12},{1,5},{9... | collective-permute-start | bytes 3145736 | tf_op jit(solution)/shard_map/ppermute | solution.py:102
  398.9 24.4 %collective-permute-start.47 = (bf16[128,4096]{1,0:T(8,128)(2,1)}, bf16[128,4096]{1,0:T(8,128)(2,1)}, u32[]{:S(2)}, u32[]{:S(2)}) collective-permute-start(bf16[128,4096]{1,0:T(8,128)(2,1)} %add_convert_fusion.1), channel_id=1, source_target_pairs={{0,8},{8,16},{16,24},{24,28},{28,20},{20,12},{12,4},{4,0},{1,9},{9... | collective-permute-start | bytes 3145736 | tf_op jit(solution)/shard_map/ppermute | solution.py:102
  406.3 39.8 %all-to-all-start.3 = ((bf16[8,64,1024]{2,1,0:T(8,128)(2,1)}), bf16[8,64,1024]{2,1,0:T(8,128)(2,1)S(1)}, u32[]{:S(2)}, u32[]{:S(2)}) async-start(bf16[8,64,1024]{2,1,0:T(8,128)(2,1)} %bitcast.123), calls=%async_computation.3 | async-start | bytes 2097152 | tf_op jit(solution)/shard_map/all_to_all | solution.py:353
  410.8 48.1 %collective-permute-start.50 = (bf16[512,2048]{1,0:T(8,128)(2,1)}, bf16[512,2048]{1,0:T(8,128)(2,1)}, u32[]{:S(2)}, u32[]{:S(2)}) collective-permute-start(bf16[512,2048]{1,0:T(8,128)(2,1)} %fusion.13), channel_id=1, source_target_pairs={{0,2},{1,3},{2,0},{3,1},{4,6},{5,7},{6,4},{7,5},{8,10},{9,11},{10,... | collective-permute-start | bytes 6291464 | tf_op jit(solution)/shard_map/ppermute | solution.py:91
  446.1 45.8 %all-to-all-start.4 = ((bf16[8,128,512]{1,2,0:T(8,128)(2,1)}), bf16[8,128,512]{1,2,0:T(8,128)(2,1)}, u32[]{:S(2)}, u32[]{:S(2)}) async-start(bf16[8,128,512]{1,2,0:T(8,128)(2,1)} %maximum_bitcast_fusion), calls=%async_computation.4 | async-start | bytes 2097152 | tf_op jit(solution)/shard_map/all_to_all | solution.py:929
  493.3 48.8 %all-to-all-start.5 = ((bf16[8,64,2048]{2,1,0:T(8,128)(2,1)}), bf16[8,64,2048]{2,1,0:T(8,128)(2,1)}, u32[]{:S(2)}, u32[]{:S(2)}) async-start(bf16[8,64,2048]{2,1,0:T(8,128)(2,1)} %bitcast.110), calls=%async_computation.5 | async-start | bytes 4194304 | tf_op jit(solution)/shard_map/all_to_all | solution.py:353
  518.4 20.7 %collective-permute-start.52 = (bf16[512,768]{1,0:T(8,128)(2,1)}, bf16[512,768]{1,0:T(8,128)(2,1)}, u32[]{:S(2)}, u32[]{:S(2)}) collective-permute-start(bf16[512,768]{1,0:T(8,128)(2,1)} %fusion.31), channel_id=1, source_target_pairs={{0,2},{1,3},{2,0},{3,1},{4,6},{5,7},{6,4},{7,5},{8,10},{9,11},{10,... | collective-permute-start | bytes 2359304 | tf_op jit(solution)/shard_map/ppermute | solution.py:91
  520.1 42.5 %collective-permute-start.65 = (bf16[1,512,256]{2,1,0:T(8,128)(2,1)S(1)}, bf16[1,512,256]{2,1,0:T(8,128)(2,1)S(1)}, u32[]{:S(2)}, u32[]{:S(2)}) collective-permute-start(bf16[1,512,256]{2,1,0:T(8,128)(2,1)S(1)} %slice_bitcast_fusion.2), channel_id=1, source_target_pairs={{0,2},{1,3},{2,0},{3,1},{4,6},{5,7},{6,4},{7,5},{8,10},{9,11},{10,... | collective-permute-start | bytes 786440 | tf_op jit(solution)/shard_map/ppermute | solution.py:91
  560.6 24.1 %collective-permute-start.57 = (bf16[128,2048]{1,0:T(8,128)(2,1)S(1)}, bf16[128,2048]{1,0:T(8,128)(2,1)S(1)}, u32[]{:S(2)}, u32[]{:S(2)}) collective-permute-start(bf16[128,2048]{1,0:T(8,128)(2,1)S(1)} %get-tuple-element.139), channel_id=1, source_target_pairs={{0,4},{8,0},{16,8},{24,16},{28,24},{20,28},{12,20},{4,12},{1,5},{9... | collective-permute-start | bytes 1572872 | tf_op jit(solution)/shard_map/ppermute | solution.py:102
  562.1 22.6 %collective-permute-start.56 = (bf16[128,2048]{1,0:T(8,128)(2,1)S(1)}, bf16[128,2048]{1,0:T(8,128)(2,1)}, u32[]{:S(2)}, u32[]{:S(2)}) collective-permute-start(bf16[128,2048]{1,0:T(8,128)(2,1)S(1)} %get-tuple-element.138), channel_id=1, source_target_pairs={{0,8},{8,16},{16,24},{24,28},{28,20},{20,12},{12,4},{4,0},{1,9},{9... | collective-permute-start | bytes 1572872 | tf_op jit(solution)/shard_map/ppermute | solution.py:102
  562.7 21.9 %collective-permute-start.58 = (f32[2,2048]{1,0:T(2,128)S(1)}, f32[2,2048]{1,0:T(2,128)S(1)}, u32[]{:S(2)}, u32[]{:S(2)}) collective-permute-start(f32[2,2048]{1,0:T(2,128)S(1)} %add.644), channel_id=1, source_target_pairs={{0,2},{1,3},{2,0},{3,1},{4,6},{5,7},{6,4},{7,5},{8,10},{9,11},{10,... | collective-permute-start | bytes 49160 | tf_op jit(solution)/shard_map/ppermute | solution.py:91
  564.4 55.2 %all-to-all-start.6 = ((bf16[8,64,1024]{2,1,0:T(8,128)(2,1)}), bf16[8,64,1024]{2,1,0:T(8,128)(2,1)S(1)}, u32[]{:S(2)}, u32[]{:S(2)}) async-start(bf16[8,64,1024]{2,1,0:T(8,128)(2,1)} %pad_maximum_fusion.4), calls=%async_computation.6 | async-start | bytes 2097152 | tf_op jit(solution)/shard_map/all_to_all | solution.py:353
  603.4 26.1 %collective-permute-start.62 = (bf16[128,2048]{1,0:T(8,128)(2,1)}, bf16[128,2048]{1,0:T(8,128)(2,1)S(1)}, u32[]{:S(2)}, u32[]{:S(2)}) collective-permute-start(bf16[128,2048]{1,0:T(8,128)(2,1)} %get-tuple-element.148), channel_id=1, source_target_pairs={{0,8},{8,16},{16,24},{24,28},{28,20},{20,12},{12,4},{4,0},{1,9},{9... | collective-permute-start | bytes 1572872 | tf_op jit(solution)/shard_map/ppermute | solution.py:102
  608.4 21.2 %collective-permute-start.63 = (bf16[128,2048]{1,0:T(8,128)(2,1)S(1)}, bf16[128,2048]{1,0:T(8,128)(2,1)S(1)}, u32[]{:S(2)}, u32[]{:S(2)}) collective-permute-start(bf16[128,2048]{1,0:T(8,128)(2,1)S(1)} %get-tuple-element.149), channel_id=1, source_target_pairs={{0,4},{8,0},{16,8},{24,16},{28,24},{20,28},{12,20},{4,12},{1,5},{9... | collective-permute-start | bytes 1572872 | tf_op jit(solution)/shard_map/ppermute | solution.py:102
  (88 other events, 987.7 us)

commit v5 on v4

--- a/solution.py
+++ b/solution.py
@@ -924,13 +924,13 @@
         ],
         axis=2,
     )
-    down_grad = to_row_owners(down_own)
-    by_owner = after(jnp.transpose(by_owner, (1, 0, 2)), down_grad)
+    by_owner = jnp.transpose(by_owner, (1, 0, 2))
     got = lax.all_to_all(by_owner, "seq", 0, 0, tiled=True)
     got = got.reshape(length, 2 * head_width)
     grad_heads = got[:, :head_width]
     grad_attn_own = got[:, head_width:]
     gate_grad = to_row_owners(after(gate_own, got))
+    down_grad = to_row_owners(after(down_own, gate_grad))
 
     grad_qkv = attention_back(grad_heads, attn_kept)
     qkv_own, qkv_sends = partial_sum_batch(act_one, grad_qkv)
@@ -984,10 +984,10 @@
 
     sums["gain"], sums["gate_grad"] = gain_grad, gate_grad
     next_gain_sum()
-    sums["rest"] = to_row_owners(jnp.concatenate([after(qkv_own, gate_grad), out_own], axis=1))
+    sums["rest"] = to_row_owners(jnp.concatenate([after(qkv_own, down_grad), out_own], axis=1))
     grad_one = ring_scatter_sum(
-        ring_blocks([after(grad_one_part.astype(jnp.bfloat16), qkv_own, down_m)]),
-        (gate_update, last_transfer, lambda moved: tied(moved, "gain"), last_updates),
+        ring_blocks([after(grad_one_part.astype(jnp.bfloat16), qkv_sends[-1])]),
+        (gate_update, last_transfer, lambda moved: tied(after_all(moved, (down_m,)), "gain"), last_updates),
     )
     while steps:
         next_gain_sum()

time: 649 us -> 640 us (0.986)
  local copies, waits for them, and re-layouts: 61.1 us -> 51.8 us
    all_to_all x1, waiting for transfers between devices: 24.7 us -> 0.01 us  [on_device(): got = lax.all_to_all(by_owner, 'seq', 0, 0, tiled=True)]
    ppermute x28, waiting for transfers between devices: 44.8 us -> 61.2 us  [swapped(): lax.ppermute(value, axis, [(source, source ^ bit) for source in range(cou...]
    all_to_all x1, starting transfers between devices: 12.9 us -> 4.96 us  [on_device(): got = lax.all_to_all(by_owner, 'seq', 0, 0, tiled=True)]
    unnamed x94 -> x100, local copies, waits for them, and re-layouts: 16.2 us -> 13.1 us
  transfers between devices with their start and end apart: 75 -> 75, of which waited for: 31 -> 31; matrix products, arithmetic and copies ran while one was open for 23% -> 22% of each run, Pallas kernels for 20% -> 21%
where the time goes in v5:
time: 640 us; the launch traced here: 630 us
  waiting for transfers between devices  221 us (35%)
  Pallas kernels  135 us (21%)
  starting transfers between devices  112 us (18%)
  matrix products  63.2 us (10%)
  local copies, waits for them, and re-layouts  51.8 us (8%)
  other arithmetic  44.7 us (7%)
    ppermute x40, waiting for transfers between devices, ring_shift(): return lax.ppermute(value, 'seq', pairs)  137 us
    ppermute x28, waiting for transfers between devices, swapped(): lax.ppermute(value, axis, [(source, source ^ bit) for source in range(cou...  61.2 us
    ppermute x40, starting transfers between devices, ring_shift(): return lax.ppermute(value, 'seq', pairs)  51.1 us
    dot_general x10, matrix products, contract_rows(): lax.dot_general(left_side, right_side, (((0,), (0,)), ((), ())), preferre...  43 us
    pallas_call x4, Pallas kernels, adam_by_owner(): pl.pallas_call(kernel, grid=(groups, steps), in_specs=[whole] * 3 + [pl.B...  32.7 us
    pallas_call x2, Pallas kernels, back_to_model(): pl.pallas_call(lambda *refs: back_kernel(total, *refs), grid=(total * eac...  24.1 us
    all_to_all x3, waiting for transfers between devices, to_column_owners(): got = lax.all_to_all(blocks, 'seq', 0, 0, tiled=True)  22.5 us
    pallas_call x3, Pallas kernels, rounded_by_owner(): pl.pallas_call(kernel, grid=(groups, steps), in_specs=[pl.BlockSpec((rows...  19.8 us
  transfers between devices with their start and end apart: 75, of which 31 were waited for; matrix products, arithmetic and copies ran while one was open for 22% of the time, Pallas kernels for 21%

profile of v5, /device:TPU:0, one launch (start us, length us, event | category | flops | bytes accessed | tf_op | source)
XLA Modules:
  0.0 630.4 jit_solution(9225444533800104564)
XLA Ops:
  5.1 7.3 %all-to-all-start = ((bf16[8,64,768]{2,1,0:T(8,128)(2,1)}), bf16[8,64,768]{2,1,0:T(8,128)(2,1)}, u32[]{:S(2)}, u32[]{:S(2)}) async-start(bf16[8,64,768]{2,1,0:T(8,128)(2,1)} %shard_map.305), calls=%async_computation | async-start | bytes 1572864 | tf_op jit(solution)/shard_map/all_to_all | solution.py:346
  27.1 10.0 %shard_map.306 = bf16[8,64,2048]{2,1,0:T(8,128)(2,1)} custom-call(f32[64,16384]{1,0:T(8,128)} %weight_ref.10), custom_call_target="tpu_custom_call" | custom-call | bytes 6291456 | tf_op jit(solution)/shard_map/pallas_call | solution.py:333
  46.2 10.9 %collective-permute-done.3 = bf16[128,3072]{1,0:T(8,128)(2,1)} collective-permute-done((bf16[128,3072]{1,0:T(8,128)(2,1)S(1)}, bf16[128,3072]{1,0:T(8,128)(2,1)}, u32[]{:S(2)}, u32[]{:S(2)}) %collective-permute-start.3) | collective-permute-done | bytes 786464 | tf_op jit(solution)/shard_map/ppermute | solution.py:102
  66.7 12.3 %collective-permute-done.5 = bf16[128,3072]{1,0:T(8,128)(2,1)S(1)} collective-permute-done((bf16[128,3072]{1,0:T(8,128)(2,1)}, bf16[128,3072]{1,0:T(8,128)(2,1)S(1)}, u32[]{:S(2)}, u32[]{:S(2)}) %collective-permute-start.5) | collective-permute-done | bytes 786464 | tf_op jit(solution)/shard_map/ppermute | solution.py:102
  84.4 14.6 %collective-permute-done.8 = bf16[128,3072]{1,0:T(8,128)(2,1)S(1)} collective-permute-done((bf16[128,3072]{1,0:T(8,128)(2,1)S(1)}, bf16[128,3072]{1,0:T(8,128)(2,1)S(1)}, u32[]{:S(2)}, u32[]{:S(2)}) %collective-permute-start.8) | collective-permute-done | bytes 786464 | tf_op jit(solution)/shard_map/ppermute | solution.py:102
  123.8 8.4 %fusion.56.query_in.key_in.value_in = f32[1024,768]{1,0:T(8,128)} fusion(bf16[1024,2048]{1,0:T(8,128)(2,1)S(1)} %fusion.2, bf16[512,768]{1,0:T(8,128)(2,1)S(1)} %collective-permute-done.13, bf16[512,768]{1,0:T(8,128)(2,1)} %collective-permute-done.12, bf16[512,768]{1,0:T(8,128)(2,1)} %collective-permute-done.11, bf16[512,768]{1,0:T(8,128)(2,1)} %bitcast.5), kind=kOutput, calls=%fused_computation.86 | convolution fusion | flops 3233808384 | bytes 10485760 | tf_op jit(solution)/shard_map/dot_general | solution.py:75
  132.2 8.7 %shard_map.308 = (f32[1024,256]{1,0:T(8,128)S(1)}, bf16[1024,256]{1,0:T(8,128)(2,1)S(1)}, bf16[1024,256]{1,0:T(8,128)(2,1)S(1)}, bf16[1024,256]{1,0:T(8,128)(2,1...) custom-call(f32[1024,768]{1,0:T(8,128)} %fusion.56.query_in.key_in.value_in, ...), custom_call_target="tpu_custom_call" | custom-call | flops 2147483648 | bytes 6291456 | tf_op jit(solution)/shard_map/pallas_call | solution.py:658
  144.3 13.0 %all-to-all-done.1 = bf16[8,64,2048]{2,1,0:T(8,128)(2,1)} async-done(((bf16[8,64,2048]{2,1,0:T(8,128)(2,1)}), bf16[8,64,2048]{2,1,0:T(8,128)(2,1)}, u32[]{:S(2)}, u32[]{:S(2)}) %all-to-all-start.1) | async-done | bytes 2097184 | tf_op jit(solution)/shard_map/all_to_all | solution.py:346
  161.4 8.4 %collective-permute-done.15 = bf16[1024,256]{1,0:T(8,128)(2,1)S(1)} collective-permute-done((bf16[1024,256]{1,0:T(8,128)(2,1)S(1)}, bf16[1024,256]{1,0:T(8,128)(2,1)S(1)}, u32[]{:S(2)}, u32[]{:S(2)}) %collective-permute-start.15) | collective-permute-done | bytes 524320 | tf_op jit(solution)/shard_map/ppermute | solution.py:102
  172.0 9.5 %collective-permute-done.17 = bf16[1024,256]{1,0:T(8,128)(2,1)S(1)} collective-permute-done((bf16[1024,256]{1,0:T(8,128)(2,1)S(1)}, bf16[1024,256]{1,0:T(8,128)(2,1)S(1)}, u32[]{:S(2)}, u32[]{:S(2)}) %collective-permute-start.17) | collective-permute-done | bytes 524320 | tf_op jit(solution)/shard_map/ppermute | solution.py:102
  199.6 9.6 %collective-permute-done.27.refs_2_.refs_6_ = bf16[512,2048]{1,0:T(8,128)(2,1)} collective-permute-done((bf16[512,2048]{1,0:T(8,128)(2,1)}, bf16[512,2048]{1,0:T(8,128)(2,1)}, u32[]{:S(2)}, u32[]{:S(2)}) %collective-permute-start.27) | collective-permute-done | bytes 2097184 | tf_op jit(solution)/shard_map/ppermute | solution.py:91
  219.1 15.9 %shard_map.309 = (f32[1024,2048]{1,0:T(8,128)}, bf16[1024,2048]{1,0:T(8,128)(2,1)}) custom-call(bf16[1024,2048]{1,0:T(8,128)(2,1)} %maximum_dynamic-update-slice_fusion.refs_0_, bf16[1024,2048]{1,0:T(8,128)(2,1)} %fusion.59.refs_1_, f32[1,2048]{1,0:T(1,128)S(1)} %get-tuple-element.312.refs_2_, bf16[2048,512]{1,0:T(8,128)(2,1)} %maximum_dynamic-update-slice_fusion.9.refs_3_, ...), custom_call_target="tpu_custom_call" | custom-call | flops 8589934592 | bytes 29360128 | tf_op jit(solution)/shard_map/pallas_call | solution.py:519
  235.0 9.5 %all-to-all-done.2 = bf16[8,64,1024]{2,1,0:T(8,128)(2,1)S(1)} async-done(((bf16[8,64,1024]{2,1,0:T(8,128)(2,1)}), bf16[8,64,1024]{2,1,0:T(8,128)(2,1)S(1)}, u32[]{:S(2)}, u32[]{:S(2)}) %all-to-all-start.2) | async-done | bytes 1048608 | tf_op jit(solution)/shard_map/all_to_all | solution.py:346
  248.0 14.3 %shard_map.310 = (f32[1024,1024]{1,0:T(8,128)}, f32[1024,1024]{1,0:T(8,128)}, bf16[1024,1024]{1,0:T(8,128)(2,1)S(1)}) custom-call(bf16[1024,2048]{1,0:T(8,128)(2,1)} %get-tuple-element.107.refs_0_, bf16[512,2048]{1,0:T(8,128)(2,1)} %bitcast.12.refs_1_.refs_5_, bf16[512,2048]{1,0:T(8,128)(2,1)} %collective-permute-done.27.refs_2_.refs_6_, ...), custom_call_target="tpu_custom_call" | custom-call | flops 8589934592 | bytes 23068672 | tf_op jit(solution)/shard_map/pallas_call | solution.py:563
  277.3 9.4 %collective-permute-done.32 = bf16[128,2048]{1,0:T(8,128)(2,1)S(1)} collective-permute-done((bf16[128,2048]{1,0:T(8,128)(2,1)S(1)}, bf16[128,2048]{1,0:T(8,128)(2,1)S(1)}, u32[]{:S(2)}, u32[]{:S(2)}) %collective-permute-start.32) | collective-permute-done | bytes 524320 | tf_op jit(solution)/shard_map/ppermute | solution.py:102
  286.8 8.7 %shard_map.311 = bf16[1024,2048]{1,0:T(8,128)(2,1)} custom-call(bf16[1024,1024]{1,0:T(8,128)(2,1)} %copy-done.8, bf16[512,1024]{1,0:T(8,128)(2,1)S(1)} %bitcast.104, bf16[512,1024]{1,0:T(8,128)(2,1)S(1)} %collective-permute-done.34.refs_2_.refs_4_, bf16[512,1024]{1,0:T(8,128)(2,1)S(1)} %collective-permute-done.35.refs_3_.refs_5_, ...), custom_call_target="tpu_custom_call" | custom-call | flops 4294967296 | bytes 10485760 | tf_op jit(solution)/shard_map/pallas_call | solution.py:635
  306.6 11.1 %shard_map.312.refs_0_ = bf16[1024,2048]{1,0:T(8,128)(2,1)} custom-call(bf16[1024,2048]{1,0:T(8,128)(2,1)} %copy-done.12, f32[1024,1024]{1,0:T(8,128)} %get-tuple-element.116.refs_1_, f32[1024,1024]{1,0:T(8,128)} %get-tuple-element.117.refs_2_, bf16[512,1024]{1,0:T(8,128)(2,1)S(1)} %bitcast.105, ...), custom_call_target="tpu_custom_call" | custom-call | flops 4294967296 | bytes 20971520 | tf_op jit(solution)/shard_map/pallas_call | solution.py:600
  317.7 15.4 %shard_map.313 = bf16[1024,2048]{1,0:T(8,128)(2,1)} custom-call(bf16[1024,2048]{1,0:T(8,128)(2,1)} %shard_map.312.refs_0_, bf16[512,2048]{1,0:T(8,128)(2,1)} %bitcast.12.refs_1_.refs_5_, bf16[512,2048]{1,0:T(8,128)(2,1)} %collective-permute-done.27.refs_2_.refs_6_, bf16[512,2048]{1,0:T(8,128)(2,1)} %collective-permute-done.28.refs_3_.refs_7_, ...), custom_call_target="tpu_custom_call" | custom-call | flops 8589934592 | bytes 16777216 | tf_op jit(solution)/shard_map/pallas_call | solution.py:635
  337.4 10.4 %collective-permute-done.39 = bf16[128,2048]{1,0:T(8,128)(2,1)S(1)} collective-permute-done((bf16[128,2048]{1,0:T(8,128)(2,1)S(1)}, bf16[128,2048]{1,0:T(8,128)(2,1)S(1)}, u32[]{:S(2)}, u32[]{:S(2)}) %collective-permute-start.39) | collective-permute-done | bytes 524320 | tf_op jit(solution)/shard_map/ppermute | solution.py:102
  358.6 11.5 %collective-permute-done.41 = bf16[128,4096]{1,0:T(8,128)(2,1)S(1)} collective-permute-done((bf16[128,4096]{1,0:T(8,128)(2,1)S(1)}, bf16[128,4096]{1,0:T(8,128)(2,1)S(1)}, u32[]{:S(2)}, u32[]{:S(2)}) %collective-permute-start.41) | collective-permute-done | bytes 1048608 | tf_op jit(solution)/shard_map/ppermute | solution.py:102
  376.4 12.0 %collective-permute-done.43 = bf16[128,4096]{1,0:T(8,128)(2,1)S(1)} collective-permute-done((bf16[128,4096]{1,0:T(8,128)(2,1)S(1)}, bf16[128,4096]{1,0:T(8,128)(2,1)S(1)}, u32[]{:S(2)}, u32[]{:S(2)}) %collective-permute-start.43) | collective-permute-done | bytes 1048608 | tf_op jit(solution)/shard_map/ppermute | solution.py:102
  402.2 13.1 %collective-permute-done.48 = bf16[128,4096]{1,0:T(8,128)(2,1)} collective-permute-done((bf16[128,4096]{1,0:T(8,128)(2,1)}, bf16[128,4096]{1,0:T(8,128)(2,1)}, u32[]{:S(2)}, u32[]{:S(2)}) %collective-permute-start.48) | collective-permute-done | bytes 1048608 | tf_op jit(solution)/shard_map/ppermute | solution.py:102
  434.9 15.5 %collective-permute-done.49 = bf16[512,2048]{1,0:T(8,128)(2,1)} collective-permute-done((bf16[512,2048]{1,0:T(8,128)(2,1)}, bf16[512,2048]{1,0:T(8,128)(2,1)}, u32[]{:S(2)}, u32[]{:S(2)}) %collective-permute-start.49) | collective-permute-done | bytes 2097184 | tf_op jit(solution)/shard_map/ppermute | solution.py:91
  450.5 8.2 %fusion.12 = bf16[512,2048]{1,0:T(8,128)(2,1)} fusion(f32[1024,2048]{1,0:T(8,128)} %copy-done.11, bf16[512,2048]{1,0:T(8,128)(2,1)} %collective-permute-done.49, bf16[1024,2048]{1,0:T(8,128)(2,1)} %shard_map.312.refs_0_, bf16[1024,2048]{1,0:T(8,128)(2,1)} %get-tuple-element.107.refs_0_), kind=kOutput, calls=%fused_computation.16 | convolution fusion | flops 2151677952 | bytes 13631488 | tf_op jit(solution)/shard_map/dot_general | solution.py:63
  471.6 8.6 %shard_map.314 = bf16[1024,768]{1,0:T(8,128)(2,1)S(1)} custom-call(bf16[1024,256]{1,0:T(8,128)(2,1)S(1)} %copy-done.3, bf16[1024,256]{1,0:T(8,128)(2,1)S(1)} %copy-done.5, bf16[1024,256]{1,0:T(8,128)(2,1)S(1)} %copy-done.7, bf16[1024,256]{1,0:T(8,128)(2,1)S(1)} %slice.388.grad_ref, f32[1024,256]{1,0:T(8,128)S(1)} %copy-done.1, ...), custom_call_target="tpu_custom_call" | custom-call | flops 268435456 | bytes 1048576 | tf_op jit(solution)/shard_map/pallas_call | solution.py:695
  499.6 6.4 %multiply_reduce_fusion = (f32[2048]{0:T(1024)S(1)}, bf16[1024,2048]{1,0:T(8,128)(2,1)S(1)}) fusion(bf16[1024,2048]{1,0:T(8,128)(2,1)} %copy-done.25, bf16[1024,768]{1,0:T(8,128)(2,1)S(1)} %shard_map.314, bf16[512,768]{1,0:T(8,128)(2,1)S(1)} %copy-done.46, bf16[512,768]{1,0:T(8,128)(2,1)} %collective-permute-done.12, ...), kind=kOutput, calls=%fused_computation.13 | convolution fusion | flops 3242194944 | bytes 13115392 | tf_op jit(solution)/shard_map/dot_general | solution.py:69
  527.9 15.7 %shard_map.315 = (f32[64,16384]{1,0:T(8,128)}, f32[64,16384]{1,0:T(8,128)}, f32[64,16384]{1,0:T(8,128)}) custom-call(f32[64,16384]{1,0:T(8,128)} %weight_ref.10, f32[64,16384]{1,0:T(8,128)} %first_ref.4, f32[64,16384]{1,0:T(8,128)} %second_ref.4, bf16[8,64,2048]{2,1,0:T(8,128)(2,1)} %all-to-all-done.4.gradient_ref), custom_call_target="tpu_custom_call" | custom-call | flops 15728640 | bytes 27262976 | tf_op jit(solution)/shard_map/pallas_call | solution.py:383
  545.5 7.8 %all-to-all-start.6 = ((bf16[8,64,1024]{2,1,0:T(8,128)(2,1)}), bf16[8,64,1024]{2,1,0:T(8,128)(2,1)S(1)}, u32[]{:S(2)}, u32[]{:S(2)}) async-start(bf16[8,64,1024]{2,1,0:T(8,128)(2,1)} %pad_maximum_fusion.4), calls=%async_computation.6 | async-start | bytes 2097152 | tf_op jit(solution)/shard_map/all_to_all | solution.py:353
  559.3 17.3 %collective-permute-done.60 = f32[2,2048]{1,0:T(2,128)S(1)} collective-permute-done((f32[2,2048]{1,0:T(2,128)S(1)}, f32[2,2048]{1,0:T(2,128)S(1)}, u32[]{:S(2)}, u32[]{:S(2)}) %collective-permute-start.60) | collective-permute-done | bytes 16416 | tf_op jit(solution)/shard_map/ppermute | solution.py:91
  583.7 8.2 %shard_map.316 = (f32[64,8192]{1,0:T(8,128)}, f32[64,8192]{1,0:T(8,128)}, f32[64,8192]{1,0:T(8,128)}) custom-call(f32[64,8192]{1,0:T(8,128)} %weight_ref.11, f32[64,8192]{1,0:T(8,128)} %first_ref.5, f32[64,8192]{1,0:T(8,128)} %second_ref.5, bf16[8,64,1024]{2,1,0:T(8,128)(2,1)} %copy-done.19), custom_call_target="tpu_custom_call" | custom-call | flops 7864320 | bytes 13631488 | tf_op jit(solution)/shard_map/pallas_call | solution.py:383
  591.9 7.3 %collective-permute-start.61 = (bf16[128,2048]{1,0:T(8,128)(2,1)}, bf16[128,2048]{1,0:T(8,128)(2,1)S(1)}, u32[]{:S(2)}, u32[]{:S(2)}) collective-permute-start(bf16[128,2048]{1,0:T(8,128)(2,1)} %get-tuple-element.152), channel_id=1, source_target_pairs={{0,8},{8,16},{16,24},{24,28},{28,20},{20,12},{12,4},{4,0},{1,9},{9... | collective-permute-start | bytes 1572872 | tf_op jit(solution)/shard_map/ppermute | solution.py:102
  603.2 7.9 %collective-permute-done.66 = f32[2,2048]{1,0:T(2,128)S(1)} collective-permute-done((f32[2,2048]{1,0:T(2,128)S(1)}, f32[2,2048]{1,0:T(2,128)S(1)}, u32[]{:S(2)}, u32[]{:S(2)}) %collective-permute-start.66) | collective-permute-done | bytes 16416 | tf_op jit(solution)/shard_map/ppermute | solution.py:91
  (421 shorter events, 280.8 us)
Async XLA Ops:
  5.1 55.3 %all-to-all-start = ((bf16[8,64,768]{2,1,0:T(8,128)(2,1)}), bf16[8,64,768]{2,1,0:T(8,128)(2,1)}, u32[]{:S(2)}, u32[]{:S(2)}) async-start(bf16[8,64,768]{2,1,0:T(8,128)(2,1)} %shard_map.305), calls=%async_computation | async-start | bytes 1572864 | tf_op jit(solution)/shard_map/all_to_all | solution.py:346
  16.6 20.4 %collective-permute-start.1 = (bf16[64,512]{1,0:T(8,128)(2,1)S(1)}, bf16[64,512]{1,0:T(8,128)(2,1)S(1)}, u32[]{:S(2)}, u32[]{:S(2)}) collective-permute-start(bf16[64,512]{1,0:T(8,128)(2,1)S(1)} %get-tuple-element.301), channel_id=1, source_target_pairs={{0,2},{1,3},{2,0},{3,1},{4,6},{5,7},{6,4},{7,5},{8,10},{9,11},{10,... | collective-permute-start | bytes 196616 | tf_op jit(solution)/shard_map/ppermute | solution.py:91
  37.2 19.9 %collective-permute-start.3 = (bf16[128,3072]{1,0:T(8,128)(2,1)S(1)}, bf16[128,3072]{1,0:T(8,128)(2,1)}, u32[]{:S(2)}, u32[]{:S(2)}) collective-permute-start(bf16[128,3072]{1,0:T(8,128)(2,1)S(1)} %maximum_maximum_fusion), channel_id=1, source_target_pairs={{0,8},{8,16},{16,24},{24,28},{28,20},{20,12},{12,4},{4,0},{1,9},{9... | collective-permute-start | bytes 2359304 | tf_op jit(solution)/shard_map/ppermute | solution.py:102
  65.2 48.5 %collective-permute-start.11 = (bf16[512,768]{1,0:T(8,128)(2,1)}, bf16[512,768]{1,0:T(8,128)(2,1)}, u32[]{:S(2)}, u32[]{:S(2)}) collective-permute-start(bf16[512,768]{1,0:T(8,128)(2,1)} %bitcast.5), channel_id=1, source_target_pairs={{0,2},{1,3},{2,0},{3,1},{4,6},{5,7},{6,4},{7,5},{8,10},{9,11},{10,... | collective-permute-start | bytes 2359304 | tf_op jit(solution)/shard_map/ppermute | solution.py:91
  66.6 57.1 %collective-permute-start.12 = (bf16[512,768]{1,0:T(8,128)(2,1)}, bf16[512,768]{1,0:T(8,128)(2,1)}, u32[]{:S(2)}, u32[]{:S(2)}) collective-permute-start(bf16[512,768]{1,0:T(8,128)(2,1)} %bitcast.5), channel_id=1, source_target_pairs={{0,1},{1,0},{2,3},{3,2},{4,5},{5,4},{6,7},{7,6},{8,9},{9,8},{10,11... | collective-permute-start | bytes 2359304 | tf_op jit(solution)/shard_map/ppermute | solution.py:91
  108.3 49.0 %all-to-all-start.1 = ((bf16[8,64,2048]{2,1,0:T(8,128)(2,1)}), bf16[8,64,2048]{2,1,0:T(8,128)(2,1)}, u32[]{:S(2)}, u32[]{:S(2)}) async-start(bf16[8,64,2048]{2,1,0:T(8,128)(2,1)} %shard_map.306), calls=%async_computation.1 | async-start | bytes 4194304 | tf_op jit(solution)/shard_map/all_to_all | solution.py:346
  115.9 68.1 %collective-permute-start.22 = (bf16[2048,512]{1,0:T(8,128)(2,1)}, bf16[2048,512]{1,0:T(8,128)(2,1)}, u32[]{:S(2)}, u32[]{:S(2)}) collective-permute-start(bf16[2048,512]{1,0:T(8,128)(2,1)} %maximum_dynamic-update-slice_fusion.9.refs_3_), channel_id=1, source_target_pairs={{0,2},{1,3},{2,0},{3,1},{4,6},{5,7},{6,4},{7,5},{8,10},{9,11},{10,... | collective-permute-start | bytes 6291464 | tf_op jit(solution)/shard_map/ppermute | solution.py:91
  157.3 51.9 %collective-permute-start.27 = (bf16[512,2048]{1,0:T(8,128)(2,1)}, bf16[512,2048]{1,0:T(8,128)(2,1)}, u32[]{:S(2)}, u32[]{:S(2)}) collective-permute-start(bf16[512,2048]{1,0:T(8,128)(2,1)} %bitcast.12.refs_1_.refs_5_), channel_id=1, source_target_pairs={{0,2},{1,3},{2,0},{3,1},{4,6},{5,7},{6,4},{7,5},{8,10},{9,11},{10,... | collective-permute-start | bytes 6291464 | tf_op jit(solution)/shard_map/ppermute | solution.py:91
  184.0 35.1 %collective-permute-start.23 = (bf16[2048,512]{1,0:T(8,128)(2,1)}, bf16[2048,512]{1,0:T(8,128)(2,1)}, u32[]{:S(2)}, u32[]{:S(2)}) collective-permute-start(bf16[2048,512]{1,0:T(8,128)(2,1)} %maximum_dynamic-update-slice_fusion.9.refs_3_), channel_id=1, source_target_pairs={{0,1},{1,0},{2,3},{3,2},{4,5},{5,4},{6,7},{7,6},{8,9},{9,8},{10,11... | collective-permute-start | bytes 6291464 | tf_op jit(solution)/shard_map/ppermute | solution.py:91
  184.0 35.1 %collective-permute-start.24 = (bf16[2048,512]{1,0:T(8,128)(2,1)}, bf16[2048,512]{1,0:T(8,128)(2,1)}, u32[]{:S(2)}, u32[]{:S(2)}) collective-permute-start(bf16[2048,512]{1,0:T(8,128)(2,1)} %collective-permute-done.22.refs_4_), channel_id=1, source_target_pairs={{0,1},{1,0},{2,3},{3,2},{4,5},{5,4},{6,7},{7,6},{8,9},{9,8},{10,11... | collective-permute-start | bytes 6291464 | tf_op jit(solution)/shard_map/ppermute | solution.py:91
  199.6 48.5 %collective-permute-start.28 = (bf16[512,2048]{1,0:T(8,128)(2,1)}, bf16[512,2048]{1,0:T(8,128)(2,1)}, u32[]{:S(2)}, u32[]{:S(2)}) collective-permute-start(bf16[512,2048]{1,0:T(8,128)(2,1)} %bitcast.12.refs_1_.refs_5_), channel_id=1, source_target_pairs={{0,1},{1,0},{2,3},{3,2},{4,5},{5,4},{6,7},{7,6},{8,9},{9,8},{10,11... | collective-permute-start | bytes 6291464 | tf_op jit(solution)/shard_map/ppermute | solution.py:91
  209.2 38.8 %collective-permute-start.29 = (bf16[512,2048]{1,0:T(8,128)(2,1)}, bf16[512,2048]{1,0:T(8,128)(2,1)}, u32[]{:S(2)}, u32[]{:S(2)}) collective-permute-start(bf16[512,2048]{1,0:T(8,128)(2,1)} %collective-permute-done.27.refs_2_.refs_6_), channel_id=1, source_target_pairs={{0,1},{1,0},{2,3},{3,2},{4,5},{5,4},{6,7},{7,6},{8,9},{9,8},{10,11... | collective-permute-start | bytes 6291464 | tf_op jit(solution)/shard_map/ppermute | solution.py:91
  211.7 32.8 %all-to-all-start.2 = ((bf16[8,64,1024]{2,1,0:T(8,128)(2,1)}), bf16[8,64,1024]{2,1,0:T(8,128)(2,1)S(1)}, u32[]{:S(2)}, u32[]{:S(2)}) async-start(bf16[8,64,1024]{2,1,0:T(8,128)(2,1)} %shard_map.307), calls=%async_computation.2 | async-start | bytes 2097152 | tf_op jit(solution)/shard_map/all_to_all | solution.py:346
  246.5 23.9 %collective-permute-start.34 = (bf16[512,1024]{1,0:T(8,128)(2,1)S(1)}, bf16[512,1024]{1,0:T(8,128)(2,1)S(1)}, u32[]{:S(2)}, u32[]{:S(2)}) collective-permute-start(bf16[512,1024]{1,0:T(8,128)(2,1)S(1)} %bitcast.102), channel_id=1, source_target_pairs={{0,2},{1,3},{2,0},{3,1},{4,6},{5,7},{6,4},{7,5},{8,10},{9,11},{10,... | collective-permute-start | bytes 3145736 | tf_op jit(solution)/shard_map/ppermute | solution.py:91
  264.4 22.3 %collective-permute-start.35 = (bf16[512,1024]{1,0:T(8,128)(2,1)S(1)}, bf16[512,1024]{1,0:T(8,128)(2,1)S(1)}, u32[]{:S(2)}, u32[]{:S(2)}) collective-permute-start(bf16[512,1024]{1,0:T(8,128)(2,1)S(1)} %bitcast.103), channel_id=1, source_target_pairs={{0,1},{1,0},{2,3},{3,2},{4,5},{5,4},{6,7},{7,6},{8,9},{9,8},{10,11... | collective-permute-start | bytes 3145736 | tf_op jit(solution)/shard_map/ppermute | solution.py:91
  299.8 37.3 %collective-permute-start.40 = (bf16[128,2048]{1,0:T(8,128)(2,1)}, bf16[128,2048]{1,0:T(8,128)(2,1)S(1)}, u32[]{:S(2)}, u32[]{:S(2)}) collective-permute-start(bf16[128,2048]{1,0:T(8,128)(2,1)} %constant_dynamic-slice_fusion.7), channel_id=1, source_target_pairs={{0,4},{8,0},{16,8},{24,16},{28,24},{20,28},{12,20},{4,12},{1,5},{9... | collective-permute-start | bytes 1572872 | tf_op jit(solution)/shard_map/ppermute | solution.py:102
  348.0 22.1 %collective-permute-start.41 = (bf16[128,4096]{1,0:T(8,128)(2,1)S(1)}, bf16[128,4096]{1,0:T(8,128)(2,1)S(1)}, u32[]{:S(2)}, u32[]{:S(2)}) collective-permute-start(bf16[128,4096]{1,0:T(8,128)(2,1)S(1)} %pad_maximum_fusion.1), channel_id=1, source_target_pairs={{0,8},{8,16},{16,24},{24,28},{28,20},{20,12},{12,4},{4,0},{1,9},{9... | collective-permute-start | bytes 3145736 | tf_op jit(solution)/shard_map/ppermute | solution.py:102
  358.1 32.9 %collective-permute-start.46 = (bf16[1024,2048]{1,0:T(8,128)(2,1)S(1)}, bf16[1024,2048]{1,0:T(8,128)(2,1)S(1)}, u32[]{:S(2)}, u32[]{:S(2)}) collective-permute-start(bf16[1024,2048]{1,0:T(8,128)(2,1)S(1)} %convolution_convert_fusion), channel_id=1, source_target_pairs={{0,1},{1,0},{2,3},{3,2},{4,5},{5,4},{6,7},{7,6},{8,9},{9,8},{10,11... | collective-permute-start | bytes 12582920 | tf_op jit(solution)/shard_map/ppermute | solution.py:91
  401.5 48.9 %collective-permute-start.49 = (bf16[512,2048]{1,0:T(8,128)(2,1)}, bf16[512,2048]{1,0:T(8,128)(2,1)}, u32[]{:S(2)}, u32[]{:S(2)}) collective-permute-start(bf16[512,2048]{1,0:T(8,128)(2,1)} %fusion.13), channel_id=1, source_target_pairs={{0,2},{1,3},{2,0},{3,1},{4,6},{5,7},{6,4},{7,5},{8,10},{9,11},{10,... | collective-permute-start | bytes 6291464 | tf_op jit(solution)/shard_map/ppermute | solution.py:91
  429.4 29.4 %all-to-all-start.3 = ((bf16[8,128,512]{1,2,0:T(8,128)(2,1)}), bf16[8,128,512]{1,2,0:T(8,128)(2,1)S(1)}, u32[]{:S(2)}, u32[]{:S(2)}) async-start(bf16[8,128,512]{1,2,0:T(8,128)(2,1)} %maximum_bitcast_fusion), calls=%async_computation.3 | async-start | bytes 2097152 | tf_op jit(solution)/shard_map/all_to_all | solution.py:928
  434.3 50.7 %collective-permute-start.59 = (bf16[512,1024]{1,0:T(8,128)(2,1)}, bf16[512,1024]{1,0:T(8,128)(2,1)}, u32[]{:S(2)}, u32[]{:S(2)}) collective-permute-start(bf16[512,1024]{1,0:T(8,128)(2,1)} %fusion.21), channel_id=1, source_target_pairs={{0,2},{1,3},{2,0},{3,1},{4,6},{5,7},{6,4},{7,5},{8,10},{9,11},{10,... | collective-permute-start | bytes 3145736 | tf_op jit(solution)/shard_map/ppermute | solution.py:91
  461.2 38.4 %all-to-all-start.4 = ((bf16[8,64,2048]{2,1,0:T(8,128)(2,1)}), bf16[8,64,2048]{2,1,0:T(8,128)(2,1)}, u32[]{:S(2)}, u32[]{:S(2)}) async-start(bf16[8,64,2048]{2,1,0:T(8,128)(2,1)} %bitcast.110), calls=%async_computation.4 | async-start | bytes 4194304 | tf_op jit(solution)/shard_map/all_to_all | solution.py:353
  499.1 25.4 %collective-permute-start.63 = (bf16[512,768]{1,0:T(8,128)(2,1)}, bf16[512,768]{1,0:T(8,128)(2,1)}, u32[]{:S(2)}, u32[]{:S(2)}) collective-permute-start(bf16[512,768]{1,0:T(8,128)(2,1)} %fusion.33), channel_id=1, source_target_pairs={{0,2},{1,3},{2,0},{3,1},{4,6},{5,7},{6,4},{7,5},{8,10},{9,11},{10,... | collective-permute-start | bytes 2359304 | tf_op jit(solution)/shard_map/ppermute | solution.py:91
  510.9 33.2 %all-to-all-start.5 = ((bf16[8,64,1024]{2,1,0:T(8,128)(2,1)}), bf16[8,64,1024]{2,1,0:T(8,128)(2,1)S(1)}, u32[]{:S(2)}, u32[]{:S(2)}) async-start(bf16[8,64,1024]{2,1,0:T(8,128)(2,1)} %bitcast.123), calls=%async_computation.5 | async-start | bytes 2097152 | tf_op jit(solution)/shard_map/all_to_all | solution.py:353
  520.9 32.4 %collective-permute-start.55 = (bf16[128,2048]{1,0:T(8,128)(2,1)}, bf16[128,2048]{1,0:T(8,128)(2,1)}, u32[]{:S(2)}, u32[]{:S(2)}) collective-permute-start(bf16[128,2048]{1,0:T(8,128)(2,1)} %get-tuple-element.138), channel_id=1, source_target_pairs={{0,4},{8,0},{16,8},{24,16},{28,24},{20,28},{12,20},{4,12},{1,5},{9... | collective-permute-start | bytes 1572872 | tf_op jit(solution)/shard_map/ppermute | solution.py:102
  522.9 30.4 %collective-permute-start.54 = (bf16[128,2048]{1,0:T(8,128)(2,1)S(1)}, bf16[128,2048]{1,0:T(8,128)(2,1)}, u32[]{:S(2)}, u32[]{:S(2)}) collective-permute-start(bf16[128,2048]{1,0:T(8,128)(2,1)S(1)} %get-tuple-element.137), channel_id=1, source_target_pairs={{0,8},{8,16},{16,24},{24,28},{28,20},{20,12},{12,4},{4,0},{1,9},{9... | collective-permute-start | bytes 1572872 | tf_op jit(solution)/shard_map/ppermute | solution.py:102
  523.0 20.6 %collective-permute-start.56 = (f32[2,2048]{1,0:T(2,128)S(1)}, f32[2,2048]{1,0:T(2,128)S(1)}, u32[]{:S(2)}, u32[]{:S(2)}) collective-permute-start(f32[2,2048]{1,0:T(2,128)S(1)} %add.640), channel_id=1, source_target_pairs={{0,2},{1,3},{2,0},{3,1},{4,6},{5,7},{6,4},{7,5},{8,10},{9,11},{10,... | collective-permute-start | bytes 49160 | tf_op jit(solution)/shard_map/ppermute | solution.py:91
  545.5 65.7 %all-to-all-start.6 = ((bf16[8,64,1024]{2,1,0:T(8,128)(2,1)}), bf16[8,64,1024]{2,1,0:T(8,128)(2,1)S(1)}, u32[]{:S(2)}, u32[]{:S(2)}) async-start(bf16[8,64,1024]{2,1,0:T(8,128)(2,1)} %pad_maximum_fusion.4), calls=%async_computation.6 | async-start | bytes 2097152 | tf_op jit(solution)/shard_map/all_to_all | solution.py:353
  555.2 25.9 %collective-permute-start.58 = (bf16[128,2048]{1,0:T(8,128)(2,1)S(1)}, bf16[128,2048]{1,0:T(8,128)(2,1)S(1)}, u32[]{:S(2)}, u32[]{:S(2)}) collective-permute-start(bf16[128,2048]{1,0:T(8,128)(2,1)S(1)} %get-tuple-element.145), channel_id=1, source_target_pairs={{0,4},{8,0},{16,8},{24,16},{28,24},{20,28},{12,20},{4,12},{1,5},{9... | collective-permute-start | bytes 1572872 | tf_op jit(solution)/shard_map/ppermute | solution.py:102
  557.3 23.8 %collective-permute-start.57 = (bf16[128,2048]{1,0:T(8,128)(2,1)S(1)}, bf16[128,2048]{1,0:T(8,128)(2,1)S(1)}, u32[]{:S(2)}, u32[]{:S(2)}) collective-permute-start(bf16[128,2048]{1,0:T(8,128)(2,1)S(1)} %get-tuple-element.144), channel_id=1, source_target_pairs={{0,8},{8,16},{16,24},{24,28},{28,20},{20,12},{12,4},{4,0},{1,9},{9... | collective-permute-start | bytes 1572872 | tf_op jit(solution)/shard_map/ppermute | solution.py:102
  591.9 29.1 %collective-permute-start.61 = (bf16[128,2048]{1,0:T(8,128)(2,1)}, bf16[128,2048]{1,0:T(8,128)(2,1)S(1)}, u32[]{:S(2)}, u32[]{:S(2)}) collective-permute-start(bf16[128,2048]{1,0:T(8,128)(2,1)} %get-tuple-element.152), channel_id=1, source_target_pairs={{0,8},{8,16},{16,24},{24,28},{28,20},{20,12},{12,4},{4,0},{1,9},{9... | collective-permute-start | bytes 1572872 | tf_op jit(solution)/shard_map/ppermute | solution.py:102
  599.2 21.8 %collective-permute-start.62 = (bf16[128,2048]{1,0:T(8,128)(2,1)}, bf16[128,2048]{1,0:T(8,128)(2,1)S(1)}, u32[]{:S(2)}, u32[]{:S(2)}) collective-permute-start(bf16[128,2048]{1,0:T(8,128)(2,1)} %get-tuple-element.153), channel_id=1, source_target_pairs={{0,4},{8,0},{16,8},{24,16},{28,24},{20,28},{12,20},{4,12},{1,5},{9... | collective-permute-start | bytes 1572872 | tf_op jit(solution)/shard_map/ppermute | solution.py:102
  (91 other events, 1012.3 us)

commit v6 on v5

--- a/solution.py
+++ b/solution.py
@@ -980,14 +980,14 @@
         sums["out"] = adam_by_owner(
             out_weight, out_first, out_second, sums["rest"], 1, rate_out, skipped=3
         )
-        return tied(after_all(moved, (sums["qkv"][0], sums["out"][0])), "gain")
+        return tied(after_all(moved, (sums["qkv"][0], sums["out"][0], down_m)), "gain")
 
     sums["gain"], sums["gate_grad"] = gain_grad, gate_grad
     next_gain_sum()
     sums["rest"] = to_row_owners(jnp.concatenate([after(qkv_own, down_grad), out_own], axis=1))
     grad_one = ring_scatter_sum(
         ring_blocks([after(grad_one_part.astype(jnp.bfloat16), qkv_sends[-1])]),
-        (gate_update, last_transfer, lambda moved: tied(after_all(moved, (down_m,)), "gain"), last_updates),
+        (gate_update, last_transfer, lambda moved: tied(moved, "gain"), last_updates),
     )
     while steps:
         next_gain_sum()

time: 640 us -> 640 us (level)
  no operation moved by 1% of the time
where the time goes in v6:
time: 640 us; the launch traced here: 630 us
  waiting for transfers between devices  221 us (35%)
  Pallas kernels  135 us (21%)
  starting transfers between devices  112 us (18%)
  matrix products  63.2 us (10%)
  local copies, waits for them, and re-layouts  51.8 us (8%)
  other arithmetic  44.7 us (7%)
    ppermute x40, waiting for transfers between devices, ring_shift(): return lax.ppermute(value, 'seq', pairs)  137 us
    ppermute x28, waiting for transfers between devices, swapped(): lax.ppermute(value, axis, [(source, source ^ bit) for source in range(cou...  61.3 us
    ppermute x40, starting transfers between devices, ring_shift(): return lax.ppermute(value, 'seq', pairs)  50.9 us
    dot_general x10, matrix products, contract_rows(): lax.dot_general(left_side, right_side, (((0,), (0,)), ((), ())), preferre...  43 us
    pallas_call x4, Pallas kernels, adam_by_owner(): pl.pallas_call(kernel, grid=(groups, steps), in_specs=[whole] * 3 + [pl.B...  32.9 us
    pallas_call x2, Pallas kernels, back_to_model(): pl.pallas_call(lambda *refs: back_kernel(total, *refs), grid=(total * eac...  24.1 us
    all_to_all x3, waiting for transfers between devices, to_column_owners(): got = lax.all_to_all(blocks, 'seq', 0, 0, tiled=True)  22.5 us
    pallas_call x3, Pallas kernels, rounded_by_owner(): pl.pallas_call(kernel, grid=(groups, steps), in_specs=[pl.BlockSpec((rows...  19.8 us
  transfers between devices with their start and end apart: 75, of which 31 were waited for; matrix products, arithmetic and copies ran while one was open for 22% of the time, Pallas kernels for 21%

profile of v6, /device:TPU:0, one launch (start us, length us, event | category | flops | bytes accessed | tf_op | source)
XLA Modules:
  0.0 630.5 jit_solution(4651460872550212807)
XLA Ops:
  5.1 7.3 %all-to-all-start = ((bf16[8,64,768]{2,1,0:T(8,128)(2,1)}), bf16[8,64,768]{2,1,0:T(8,128)(2,1)}, u32[]{:S(2)}, u32[]{:S(2)}) async-start(bf16[8,64,768]{2,1,0:T(8,128)(2,1)} %shard_map.305), calls=%async_computation | async-start | bytes 1572864 | tf_op jit(solution)/shard_map/all_to_all | solution.py:346
  27.1 10.0 %shard_map.306 = bf16[8,64,2048]{2,1,0:T(8,128)(2,1)} custom-call(f32[64,16384]{1,0:T(8,128)} %weight_ref.10), custom_call_target="tpu_custom_call" | custom-call | bytes 6291456 | tf_op jit(solution)/shard_map/pallas_call | solution.py:333
  46.2 10.9 %collective-permute-done.3 = bf16[128,3072]{1,0:T(8,128)(2,1)} collective-permute-done((bf16[128,3072]{1,0:T(8,128)(2,1)S(1)}, bf16[128,3072]{1,0:T(8,128)(2,1)}, u32[]{:S(2)}, u32[]{:S(2)}) %collective-permute-start.3) | collective-permute-done | bytes 786464 | tf_op jit(solution)/shard_map/ppermute | solution.py:102
  66.7 12.3 %collective-permute-done.5 = bf16[128,3072]{1,0:T(8,128)(2,1)S(1)} collective-permute-done((bf16[128,3072]{1,0:T(8,128)(2,1)}, bf16[128,3072]{1,0:T(8,128)(2,1)S(1)}, u32[]{:S(2)}, u32[]{:S(2)}) %collective-permute-start.5) | collective-permute-done | bytes 786464 | tf_op jit(solution)/shard_map/ppermute | solution.py:102
  84.4 14.6 %collective-permute-done.8 = bf16[128,3072]{1,0:T(8,128)(2,1)S(1)} collective-permute-done((bf16[128,3072]{1,0:T(8,128)(2,1)S(1)}, bf16[128,3072]{1,0:T(8,128)(2,1)S(1)}, u32[]{:S(2)}, u32[]{:S(2)}) %collective-permute-start.8) | collective-permute-done | bytes 786464 | tf_op jit(solution)/shard_map/ppermute | solution.py:102
  123.8 8.4 %fusion.56.query_in.key_in.value_in = f32[1024,768]{1,0:T(8,128)} fusion(bf16[1024,2048]{1,0:T(8,128)(2,1)S(1)} %fusion.2, bf16[512,768]{1,0:T(8,128)(2,1)S(1)} %collective-permute-done.13, bf16[512,768]{1,0:T(8,128)(2,1)} %collective-permute-done.12, bf16[512,768]{1,0:T(8,128)(2,1)} %collective-permute-done.11, bf16[512,768]{1,0:T(8,128)(2,1)} %bitcast.5), kind=kOutput, calls=%fused_computation.86 | convolution fusion | flops 3233808384 | bytes 10485760 | tf_op jit(solution)/shard_map/dot_general | solution.py:75
  132.2 8.7 %shard_map.308 = (f32[1024,256]{1,0:T(8,128)S(1)}, bf16[1024,256]{1,0:T(8,128)(2,1)S(1)}, bf16[1024,256]{1,0:T(8,128)(2,1)S(1)}, bf16[1024,256]{1,0:T(8,128)(2,1...) custom-call(f32[1024,768]{1,0:T(8,128)} %fusion.56.query_in.key_in.value_in, ...), custom_call_target="tpu_custom_call" | custom-call | flops 2147483648 | bytes 6291456 | tf_op jit(solution)/shard_map/pallas_call | solution.py:658
  144.3 13.0 %all-to-all-done.1 = bf16[8,64,2048]{2,1,0:T(8,128)(2,1)} async-done(((bf16[8,64,2048]{2,1,0:T(8,128)(2,1)}), bf16[8,64,2048]{2,1,0:T(8,128)(2,1)}, u32[]{:S(2)}, u32[]{:S(2)}) %all-to-all-start.1) | async-done | bytes 2097184 | tf_op jit(solution)/shard_map/all_to_all | solution.py:346
  161.4 8.4 %collective-permute-done.15 = bf16[1024,256]{1,0:T(8,128)(2,1)S(1)} collective-permute-done((bf16[1024,256]{1,0:T(8,128)(2,1)S(1)}, bf16[1024,256]{1,0:T(8,128)(2,1)S(1)}, u32[]{:S(2)}, u32[]{:S(2)}) %collective-permute-start.15) | collective-permute-done | bytes 524320 | tf_op jit(solution)/shard_map/ppermute | solution.py:102
  172.0 9.5 %collective-permute-done.17 = bf16[1024,256]{1,0:T(8,128)(2,1)S(1)} collective-permute-done((bf16[1024,256]{1,0:T(8,128)(2,1)S(1)}, bf16[1024,256]{1,0:T(8,128)(2,1)S(1)}, u32[]{:S(2)}, u32[]{:S(2)}) %collective-permute-start.17) | collective-permute-done | bytes 524320 | tf_op jit(solution)/shard_map/ppermute | solution.py:102
  199.6 9.6 %collective-permute-done.27.refs_2_.refs_6_ = bf16[512,2048]{1,0:T(8,128)(2,1)} collective-permute-done((bf16[512,2048]{1,0:T(8,128)(2,1)}, bf16[512,2048]{1,0:T(8,128)(2,1)}, u32[]{:S(2)}, u32[]{:S(2)}) %collective-permute-start.27) | collective-permute-done | bytes 2097184 | tf_op jit(solution)/shard_map/ppermute | solution.py:91
  219.1 15.9 %shard_map.309 = (f32[1024,2048]{1,0:T(8,128)}, bf16[1024,2048]{1,0:T(8,128)(2,1)}) custom-call(bf16[1024,2048]{1,0:T(8,128)(2,1)} %maximum_dynamic-update-slice_fusion.refs_0_, bf16[1024,2048]{1,0:T(8,128)(2,1)} %fusion.59.refs_1_, f32[1,2048]{1,0:T(1,128)S(1)} %get-tuple-element.308.refs_2_, bf16[2048,512]{1,0:T(8,128)(2,1)} %maximum_dynamic-update-slice_fusion.9.refs_3_, ...), custom_call_target="tpu_custom_call" | custom-call | flops 8589934592 | bytes 29360128 | tf_op jit(solution)/shard_map/pallas_call | solution.py:519
  235.0 9.5 %all-to-all-done.2 = bf16[8,64,1024]{2,1,0:T(8,128)(2,1)S(1)} async-done(((bf16[8,64,1024]{2,1,0:T(8,128)(2,1)}), bf16[8,64,1024]{2,1,0:T(8,128)(2,1)S(1)}, u32[]{:S(2)}, u32[]{:S(2)}) %all-to-all-start.2) | async-done | bytes 1048608 | tf_op jit(solution)/shard_map/all_to_all | solution.py:346
  248.0 14.3 %shard_map.310 = (f32[1024,1024]{1,0:T(8,128)}, f32[1024,1024]{1,0:T(8,128)}, bf16[1024,1024]{1,0:T(8,128)(2,1)S(1)}) custom-call(bf16[1024,2048]{1,0:T(8,128)(2,1)} %get-tuple-element.105.refs_0_, bf16[512,2048]{1,0:T(8,128)(2,1)} %bitcast.12.refs_1_.refs_5_, bf16[512,2048]{1,0:T(8,128)(2,1)} %collective-permute-done.27.refs_2_.refs_6_, ...), custom_call_target="tpu_custom_call" | custom-call | flops 8589934592 | bytes 23068672 | tf_op jit(solution)/shard_map/pallas_call | solution.py:563
  277.3 9.4 %collective-permute-done.32 = bf16[128,2048]{1,0:T(8,128)(2,1)S(1)} collective-permute-done((bf16[128,2048]{1,0:T(8,128)(2,1)S(1)}, bf16[128,2048]{1,0:T(8,128)(2,1)S(1)}, u32[]{:S(2)}, u32[]{:S(2)}) %collective-permute-start.32) | collective-permute-done | bytes 524320 | tf_op jit(solution)/shard_map/ppermute | solution.py:102
  286.8 8.7 %shard_map.311 = bf16[1024,2048]{1,0:T(8,128)(2,1)} custom-call(bf16[1024,1024]{1,0:T(8,128)(2,1)} %copy-done.8, bf16[512,1024]{1,0:T(8,128)(2,1)S(1)} %bitcast.104, bf16[512,1024]{1,0:T(8,128)(2,1)S(1)} %collective-permute-done.34.refs_2_.refs_4_, bf16[512,1024]{1,0:T(8,128)(2,1)S(1)} %collective-permute-done.35.refs_3_.refs_5_, ...), custom_call_target="tpu_custom_call" | custom-call | flops 4294967296 | bytes 10485760 | tf_op jit(solution)/shard_map/pallas_call | solution.py:635
  306.6 11.1 %shard_map.312.refs_0_ = bf16[1024,2048]{1,0:T(8,128)(2,1)} custom-call(bf16[1024,2048]{1,0:T(8,128)(2,1)} %copy-done.12, f32[1024,1024]{1,0:T(8,128)} %get-tuple-element.114.refs_1_, f32[1024,1024]{1,0:T(8,128)} %get-tuple-element.115.refs_2_, bf16[512,1024]{1,0:T(8,128)(2,1)S(1)} %bitcast.105, ...), custom_call_target="tpu_custom_call" | custom-call | flops 4294967296 | bytes 20971520 | tf_op jit(solution)/shard_map/pallas_call | solution.py:600
  317.7 15.4 %shard_map.313 = bf16[1024,2048]{1,0:T(8,128)(2,1)} custom-call(bf16[1024,2048]{1,0:T(8,128)(2,1)} %shard_map.312.refs_0_, bf16[512,2048]{1,0:T(8,128)(2,1)} %bitcast.12.refs_1_.refs_5_, bf16[512,2048]{1,0:T(8,128)(2,1)} %collective-permute-done.27.refs_2_.refs_6_, bf16[512,2048]{1,0:T(8,128)(2,1)} %collective-permute-done.28.refs_3_.refs_7_, ...), custom_call_target="tpu_custom_call" | custom-call | flops 8589934592 | bytes 16777216 | tf_op jit(solution)/shard_map/pallas_call | solution.py:635
  337.4 10.4 %collective-permute-done.39 = bf16[128,2048]{1,0:T(8,128)(2,1)S(1)} collective-permute-done((bf16[128,2048]{1,0:T(8,128)(2,1)S(1)}, bf16[128,2048]{1,0:T(8,128)(2,1)S(1)}, u32[]{:S(2)}, u32[]{:S(2)}) %collective-permute-start.39) | collective-permute-done | bytes 524320 | tf_op jit(solution)/shard_map/ppermute | solution.py:102
  358.6 11.5 %collective-permute-done.41 = bf16[128,4096]{1,0:T(8,128)(2,1)S(1)} collective-permute-done((bf16[128,4096]{1,0:T(8,128)(2,1)S(1)}, bf16[128,4096]{1,0:T(8,128)(2,1)S(1)}, u32[]{:S(2)}, u32[]{:S(2)}) %collective-permute-start.41) | collective-permute-done | bytes 1048608 | tf_op jit(solution)/shard_map/ppermute | solution.py:102
  376.4 12.0 %collective-permute-done.43 = bf16[128,4096]{1,0:T(8,128)(2,1)S(1)} collective-permute-done((bf16[128,4096]{1,0:T(8,128)(2,1)S(1)}, bf16[128,4096]{1,0:T(8,128)(2,1)S(1)}, u32[]{:S(2)}, u32[]{:S(2)}) %collective-permute-start.43) | collective-permute-done | bytes 1048608 | tf_op jit(solution)/shard_map/ppermute | solution.py:102
  402.2 13.1 %collective-permute-done.48 = bf16[128,4096]{1,0:T(8,128)(2,1)} collective-permute-done((bf16[128,4096]{1,0:T(8,128)(2,1)}, bf16[128,4096]{1,0:T(8,128)(2,1)}, u32[]{:S(2)}, u32[]{:S(2)}) %collective-permute-start.48) | collective-permute-done | bytes 1048608 | tf_op jit(solution)/shard_map/ppermute | solution.py:102
  434.9 15.5 %collective-permute-done.49 = bf16[512,2048]{1,0:T(8,128)(2,1)} collective-permute-done((bf16[512,2048]{1,0:T(8,128)(2,1)}, bf16[512,2048]{1,0:T(8,128)(2,1)}, u32[]{:S(2)}, u32[]{:S(2)}) %collective-permute-start.49) | collective-permute-done | bytes 2097184 | tf_op jit(solution)/shard_map/ppermute | solution.py:91
  450.5 8.2 %fusion.12 = bf16[512,2048]{1,0:T(8,128)(2,1)} fusion(f32[1024,2048]{1,0:T(8,128)} %copy-done.11, bf16[512,2048]{1,0:T(8,128)(2,1)} %collective-permute-done.49, bf16[1024,2048]{1,0:T(8,128)(2,1)} %shard_map.312.refs_0_, bf16[1024,2048]{1,0:T(8,128)(2,1)} %get-tuple-element.105.refs_0_), kind=kOutput, calls=%fused_computation.16 | convolution fusion | flops 2151677952 | bytes 13631488 | tf_op jit(solution)/shard_map/dot_general | solution.py:63
  471.6 8.6 %shard_map.314 = bf16[1024,768]{1,0:T(8,128)(2,1)S(1)} custom-call(bf16[1024,256]{1,0:T(8,128)(2,1)S(1)} %copy-done.3, bf16[1024,256]{1,0:T(8,128)(2,1)S(1)} %copy-done.5, bf16[1024,256]{1,0:T(8,128)(2,1)S(1)} %copy-done.7, bf16[1024,256]{1,0:T(8,128)(2,1)S(1)} %slice.388.grad_ref, f32[1024,256]{1,0:T(8,128)S(1)} %copy-done.1, ...), custom_call_target="tpu_custom_call" | custom-call | flops 268435456 | bytes 1048576 | tf_op jit(solution)/shard_map/pallas_call | solution.py:695
  499.6 6.4 %multiply_reduce_fusion = (f32[2048]{0:T(1024)S(1)}, bf16[1024,2048]{1,0:T(8,128)(2,1)S(1)}) fusion(bf16[1024,2048]{1,0:T(8,128)(2,1)} %copy-done.25, bf16[1024,768]{1,0:T(8,128)(2,1)S(1)} %shard_map.314, bf16[512,768]{1,0:T(8,128)(2,1)S(1)} %copy-done.46, bf16[512,768]{1,0:T(8,128)(2,1)} %collective-permute-done.12, ...), kind=kOutput, calls=%fused_computation.13 | convolution fusion | flops 3242194944 | bytes 13115392 | tf_op jit(solution)/shard_map/dot_general | solution.py:69
  527.9 15.7 %shard_map.315 = (f32[64,16384]{1,0:T(8,128)}, f32[64,16384]{1,0:T(8,128)}, f32[64,16384]{1,0:T(8,128)}) custom-call(f32[64,16384]{1,0:T(8,128)} %weight_ref.10, f32[64,16384]{1,0:T(8,128)} %first_ref.4, f32[64,16384]{1,0:T(8,128)} %second_ref.4, bf16[8,64,2048]{2,1,0:T(8,128)(2,1)} %all-to-all-done.4.gradient_ref), custom_call_target="tpu_custom_call" | custom-call | flops 15728640 | bytes 27262976 | tf_op jit(solution)/shard_map/pallas_call | solution.py:383
  545.5 8.0 %all-to-all-start.6 = ((bf16[8,64,1024]{2,1,0:T(8,128)(2,1)}), bf16[8,64,1024]{2,1,0:T(8,128)(2,1)S(1)}, u32[]{:S(2)}, u32[]{:S(2)}) async-start(bf16[8,64,1024]{2,1,0:T(8,128)(2,1)} %pad_maximum_fusion.4), calls=%async_computation.6 | async-start | bytes 2097152 | tf_op jit(solution)/shard_map/all_to_all | solution.py:353
  559.5 17.3 %collective-permute-done.59 = f32[2,2048]{1,0:T(2,128)S(1)} collective-permute-done((f32[2,2048]{1,0:T(2,128)S(1)}, f32[2,2048]{1,0:T(2,128)S(1)}, u32[]{:S(2)}, u32[]{:S(2)}) %collective-permute-start.59) | collective-permute-done | bytes 16416 | tf_op jit(solution)/shard_map/ppermute | solution.py:91
  583.8 7.3 %collective-permute-start.60 = (bf16[128,2048]{1,0:T(8,128)(2,1)}, bf16[128,2048]{1,0:T(8,128)(2,1)S(1)}, u32[]{:S(2)}, u32[]{:S(2)}) collective-permute-start(bf16[128,2048]{1,0:T(8,128)(2,1)} %get-tuple-element.145), channel_id=1, source_target_pairs={{0,8},{8,16},{16,24},{24,28},{28,20},{20,12},{12,4},{4,0},{1,9},{9... | collective-permute-start | bytes 1572872 | tf_op jit(solution)/shard_map/ppermute | solution.py:102
  594.9 7.9 %collective-permute-done.66 = f32[2,2048]{1,0:T(2,128)S(1)} collective-permute-done((f32[2,2048]{1,0:T(2,128)S(1)}, f32[2,2048]{1,0:T(2,128)S(1)}, u32[]{:S(2)}, u32[]{:S(2)}) %collective-permute-start.66) | collective-permute-done | bytes 16416 | tf_op jit(solution)/shard_map/ppermute | solution.py:91
  602.9 8.3 %shard_map.318 = (f32[64,8192]{1,0:T(8,128)}, f32[64,8192]{1,0:T(8,128)}, f32[64,8192]{1,0:T(8,128)}) custom-call(f32[64,8192]{1,0:T(8,128)} %weight_ref.13, f32[64,8192]{1,0:T(8,128)} %first_ref.7, f32[64,8192]{1,0:T(8,128)} %second_ref.7, bf16[8,64,1024]{2,1,0:T(8,128)(2,1)} %copy-done.19), custom_call_target="tpu_custom_call" | custom-call | flops 7864320 | bytes 13631488 | tf_op jit(solution)/shard_map/pallas_call | solution.py:383
  (421 shorter events, 280.6 us)
Async XLA Ops:
  5.1 55.3 %all-to-all-start = ((bf16[8,64,768]{2,1,0:T(8,128)(2,1)}), bf16[8,64,768]{2,1,0:T(8,128)(2,1)}, u32[]{:S(2)}, u32[]{:S(2)}) async-start(bf16[8,64,768]{2,1,0:T(8,128)(2,1)} %shard_map.305), calls=%async_computation | async-start | bytes 1572864 | tf_op jit(solution)/shard_map/all_to_all | solution.py:346
  16.6 20.4 %collective-permute-start.1 = (bf16[64,512]{1,0:T(8,128)(2,1)S(1)}, bf16[64,512]{1,0:T(8,128)(2,1)S(1)}, u32[]{:S(2)}, u32[]{:S(2)}) collective-permute-start(bf16[64,512]{1,0:T(8,128)(2,1)S(1)} %get-tuple-element.297), channel_id=1, source_target_pairs={{0,2},{1,3},{2,0},{3,1},{4,6},{5,7},{6,4},{7,5},{8,10},{9,11},{10,... | collective-permute-start | bytes 196616 | tf_op jit(solution)/shard_map/ppermute | solution.py:91
  37.2 19.9 %collective-permute-start.3 = (bf16[128,3072]{1,0:T(8,128)(2,1)S(1)}, bf16[128,3072]{1,0:T(8,128)(2,1)}, u32[]{:S(2)}, u32[]{:S(2)}) collective-permute-start(bf16[128,3072]{1,0:T(8,128)(2,1)S(1)} %maximum_maximum_fusion), channel_id=1, source_target_pairs={{0,8},{8,16},{16,24},{24,28},{28,20},{20,12},{12,4},{4,0},{1,9},{9... | collective-permute-start | bytes 2359304 | tf_op jit(solution)/shard_map/ppermute | solution.py:102
  65.2 48.5 %collective-permute-start.11 = (bf16[512,768]{1,0:T(8,128)(2,1)}, bf16[512,768]{1,0:T(8,128)(2,1)}, u32[]{:S(2)}, u32[]{:S(2)}) collective-permute-start(bf16[512,768]{1,0:T(8,128)(2,1)} %bitcast.5), channel_id=1, source_target_pairs={{0,2},{1,3},{2,0},{3,1},{4,6},{5,7},{6,4},{7,5},{8,10},{9,11},{10,... | collective-permute-start | bytes 2359304 | tf_op jit(solution)/shard_map/ppermute | solution.py:91
  66.6 57.1 %collective-permute-start.12 = (bf16[512,768]{1,0:T(8,128)(2,1)}, bf16[512,768]{1,0:T(8,128)(2,1)}, u32[]{:S(2)}, u32[]{:S(2)}) collective-permute-start(bf16[512,768]{1,0:T(8,128)(2,1)} %bitcast.5), channel_id=1, source_target_pairs={{0,1},{1,0},{2,3},{3,2},{4,5},{5,4},{6,7},{7,6},{8,9},{9,8},{10,11... | collective-permute-start | bytes 2359304 | tf_op jit(solution)/shard_map/ppermute | solution.py:91
  108.3 49.0 %all-to-all-start.1 = ((bf16[8,64,2048]{2,1,0:T(8,128)(2,1)}), bf16[8,64,2048]{2,1,0:T(8,128)(2,1)}, u32[]{:S(2)}, u32[]{:S(2)}) async-start(bf16[8,64,2048]{2,1,0:T(8,128)(2,1)} %shard_map.306), calls=%async_computation.1 | async-start | bytes 4194304 | tf_op jit(solution)/shard_map/all_to_all | solution.py:346
  115.9 68.1 %collective-permute-start.22 = (bf16[2048,512]{1,0:T(8,128)(2,1)}, bf16[2048,512]{1,0:T(8,128)(2,1)}, u32[]{:S(2)}, u32[]{:S(2)}) collective-permute-start(bf16[2048,512]{1,0:T(8,128)(2,1)} %maximum_dynamic-update-slice_fusion.9.refs_3_), channel_id=1, source_target_pairs={{0,2},{1,3},{2,0},{3,1},{4,6},{5,7},{6,4},{7,5},{8,10},{9,11},{10,... | collective-permute-start | bytes 6291464 | tf_op jit(solution)/shard_map/ppermute | solution.py:91
  157.3 51.9 %collective-permute-start.27 = (bf16[512,2048]{1,0:T(8,128)(2,1)}, bf16[512,2048]{1,0:T(8,128)(2,1)}, u32[]{:S(2)}, u32[]{:S(2)}) collective-permute-start(bf16[512,2048]{1,0:T(8,128)(2,1)} %bitcast.12.refs_1_.refs_5_), channel_id=1, source_target_pairs={{0,2},{1,3},{2,0},{3,1},{4,6},{5,7},{6,4},{7,5},{8,10},{9,11},{10,... | collective-permute-start | bytes 6291464 | tf_op jit(solution)/shard_map/ppermute | solution.py:91
  184.0 35.1 %collective-permute-start.23 = (bf16[2048,512]{1,0:T(8,128)(2,1)}, bf16[2048,512]{1,0:T(8,128)(2,1)}, u32[]{:S(2)}, u32[]{:S(2)}) collective-permute-start(bf16[2048,512]{1,0:T(8,128)(2,1)} %maximum_dynamic-update-slice_fusion.9.refs_3_), channel_id=1, source_target_pairs={{0,1},{1,0},{2,3},{3,2},{4,5},{5,4},{6,7},{7,6},{8,9},{9,8},{10,11... | collective-permute-start | bytes 6291464 | tf_op jit(solution)/shard_map/ppermute | solution.py:91
  184.0 35.1 %collective-permute-start.24 = (bf16[2048,512]{1,0:T(8,128)(2,1)}, bf16[2048,512]{1,0:T(8,128)(2,1)}, u32[]{:S(2)}, u32[]{:S(2)}) collective-permute-start(bf16[2048,512]{1,0:T(8,128)(2,1)} %collective-permute-done.22.refs_4_), channel_id=1, source_target_pairs={{0,1},{1,0},{2,3},{3,2},{4,5},{5,4},{6,7},{7,6},{8,9},{9,8},{10,11... | collective-permute-start | bytes 6291464 | tf_op jit(solution)/shard_map/ppermute | solution.py:91
  199.6 48.5 %collective-permute-start.28 = (bf16[512,2048]{1,0:T(8,128)(2,1)}, bf16[512,2048]{1,0:T(8,128)(2,1)}, u32[]{:S(2)}, u32[]{:S(2)}) collective-permute-start(bf16[512,2048]{1,0:T(8,128)(2,1)} %bitcast.12.refs_1_.refs_5_), channel_id=1, source_target_pairs={{0,1},{1,0},{2,3},{3,2},{4,5},{5,4},{6,7},{7,6},{8,9},{9,8},{10,11... | collective-permute-start | bytes 6291464 | tf_op jit(solution)/shard_map/ppermute | solution.py:91
  209.2 38.8 %collective-permute-start.29 = (bf16[512,2048]{1,0:T(8,128)(2,1)}, bf16[512,2048]{1,0:T(8,128)(2,1)}, u32[]{:S(2)}, u32[]{:S(2)}) collective-permute-start(bf16[512,2048]{1,0:T(8,128)(2,1)} %collective-permute-done.27.refs_2_.refs_6_), channel_id=1, source_target_pairs={{0,1},{1,0},{2,3},{3,2},{4,5},{5,4},{6,7},{7,6},{8,9},{9,8},{10,11... | collective-permute-start | bytes 6291464 | tf_op jit(solution)/shard_map/ppermute | solution.py:91
  211.7 32.8 %all-to-all-start.2 = ((bf16[8,64,1024]{2,1,0:T(8,128)(2,1)}), bf16[8,64,1024]{2,1,0:T(8,128)(2,1)S(1)}, u32[]{:S(2)}, u32[]{:S(2)}) async-start(bf16[8,64,1024]{2,1,0:T(8,128)(2,1)} %shard_map.307), calls=%async_computation.2 | async-start | bytes 2097152 | tf_op jit(solution)/shard_map/all_to_all | solution.py:346
  246.5 23.9 %collective-permute-start.34 = (bf16[512,1024]{1,0:T(8,128)(2,1)S(1)}, bf16[512,1024]{1,0:T(8,128)(2,1)S(1)}, u32[]{:S(2)}, u32[]{:S(2)}) collective-permute-start(bf16[512,1024]{1,0:T(8,128)(2,1)S(1)} %bitcast.102), channel_id=1, source_target_pairs={{0,2},{1,3},{2,0},{3,1},{4,6},{5,7},{6,4},{7,5},{8,10},{9,11},{10,... | collective-permute-start | bytes 3145736 | tf_op jit(solution)/shard_map/ppermute | solution.py:91
  264.4 22.3 %collective-permute-start.35 = (bf16[512,1024]{1,0:T(8,128)(2,1)S(1)}, bf16[512,1024]{1,0:T(8,128)(2,1)S(1)}, u32[]{:S(2)}, u32[]{:S(2)}) collective-permute-start(bf16[512,1024]{1,0:T(8,128)(2,1)S(1)} %bitcast.103), channel_id=1, source_target_pairs={{0,1},{1,0},{2,3},{3,2},{4,5},{5,4},{6,7},{7,6},{8,9},{9,8},{10,11... | collective-permute-start | bytes 3145736 | tf_op jit(solution)/shard_map/ppermute | solution.py:91
  299.8 37.3 %collective-permute-start.40 = (bf16[128,2048]{1,0:T(8,128)(2,1)}, bf16[128,2048]{1,0:T(8,128)(2,1)S(1)}, u32[]{:S(2)}, u32[]{:S(2)}) collective-permute-start(bf16[128,2048]{1,0:T(8,128)(2,1)} %constant_dynamic-slice_fusion.7), channel_id=1, source_target_pairs={{0,4},{8,0},{16,8},{24,16},{28,24},{20,28},{12,20},{4,12},{1,5},{9... | collective-permute-start | bytes 1572872 | tf_op jit(solution)/shard_map/ppermute | solution.py:102
  348.0 22.1 %collective-permute-start.41 = (bf16[128,4096]{1,0:T(8,128)(2,1)S(1)}, bf16[128,4096]{1,0:T(8,128)(2,1)S(1)}, u32[]{:S(2)}, u32[]{:S(2)}) collective-permute-start(bf16[128,4096]{1,0:T(8,128)(2,1)S(1)} %pad_maximum_fusion.1), channel_id=1, source_target_pairs={{0,8},{8,16},{16,24},{24,28},{28,20},{20,12},{12,4},{4,0},{1,9},{9... | collective-permute-start | bytes 3145736 | tf_op jit(solution)/shard_map/ppermute | solution.py:102
  358.1 32.9 %collective-permute-start.46 = (bf16[1024,2048]{1,0:T(8,128)(2,1)S(1)}, bf16[1024,2048]{1,0:T(8,128)(2,1)S(1)}, u32[]{:S(2)}, u32[]{:S(2)}) collective-permute-start(bf16[1024,2048]{1,0:T(8,128)(2,1)S(1)} %convolution_convert_fusion), channel_id=1, source_target_pairs={{0,1},{1,0},{2,3},{3,2},{4,5},{5,4},{6,7},{7,6},{8,9},{9,8},{10,11... | collective-permute-start | bytes 12582920 | tf_op jit(solution)/shard_map/ppermute | solution.py:91
  401.5 48.9 %collective-permute-start.49 = (bf16[512,2048]{1,0:T(8,128)(2,1)}, bf16[512,2048]{1,0:T(8,128)(2,1)}, u32[]{:S(2)}, u32[]{:S(2)}) collective-permute-start(bf16[512,2048]{1,0:T(8,128)(2,1)} %fusion.13), channel_id=1, source_target_pairs={{0,2},{1,3},{2,0},{3,1},{4,6},{5,7},{6,4},{7,5},{8,10},{9,11},{10,... | collective-permute-start | bytes 6291464 | tf_op jit(solution)/shard_map/ppermute | solution.py:91
  429.4 29.4 %all-to-all-start.3 = ((bf16[8,128,512]{1,2,0:T(8,128)(2,1)}), bf16[8,128,512]{1,2,0:T(8,128)(2,1)S(1)}, u32[]{:S(2)}, u32[]{:S(2)}) async-start(bf16[8,128,512]{1,2,0:T(8,128)(2,1)} %maximum_bitcast_fusion), calls=%async_computation.3 | async-start | bytes 2097152 | tf_op jit(solution)/shard_map/all_to_all | solution.py:928
  434.3 50.7 %collective-permute-start.63 = (bf16[512,1024]{1,0:T(8,128)(2,1)}, bf16[512,1024]{1,0:T(8,128)(2,1)}, u32[]{:S(2)}, u32[]{:S(2)}) collective-permute-start(bf16[512,1024]{1,0:T(8,128)(2,1)} %fusion.21), channel_id=1, source_target_pairs={{0,2},{1,3},{2,0},{3,1},{4,6},{5,7},{6,4},{7,5},{8,10},{9,11},{10,... | collective-permute-start | bytes 3145736 | tf_op jit(solution)/shard_map/ppermute | solution.py:91
  461.2 38.4 %all-to-all-start.4 = ((bf16[8,64,2048]{2,1,0:T(8,128)(2,1)}), bf16[8,64,2048]{2,1,0:T(8,128)(2,1)}, u32[]{:S(2)}, u32[]{:S(2)}) async-start(bf16[8,64,2048]{2,1,0:T(8,128)(2,1)} %bitcast.110), calls=%async_computation.4 | async-start | bytes 4194304 | tf_op jit(solution)/shard_map/all_to_all | solution.py:353
  499.1 25.4 %collective-permute-start.62 = (bf16[512,768]{1,0:T(8,128)(2,1)}, bf16[512,768]{1,0:T(8,128)(2,1)}, u32[]{:S(2)}, u32[]{:S(2)}) collective-permute-start(bf16[512,768]{1,0:T(8,128)(2,1)} %fusion.33), channel_id=1, source_target_pairs={{0,2},{1,3},{2,0},{3,1},{4,6},{5,7},{6,4},{7,5},{8,10},{9,11},{10,... | collective-permute-start | bytes 2359304 | tf_op jit(solution)/shard_map/ppermute | solution.py:91
  510.9 33.2 %all-to-all-start.5 = ((bf16[8,64,1024]{2,1,0:T(8,128)(2,1)}), bf16[8,64,1024]{2,1,0:T(8,128)(2,1)S(1)}, u32[]{:S(2)}, u32[]{:S(2)}) async-start(bf16[8,64,1024]{2,1,0:T(8,128)(2,1)} %bitcast.123), calls=%async_computation.5 | async-start | bytes 2097152 | tf_op jit(solution)/shard_map/all_to_all | solution.py:353
  520.9 32.5 %collective-permute-start.55 = (bf16[128,2048]{1,0:T(8,128)(2,1)}, bf16[128,2048]{1,0:T(8,128)(2,1)}, u32[]{:S(2)}, u32[]{:S(2)}) collective-permute-start(bf16[128,2048]{1,0:T(8,128)(2,1)} %get-tuple-element.136), channel_id=1, source_target_pairs={{0,4},{8,0},{16,8},{24,16},{28,24},{20,28},{12,20},{4,12},{1,5},{9... | collective-permute-start | bytes 1572872 | tf_op jit(solution)/shard_map/ppermute | solution.py:102
  522.9 30.5 %collective-permute-start.54 = (bf16[128,2048]{1,0:T(8,128)(2,1)S(1)}, bf16[128,2048]{1,0:T(8,128)(2,1)}, u32[]{:S(2)}, u32[]{:S(2)}) collective-permute-start(bf16[128,2048]{1,0:T(8,128)(2,1)S(1)} %get-tuple-element.135), channel_id=1, source_target_pairs={{0,8},{8,16},{16,24},{24,28},{28,20},{20,12},{12,4},{4,0},{1,9},{9... | collective-permute-start | bytes 1572872 | tf_op jit(solution)/shard_map/ppermute | solution.py:102
  523.0 20.6 %collective-permute-start.56 = (f32[2,2048]{1,0:T(2,128)S(1)}, f32[2,2048]{1,0:T(2,128)S(1)}, u32[]{:S(2)}, u32[]{:S(2)}) collective-permute-start(f32[2,2048]{1,0:T(2,128)S(1)} %add.640), channel_id=1, source_target_pairs={{0,2},{1,3},{2,0},{3,1},{4,6},{5,7},{6,4},{7,5},{8,10},{9,11},{10,... | collective-permute-start | bytes 49160 | tf_op jit(solution)/shard_map/ppermute | solution.py:91
  545.5 65.8 %all-to-all-start.6 = ((bf16[8,64,1024]{2,1,0:T(8,128)(2,1)}), bf16[8,64,1024]{2,1,0:T(8,128)(2,1)S(1)}, u32[]{:S(2)}, u32[]{:S(2)}) async-start(bf16[8,64,1024]{2,1,0:T(8,128)(2,1)} %pad_maximum_fusion.4), calls=%async_computation.6 | async-start | bytes 2097152 | tf_op jit(solution)/shard_map/all_to_all | solution.py:353
  555.4 25.9 %collective-permute-start.58 = (bf16[128,2048]{1,0:T(8,128)(2,1)S(1)}, bf16[128,2048]{1,0:T(8,128)(2,1)S(1)}, u32[]{:S(2)}, u32[]{:S(2)}) collective-permute-start(bf16[128,2048]{1,0:T(8,128)(2,1)S(1)} %get-tuple-element.143), channel_id=1, source_target_pairs={{0,4},{8,0},{16,8},{24,16},{28,24},{20,28},{12,20},{4,12},{1,5},{9... | collective-permute-start | bytes 1572872 | tf_op jit(solution)/shard_map/ppermute | solution.py:102
  557.4 23.8 %collective-permute-start.57 = (bf16[128,2048]{1,0:T(8,128)(2,1)S(1)}, bf16[128,2048]{1,0:T(8,128)(2,1)S(1)}, u32[]{:S(2)}, u32[]{:S(2)}) collective-permute-start(bf16[128,2048]{1,0:T(8,128)(2,1)S(1)} %get-tuple-element.142), channel_id=1, source_target_pairs={{0,8},{8,16},{16,24},{24,28},{28,20},{20,12},{12,4},{4,0},{1,9},{9... | collective-permute-start | bytes 1572872 | tf_op jit(solution)/shard_map/ppermute | solution.py:102
  583.8 37.3 %collective-permute-start.60 = (bf16[128,2048]{1,0:T(8,128)(2,1)}, bf16[128,2048]{1,0:T(8,128)(2,1)S(1)}, u32[]{:S(2)}, u32[]{:S(2)}) collective-permute-start(bf16[128,2048]{1,0:T(8,128)(2,1)} %get-tuple-element.145), channel_id=1, source_target_pairs={{0,8},{8,16},{16,24},{24,28},{28,20},{20,12},{12,4},{4,0},{1,9},{9... | collective-permute-start | bytes 1572872 | tf_op jit(solution)/shard_map/ppermute | solution.py:102
  591.1 30.0 %collective-permute-start.61 = (bf16[128,2048]{1,0:T(8,128)(2,1)}, bf16[128,2048]{1,0:T(8,128)(2,1)S(1)}, u32[]{:S(2)}, u32[]{:S(2)}) collective-permute-start(bf16[128,2048]{1,0:T(8,128)(2,1)} %get-tuple-element.146), channel_id=1, source_target_pairs={{0,4},{8,0},{16,8},{24,16},{28,24},{20,28},{12,20},{4,12},{1,5},{9... | collective-permute-start | bytes 1572872 | tf_op jit(solution)/shard_map/ppermute | solution.py:102
  (91 other events, 1072.5 us)
